TPU v7x, 32 devices: a whole 2x2x4 slice. The times are simulated.
32 devices in a mesh: dp: 8 (over z, x), tensor: 4 (over y, core).
Axes of the slice: x: 2, y: 2, z: 4, core: 2. Of those that a mesh axis runs over, the one named last changes fastest.
Arguments:
- layer_in: bfloat16 [4096, 1024], P(('dp', 'tensor')), may hold values from -6 to 6
- mixer_gain: float32 [1024], replicated, may hold values from 0.5 to 1.5
- w_mix: bfloat16 [1024, 8, 768], P('dp', 'tensor'), may hold values from -0.1875 to 0.1875
- w_rates: bfloat16 [1024, 8, 2], P('dp', 'tensor'), may hold values from -0.1875 to 0.1875
- conv_taps: bfloat16 [4, 8, 512], P(None, 'tensor', 'dp'), may hold values from -3 to 3
- a_log: float32 [8], replicated, may hold values from 0 to 2.77
- dt_bias: float32 [8], replicated, may hold values from -6.9 to -2.3
- head_gain: float32 [256], replicated, may hold values from 0.5 to 1.5
- w_out: bfloat16 [2048, 1024], P('tensor', 'dp'), may hold values from -0.25 to 0.25
- ffn_gain: float32 [1024], replicated, may hold values from 0.5 to 1.5
- w_gate_up: bfloat16 [1024, 2, 2816], P('dp', None, 'tensor'), may hold values from -0.1875 to 0.1875
- w_down: bfloat16 [2816, 1024], P('tensor', 'dp'), may hold values from -0.15625 to 0.15625
- out_grad: bfloat16 [4096, 1024], P(('dp', 'tensor')), may hold values from -6 to 6
Outputs:
- layer_out: bfloat16 [4096, 1024], P(('dp', 'tensor'))
- in_grad: float32 [4096, 1024], P(('dp', 'tensor'))
- grad_mixer_gain: float32 [1024], replicated
- grad_w_mix: float32 [1024, 8, 768], P('dp', 'tensor')
- grad_w_rates: float32 [1024, 8, 2], P('dp', 'tensor')
- grad_conv_taps: float32 [4, 8, 512], P(None, 'tensor', 'dp')
- grad_a_log: float32 [8], replicated
- grad_dt_bias: float32 [8], replicated
- grad_head_gain: float32 [256], replicated
- grad_w_out: float32 [2048, 1024], P('tensor', 'dp')
- grad_ffn_gain: float32 [1024], replicated
- grad_w_gate_up: float32 [1024, 2, 2816], P('dp', None, 'tensor')
- grad_w_down: float32 [2816, 1024], P('tensor', 'dp')
All inputs are finite; a program needn't handle non-finite values.
Results may differ from a plain program's by a relative error of at most 0.017.
Values may be sent and summed in bfloat16 or wider, within the bound.
No kernel may reach another device: no remote copies, remote signals or barrier semaphores. Data moves between devices by JAX's collectives and lax.ppermute only.
A program may use at most 128 MiB of HBM per device.

v0:
```python
import jax
import jax.numpy as jnp
from jax import lax
from jax.sharding import PartitionSpec as P

CONV = 4
GROUP = 64


highest = lax.Precision.HIGHEST
NORM_EPS = 1e-05
UNIT_EPS = 1e-06


def scale_norm(matrix, scale_gain):
    return (
        matrix
        * lax.rsqrt(jnp.mean(matrix * matrix, axis=-1, keepdims=True) + NORM_EPS)
        * scale_gain
    )


def unit_rows(matrix):
    return matrix * lax.rsqrt(jnp.sum(matrix * matrix, axis=-1, keepdims=True) + UNIT_EPS)


def group_step(state_now, block):
    queries, key_rows, val_rows, log_decay, strength = block
    width = log_decay.shape[1]
    cumulative = jnp.cumsum(log_decay, axis=1)
    row_ids = lax.broadcasted_iota(jnp.int32, (width, width), 0)
    col_ids = lax.broadcasted_iota(jnp.int32, (width, width), 1)
    lower_mask = row_ids >= col_ids
    strict_mask = row_ids > col_ids
    spread = cumulative[:, :, None] - cumulative[:, None, :]
    decay_map = jnp.where(lower_mask, jnp.exp(jnp.where(lower_mask, spread, 0.0)), 0.0)
    key_dots = jnp.einsum("hid,hjd->hij", key_rows, key_rows, precision=highest)
    system = jnp.where(strict_mask, strength[:, :, None] * key_dots * decay_map, 0.0) + jnp.eye(
        width, dtype=jnp.float32
    )
    start_decay = jnp.exp(cumulative)
    right_side = jnp.concatenate(
        [(strength * start_decay)[:, :, None] * key_rows, strength[:, :, None] * val_rows], axis=2
    )
    solved = jax.scipy.linalg.solve_triangular(system, right_side, lower=True)
    key_width = key_rows.shape[2]
    carried = solved[:, :, key_width:] - jnp.einsum(
        "hcd,hde->hce", solved[:, :, :key_width], state_now, precision=highest
    )
    scores = jnp.einsum("hid,hjd->hij", queries, key_rows, precision=highest) * decay_map
    output = start_decay[:, :, None] * jnp.einsum(
        "hcd,hde->hce", queries, state_now, precision=highest
    )
    output = output + jnp.einsum("hij,hje->hie", scores, carried, precision=highest)
    final_decay = cumulative[:, -1:]
    remaining = jnp.exp(final_decay - cumulative)
    state_next = jnp.exp(final_decay)[:, :, None] * state_now
    state_next = state_next + jnp.einsum(
        "hjd,hje->hde", key_rows * remaining[:, :, None], carried, precision=highest
    )
    return (state_next, output)


def to_blocks(matrix):
    length = matrix.shape[0]
    shaped = matrix.reshape((length // GROUP, GROUP) + matrix.shape[1:])
    return jnp.moveaxis(shaped, 2, 1)


def mixer_core(project, rates, taps, a_log, dt_bias, head_gain, first_head):
    heads_here = project.shape[1]
    channels = taps.shape[2]
    value_width = head_gain.shape[0]
    key_width = (channels - value_width) // 2
    length = project.shape[0]
    padded = jnp.pad(project[:, :, :channels], ((CONV - 1, 0), (0, 0), (0, 0)))
    mixed = taps[0] * padded[0:length]
    for offset in range(1, CONV):
        mixed = mixed + taps[offset] * padded[offset : offset + length]
    mixed = jax.nn.silu(mixed)
    queries = unit_rows(mixed[:, :, :key_width]) * key_width ** (-0.5)
    key_rows = unit_rows(mixed[:, :, key_width : 2 * key_width])
    val_rows = mixed[:, :, 2 * key_width :]
    log_rate = lax.dynamic_slice_in_dim(a_log, first_head, heads_here)
    bias_here = lax.dynamic_slice_in_dim(dt_bias, first_head, heads_here)
    log_decay = -jnp.exp(log_rate) * jax.nn.softplus(rates[:, :, 0] + bias_here)
    strength = jax.nn.sigmoid(rates[:, :, 1])
    initial = jnp.zeros((heads_here, key_width, value_width), jnp.float32)
    blocks = (
        to_blocks(queries),
        to_blocks(key_rows),
        to_blocks(val_rows),
        to_blocks(log_decay),
        to_blocks(strength),
    )
    final_state, outputs = lax.scan(group_step, initial, blocks)
    outputs = jnp.moveaxis(outputs, 1, 2).reshape(length, heads_here, value_width)
    gated = scale_norm(outputs, head_gain) * jax.nn.silu(project[:, :, channels:])
    return gated.reshape(length, heads_here * value_width)


def gate_product(gate_up):
    return jax.nn.silu(gate_up[:, 0]) * gate_up[:, 1]


def gather_rows(row_block):
    return lax.all_gather(row_block, "tensor", axis=0, tiled=True)


def sum_rows(partial_sum):
    return lax.psum_scatter(partial_sum, "tensor", scatter_dimension=0, tiled=True)


def gather_grads(row_block):
    return lax.all_gather(row_block, "tensor", axis=0, tiled=True)


def sum_grads(partial_sum):
    return lax.psum_scatter(
        partial_sum.astype(jnp.bfloat16), "tensor", scatter_dimension=0, tiled=True
    ).astype(jnp.float32)


def contract_rows(left, right):
    return lax.dot_general(
        left, right, (((0,), (0,)), ((), ())), preferred_element_type=jnp.float32
    )


def contract_cols(left, right):
    return lax.dot_general(
        left, right, (((1,), (1,)), ((), ())), preferred_element_type=jnp.float32
    )


def per_device(
    layer_in,
    mixer_gain,
    w_mix,
    w_rates,
    conv_taps,
    a_log,
    dt_bias,
    head_gain,
    w_out,
    ffn_gain,
    w_gate_up,
    w_down,
    out_grad,
):
    full_mix, full_rates, full_taps, full_out = (
        lax.all_gather(w_mix, "dp", axis=0, tiled=True),
        lax.all_gather(w_rates, "dp", axis=0, tiled=True),
        lax.all_gather(conv_taps, "dp", axis=2, tiled=True),
        lax.all_gather(w_out, "dp", axis=1, tiled=True),
    )
    resid_in = layer_in.astype(jnp.float32)
    normed, norm_back = jax.vjp(scale_norm, resid_in, mixer_gain)
    normed_all = gather_rows(normed.astype(jnp.bfloat16))
    project = jnp.einsum("sd,dhc->shc", normed_all, full_mix, preferred_element_type=jnp.float32)
    rates = jnp.einsum("sd,dhc->shc", normed_all, full_rates, preferred_element_type=jnp.float32)
    first_head = lax.axis_index("tensor") * full_mix.shape[1]

    def core_local(project_in, rates_in, taps_in, log_rates, decay_bias, gain_in):
        return mixer_core(project_in, rates_in, taps_in, log_rates, decay_bias, gain_in, first_head)

    gated, core_back = jax.vjp(
        core_local, project, rates, full_taps.astype(jnp.float32), a_log, dt_bias, head_gain
    )
    gated_low = gated.astype(jnp.bfloat16)
    mixer_out = sum_rows(jnp.dot(gated_low, full_out, preferred_element_type=jnp.float32))
    resid = resid_in + mixer_out
    full_gate_up, full_down = (
        lax.all_gather(w_gate_up, "dp", axis=0, tiled=True),
        lax.all_gather(w_down, "dp", axis=1, tiled=True),
    )
    ffn_in, ffn_back = jax.vjp(scale_norm, resid, ffn_gain)
    ffn_all = gather_rows(ffn_in.astype(jnp.bfloat16))
    gate_up = jnp.einsum("sd,dgf->sgf", ffn_all, full_gate_up, preferred_element_type=jnp.float32)
    hidden, act_back = jax.vjp(gate_product, gate_up)
    hidden_low = hidden.astype(jnp.bfloat16)
    ffn_out = sum_rows(jnp.dot(hidden_low, full_down, preferred_element_type=jnp.float32))
    layer_out = (resid + ffn_out).astype(jnp.bfloat16)
    top_grad = gather_grads(out_grad)
    local_down = contract_rows(hidden_low, top_grad)
    grad_hidden = contract_cols(top_grad, full_down)
    (grad_gate_up,) = act_back(grad_hidden)
    grad_gate_low = grad_gate_up.astype(jnp.bfloat16)
    local_gate_up = jnp.einsum(
        "sd,sgf->dgf", ffn_all, grad_gate_low, preferred_element_type=jnp.float32
    )
    grad_ffn_in = sum_grads(
        jnp.einsum("sgf,dgf->sd", grad_gate_low, full_gate_up, preferred_element_type=jnp.float32)
    )
    grad_resid_norm, grad_ffn_gain = ffn_back(grad_ffn_in)
    grad_w_gate_up, grad_w_down = (
        lax.psum_scatter(local_gate_up, "dp", scatter_dimension=0, tiled=True),
        lax.psum_scatter(local_down, "dp", scatter_dimension=1, tiled=True),
    )
    grad_resid = out_grad.astype(jnp.float32) + grad_resid_norm
    mix_grad = gather_grads(grad_resid.astype(jnp.bfloat16))
    local_out = contract_rows(gated_low, mix_grad)
    grad_gated = contract_cols(mix_grad, full_out)
    grad_project, grad_rates, local_taps, grad_log_rates, grad_decay_bias, grad_gain_here = (
        core_back(grad_gated)
    )
    project_low = grad_project.astype(jnp.bfloat16)
    rates_low = grad_rates.astype(jnp.bfloat16)
    local_mix = jnp.einsum(
        "sd,shc->dhc", normed_all, project_low, preferred_element_type=jnp.float32
    )
    local_rates = jnp.einsum(
        "sd,shc->dhc", normed_all, rates_low, preferred_element_type=jnp.float32
    )
    back_terms = jnp.einsum(
        "shc,dhc->sd", project_low, full_mix, preferred_element_type=jnp.float32
    )
    back_terms = back_terms + jnp.einsum(
        "shc,dhc->sd", rates_low, full_rates, preferred_element_type=jnp.float32
    )
    grad_normed = sum_grads(back_terms)
    grad_input_norm, grad_gain_first = norm_back(grad_normed)
    in_grad = grad_resid + grad_input_norm
    grad_mixer_gain, grad_ffn_total, grad_head_gain, grad_a_log, grad_dt_bias = lax.psum(
        (grad_gain_first, grad_ffn_gain, grad_gain_here, grad_log_rates, grad_decay_bias),
        ("dp", "tensor"),
    )
    grad_w_mix, grad_w_rates, grad_conv_taps, grad_w_out = (
        lax.psum_scatter(local_mix, "dp", scatter_dimension=0, tiled=True),
        lax.psum_scatter(local_rates, "dp", scatter_dimension=0, tiled=True),
        lax.psum_scatter(local_taps, "dp", scatter_dimension=2, tiled=True),
        lax.psum_scatter(local_out, "dp", scatter_dimension=1, tiled=True),
    )
    return (
        layer_out,
        in_grad,
        grad_mixer_gain,
        grad_w_mix,
        grad_w_rates,
        grad_conv_taps,
        grad_a_log,
        grad_dt_bias,
        grad_head_gain,
        grad_w_out,
        grad_ffn_total,
        grad_w_gate_up,
        grad_w_down,
    )


def solution(mesh):
    return jax.shard_map(
        per_device,
        mesh=mesh,
        in_specs=(
            P(("dp", "tensor"), None),
            P(),
            P("dp", "tensor", None),
            P("dp", "tensor", None),
            P(None, "tensor", "dp"),
            P(),
            P(),
            P(),
            P("tensor", "dp"),
            P(),
            P("dp", None, "tensor"),
            P("tensor", "dp"),
            P(("dp", "tensor"), None),
        ),
        out_specs=(
            P(("dp", "tensor"), None),
            P(("dp", "tensor"), None),
            P(),
            P("dp", "tensor", None),
            P("dp", "tensor", None),
            P(None, "tensor", "dp"),
            P(),
            P(),
            P(),
            P("tensor", "dp"),
            P(),
            P("dp", None, "tensor"),
            P("tensor", "dp"),
        ),
        check_vma=False,
    )
```

profile of v0, /device:TPU:0, one launch (start us, length us, event | category | flops | bytes accessed | tf_op | source)
XLA Modules:
  0.0 1412.6 jit_solution(8674175459306998297)
XLA Ops:
  13.1 32.7 %all_gather.32 = bf16[4,2,512]{0,1,2:T(2,128)(2,1)S(1)} all-gather(bf16[4,2,64]{0,1,2:T(2,128)(2,1)S(1)} %copy.158), channel_id=1, replica_groups=mesh['dp'=8,'tensor'=4] {'dp'}, dimensions={2}, use_global_device_ids=true | all-gather | bytes 9216 | tf_op jit(solution)/shard_map/all_gather | solution.py:154
  47.9 20.8 %all_gather.31 = bf16[1024,2,2]{0,2,1:T(2,128)(2,1)S(1)} all-gather(bf16[128,2,2]{0,2,1:T(2,128)(2,1)S(1)} %copy-done.62), channel_id=1, replica_groups=mesh['dp'=8,'tensor'=4] {'dp'}, dimensions={0}, use_global_device_ids=true | all-gather | bytes 9216 | tf_op jit(solution)/shard_map/all_gather | solution.py:153
  71.8 21.2 %all-gather.11.cloned.1.call-done = bf16[1024,2,768]{2,0,1:T(8,128)(2,1)} async-done(((bf16[128,2,768]{2,0,1:T(8,128)(2,1)}), bf16[1024,2,768]{2,0,1:T(8,128)(2,1)}) %all-gather.11.cloned.1.call-update) | async-done | bytes 3145744 | tf_op jit(solution)/shard_map/all_gather | solution.py:152
  93.0 4.0 fusion.181
  109.6 176.5 %while.88 = (s32[]{:T(128)}, f32[2,128,256]{2,1,0:T(8,128)S(1)}, f32[8,2,64,256]{3,2,1,0:T(8,128)}, f32[8,2,64,64]{3,2,1,0:T(8,128)}, f32[8,2,64,64]{3,2,1,0:T(8...) while((s32[]{:T(128)}, f32[2,128,256]{2,1,0:T(8,128)S(1)}, ...), condition=%wide.region_5.6_spmd.clone.clone, body=%wide.region_3.5_spmd.clone.clone.sunk | while | flops 239907328 | bytes 5324257 | solution.py:96
  114.1 9.8 custom-call.46
  136.2 9.8 custom-call.46
  158.3 9.8 custom-call.46
  180.3 9.8 custom-call.46
  202.3 9.8 custom-call.46
  224.4 9.8 custom-call.46
  246.5 9.8 custom-call.46
  268.5 9.8 custom-call.46
  293.3 3.4 fusion.229
  297.4 29.5 %reduce-scatter.15.cloned.1.call-done = f32[128,1024]{1,0:T(8,128)} async-done(((f32[512,1024]{1,0:T(8,128)}), f32[128,1024]{1,0:T(8,128)}) %reduce-scatter.15.cloned.1.call-update) | async-done | bytes 524304 | tf_op jit(solution)/shard_map/reduce_scatter | solution.py:111
  330.9 58.1 %all-gather.17.cloned.1.call-done = bf16[1024,2,704]{0,2,1:T(8,128)(2,1)} async-done(((bf16[128,2,704]{0,2,1:T(8,128)(2,1)}), bf16[1024,2,704]{0,2,1:T(8,128)(2,1)}) %all-gather.17.cloned.1.call-update) | async-done | bytes 2883600 | tf_op jit(solution)/shard_map/all_gather | solution.py:174
  389.1 17.0 %all-gather.15.cloned.1.call-done = bf16[512,1024]{1,0:T(8,128)(2,1)} async-done(((bf16[128,1024]{1,0:T(8,128)(2,1)}), bf16[512,1024]{1,0:T(8,128)(2,1)}) %all-gather.15.cloned.1.call-update) | async-done | bytes 1048592 | tf_op jit(solution)/shard_map/all_gather | solution.py:107
  406.1 5.5 fusion.174
  411.6 12.9 all-gather.21.cloned.1.call-done
  424.5 46.1 %all-gather.19.cloned.1.call-done = bf16[704,1024]{1,0:T(8,128)(2,1)} async-done(((bf16[704,128]{1,0:T(8,128)(2,1)}), bf16[704,1024]{1,0:T(8,128)(2,1)}) %all-gather.19.cloned.1.call-update) | async-done | bytes 1441808 | tf_op jit(solution)/shard_map/all_gather | solution.py:175
  470.6 5.0 multiply_bitcast_fusion
  480.2 23.4 %reduce-scatter.19.cloned.1.call-done = bf16[128,1024]{1,0:T(8,128)(2,1)} async-done(((bf16[512,1024]{1,0:T(8,128)(2,1)}), bf16[128,1024]{1,0:T(8,128)(2,1)}) %reduce-scatter.19.cloned.1.call-update) | async-done | bytes 262160 | tf_op jit(solution)/shard_map/reduce_scatter | solution.py:119
  507.3 16.8 %all-gather.23.cloned.1.call-done = bf16[512,1024]{1,0:T(8,128)(2,1)} async-done(((bf16[128,1024]{1,0:T(8,128)(2,1)}), bf16[512,1024]{1,0:T(8,128)(2,1)}) %all-gather.23.cloned.1.call-update) | async-done | bytes 1048592 | tf_op jit(solution)/shard_map/all_gather | solution.py:115
  524.2 3.3 fusion.231
  530.0 4.3 multiply_reduce_fusion.4
  540.5 282.1 %while.89 = (s32[]{:T(128)}, f32[2,128,256]{2,1,0:T(8,128)S(1)}, f32[8,2,64,128]{3,2,1,0:T(8,128)}, f32[8,2,64,128]{3,2,1,0:T(8,128)}, f32[8,2,64,256]{3,2,1,0:T...) while((s32[]{:T(128)}, f32[2,128,256]{2,1,0:T(8,128)S(1)}, ...), condition=%wide.region_24.25_spmd.clone.clone, body=%wide.region_13.24_spmd.clone.clone.sunk | while | flops 485823360 | bytes 9228444 | solution.py:96
  546.8 9.8 custom-call.47
  582.0 9.8 custom-call.47
  617.2 9.8 custom-call.47
  652.5 9.8 custom-call.47
  687.8 9.8 custom-call.47
  723.0 9.8 custom-call.47
  758.3 9.8 custom-call.47
  793.6 9.8 custom-call.47
  830.0 3.7 broadcast_multiply_fusion
  837.2 4.7 pad_add_fusion.3
  845.4 4.0 fusion.230
  849.5 6.1 fusion.177
  860.6 3.2 fusion.232
  864.0 5.5 fusion.172
  870.8 26.2 %reduce-scatter.33.cloned.1.call-done = f32[64,8]{1,0:T(8,128)} async-done(((f32[512,8]{1,0:T(8,128)}), f32[64,8]{1,0:T(8,128)}) %reduce-scatter.33.cloned.1.call-update) | async-done | bytes 2064
  898.5 63.1 %reduce-scatter.31.cloned.1.call-done = f32[128,4]{1,0:T(8,128)} async-done(((f32[1024,4]{1,0:T(8,128)}), f32[128,4]{1,0:T(8,128)}) %reduce-scatter.31.cloned.1.call-update) | async-done | bytes 2064
  963.2 25.2 %reduce-scatter.21.cloned.1.call-done = bf16[128,1024]{1,0:T(8,128)(2,1)} async-done(((bf16[512,1024]{1,0:T(8,128)(2,1)}), bf16[128,1024]{1,0:T(8,128)(2,1)}) %reduce-scatter.21.cloned.1.call-update) | async-done | bytes 262160 | tf_op jit(solution)/shard_map/reduce_scatter | solution.py:119
  989.6 39.6 %all-reduce.21 = (f32[1024]{0:T(1024)}, f32[8]{0:T(128)}, f32[8]{0:T(128)}, f32[256]{0:T(256)}, f32[1024]{0:T(1024)}) all-reduce(f32[1024]{0:T(1024)S(1)} %get-tuple-element.1951, f32[8]{0:T(128)S(1)} %multiply_dynamic-update-slice_fusion.1, f32[8]{0:T(128)S(1)} %dynamic_update_slice.228, ...), channel_id=1, replica_groups=mesh['dp'=8,'tensor'=4] {'dp','tensor'}, use_global_device_ids=true, to_apply=%region_30.31 | all-reduce | flops 2320 | bytes 18560 | tf_op jit(solution)/shard_map/psum | solution.py:224
  1031.5 112.6 %reduce-scatter.23.cloned.1.call-done = f32[128,2,768]{2,0,1:T(8,128)} async-done(((f32[1024,2,768]{2,0,1:T(8,128)}), f32[128,2,768]{2,0,1:T(8,128)}) %reduce-scatter.23.cloned.1.call-update) | async-done | bytes 786448 | tf_op jit(solution)/shard_map/reduce_scatter | solution.py:229
  1146.7 73.2 %reduce-scatter.29.cloned.1.call-done = f32[704,128]{1,0:T(8,128)} async-done(((f32[704,1024]{1,0:T(8,128)}), f32[704,128]{1,0:T(8,128)}) %reduce-scatter.29.cloned.1.call-update) | async-done | bytes 360464 | tf_op jit(solution)/shard_map/reduce_scatter | solution.py:198
  1220.0 71.6 %reduce-scatter.25.cloned.1.call-done = f32[512,128]{1,0:T(8,128)} async-done(((f32[512,1024]{1,0:T(8,128)}), f32[512,128]{1,0:T(8,128)}) %reduce-scatter.25.cloned.1.call-update) | async-done | bytes 262160 | tf_op jit(solution)/shard_map/reduce_scatter | solution.py:232
  1291.6 114.0 %reduce-scatter.27.cloned.1.call-done = f32[128,2,704]{0,2,1:T(8,128)} async-done(((f32[1024,2,704]{0,2,1:T(8,128)}), f32[128,2,704]{0,2,1:T(8,128)}) %reduce-scatter.27.cloned.1.call-update) | async-done | bytes 720912 | tf_op jit(solution)/shard_map/reduce_scatter | solution.py:197
  (794 shorter events, 381.4 us)
Async XLA Ops:
  7.2 61.6 %all-gather.9.cloned.1.call-start = ((), (), s32[]{:S(2)}) async-start(), calls=%async_computation.10 | async-start | bytes 1310720 | tf_op jit(solution)/shard_map/all_gather | solution.py:107
  10.2 82.8 %all-gather.11.cloned.1.call-start = ((), (), s32[]{:S(2)}) async-start(), calls=%async_computation.11 | async-start | bytes 3538944 | tf_op jit(solution)/shard_map/all_gather | solution.py:152
  12.0 281.3 %all-gather.13.cloned.1.call-start = ((), (), s32[]{:S(2)}) async-start(), calls=%async_computation.12 | async-start | bytes 1179648 | tf_op jit(solution)/shard_map/all_gather | solution.py:155
  12.8 314.2 %reduce-scatter.15.cloned.1.call-start = ((), (), s32[]{:S(2)}) async-start(), calls=%async_computation.13 | async-start | bytes 2621440 | tf_op jit(solution)/shard_map/reduce_scatter | solution.py:111
  47.3 51.4 %copy-start.27 = (f32[1,2,512]{2,1,0:T(2,128)}, f32[1,2,512]{2,1,0:T(2,128)S(1)}, u32[]{:S(2)}) copy-start(f32[1,2,512]{2,1,0:T(2,128)S(1)} %copy.162) | copy-start | bytes 12292
  47.5 51.2 %copy-start.29 = (f32[1,2,512]{2,1,0:T(2,128)}, f32[1,2,512]{2,1,0:T(2,128)S(1)}, u32[]{:S(2)}) copy-start(f32[1,2,512]{2,1,0:T(2,128)S(1)} %copy.161) | copy-start | bytes 12292
  47.7 51.0 %copy-start.31 = (f32[1,2,512]{2,1,0:T(2,128)}, f32[1,2,512]{2,1,0:T(2,128)S(1)}, u32[]{:S(2)}) copy-start(f32[1,2,512]{2,1,0:T(2,128)S(1)} %copy.159) | copy-start | bytes 12292
  47.8 49.2 %copy-start.50 = (f32[2]{0:T(128)}, f32[2]{0:T(128)S(1)}, u32[]{:S(2)}) copy-start(f32[2]{0:T(128)S(1)} %fusion.214) | copy-start | bytes 28
  47.9 49.1 %copy-start.52 = (f32[2]{0:T(128)}, f32[2]{0:T(128)S(1)}, u32[]{:S(2)}) copy-start(f32[2]{0:T(128)S(1)} %dynamic_slice.341) | copy-start | bytes 28
  296.7 30.2 %copy-start.12 = (bf16[128,1024]{1,0:T(8,128)(2,1)S(1)}, bf16[128,1024]{1,0:T(8,128)(2,1)}, u32[]{:S(2)}) copy-start(bf16[128,1024]{1,0:T(8,128)(2,1)} %param.17) | copy-start | bytes 786436
  296.7 31.4 %copy-start.26 = (f32[1024]{0:T(1024)S(1)}, f32[1024]{0:T(1024)}, u32[]{:S(2)}) copy-start(f32[1024]{0:T(1024)} %param.26) | copy-start | bytes 12292
  296.8 92.3 %all-gather.17.cloned.1.call-start = ((), (), s32[]{:S(2)}) async-start(), calls=%async_computation.15 | async-start | bytes 3244032 | tf_op jit(solution)/shard_map/all_gather | solution.py:174
  297.4 108.7 %all-gather.15.cloned.1.call-start = ((), (), s32[]{:S(2)}) async-start(), calls=%async_computation.14 | async-start | bytes 1310720 | tf_op jit(solution)/shard_map/all_gather | solution.py:107
  328.1 177.2 %copy-start.5 = (f32[128,1024]{1,0:T(8,128)}, f32[128,1024]{1,0:T(8,128)S(1)}, u32[]{:S(2)}) copy-start(f32[128,1024]{1,0:T(8,128)S(1)} %get-tuple-element.2096) | copy-start | bytes 1572868
  328.2 177.2 %copy-start.48 = (f32[128]{0:T(128)}, f32[128]{0:T(128)S(1)}, u32[]{:S(2)}) copy-start(f32[128]{0:T(128)S(1)} %fusion.216) | copy-start | bytes 1540
  329.0 95.4 %all-gather.21.cloned.1.call-start = ((), (), s32[]{:S(2)}) async-start(), calls=%async_computation.18 | async-start | bytes 1310720 | tf_op jit(solution)/shard_map/all_gather | solution.py:115
  329.8 140.8 %all-gather.19.cloned.1.call-start = ((), (), s32[]{:S(2)}) async-start(), calls=%async_computation.16 | async-start | bytes 1622016 | tf_op jit(solution)/shard_map/all_gather | solution.py:175
  330.5 173.1 %reduce-scatter.19.cloned.1.call-start = ((), (), s32[]{:S(2)}) async-start(), calls=%async_computation.19 | async-start | bytes 1310720 | tf_op jit(solution)/shard_map/reduce_scatter | solution.py:119
  480.1 44.0 %all-gather.23.cloned.1.call-start = ((), (), s32[]{:S(2)}) async-start(), calls=%async_computation.20 | async-start | bytes 1310720 | tf_op jit(solution)/shard_map/all_gather | solution.py:115
  505.3 22.1 %copy-start.59 = (f32[128]{0:T(128)}, f32[128]{0:T(128)S(1)}, u32[]{:S(2)}) copy-start(f32[128]{0:T(128)S(1)} %multiply_multiply_fusion.5) | copy-start | bytes 1540
  507.3 389.7 %reduce-scatter.33.cloned.1.call-start = ((), (), s32[]{:S(2)}) async-start(), calls=%async_computation.27 | async-start | bytes 294912
  562.3 11.5 copy-start.46
  597.5 11.5 copy-start.46
  627.1 8.5 copy-start.13
  632.8 11.5 copy-start.46
  668.1 11.5 copy-start.46
  703.3 11.5 copy-start.46
  738.6 11.5 copy-start.46
  768.1 8.5 copy-start.13
  773.9 11.5 copy-start.46
  809.1 11.5 copy-start.46
  835.6 126.1 %reduce-scatter.31.cloned.1.call-start = ((), (), s32[]{:S(2)}) async-start(), calls=%async_computation.26 | async-start | bytes 589824
  837.0 151.4 %reduce-scatter.21.cloned.1.call-start = ((), (), s32[]{:S(2)}) async-start(), calls=%async_computation.21 | async-start | bytes 1310720 | tf_op jit(solution)/shard_map/reduce_scatter | solution.py:119
  845.3 183.9 %reduce-scatter.17.cloned.1.call-start = ((), (), s32[]{:S(2)}) async-start(), calls=%async_computation.17 | async-start | bytes 2621440 | tf_op jit(solution)/shard_map/reduce_scatter | solution.py:111
  849.4 294.7 %reduce-scatter.23.cloned.1.call-start = ((), (), s32[]{:S(2)}) async-start(), calls=%async_computation.22 | async-start | bytes 7077888 | tf_op jit(solution)/shard_map/reduce_scatter | solution.py:229
  855.6 364.3 %reduce-scatter.29.cloned.1.call-start = ((), (), s32[]{:S(2)}) async-start(), calls=%async_computation.25 | async-start | bytes 3244032 | tf_op jit(solution)/shard_map/reduce_scatter | solution.py:198
  859.6 431.9 %reduce-scatter.25.cloned.1.call-start = ((), (), s32[]{:S(2)}) async-start(), calls=%async_computation.23 | async-start | bytes 2359296 | tf_op jit(solution)/shard_map/reduce_scatter | solution.py:232
  863.9 541.6 %reduce-scatter.27.cloned.1.call-start = ((), (), s32[]{:S(2)}) async-start(), calls=%async_computation.24 | async-start | bytes 6488064 | tf_op jit(solution)/shard_map/reduce_scatter | solution.py:197
  869.5 118.9 %copy-start.33 = (f32[1024]{0:T(1024)S(1)}, f32[1024]{0:T(1024)}, u32[]{:S(2)}) copy-start(f32[1024]{0:T(1024)} %param.18) | copy-start | bytes 12292
  869.5 118.9 %copy-start.55 = (f32[128]{0:T(128)S(1)}, f32[128]{0:T(128)}, u32[]{:S(2)}) copy-start(f32[128]{0:T(128)} %copy-done.54) | copy-start | bytes 1540
  869.5 120.1 %copy-start.44 = (f32[1024]{0:T(1024)S(1)}, f32[1024]{0:T(1024)}, u32[]{:S(2)}) copy-start(f32[1024]{0:T(1024)} %get-tuple-element.1949) | copy-start | bytes 12292
  869.5 120.1 %copy-start.56 = (f32[256]{0:T(256)S(1)}, f32[256]{0:T(256)}, u32[]{:S(2)}) copy-start(f32[256]{0:T(256)} %get-tuple-element.1939) | copy-start | bytes 3076
  869.5 159.7 %copy-start.64 = (f32[128]{0:T(128)S(1)}, f32[128]{0:T(128)}, u32[]{:S(2)}) copy-start(f32[128]{0:T(128)} %copy-done.63) | copy-start | bytes 1540
  869.5 159.7 %copy-start.6 = (f32[128,1024]{1,0:T(8,128)S(1)}, f32[128,1024]{1,0:T(8,128)}, u32[]{:S(2)}) copy-start(f32[128,1024]{1,0:T(8,128)} %copy-done.5) | copy-start | bytes 1572868
  869.5 159.7 %copy-start.19 = (bf16[128,1024]{1,0:T(8,128)(2,1)S(1)}, bf16[128,1024]{1,0:T(8,128)(2,1)}, u32[]{:S(2)}) copy-start(bf16[128,1024]{1,0:T(8,128)(2,1)} %param.29) | copy-start | bytes 786436
  869.5 159.7 %copy-start.20 = (bf16[128,1024]{1,0:T(8,128)(2,1)S(1)}, bf16[128,1024]{1,0:T(8,128)(2,1)}, u32[]{:S(2)}) copy-start(bf16[128,1024]{1,0:T(8,128)(2,1)} %reduce-scatter.19.cloned.1.call-done) | copy-start | bytes 786436
  869.5 159.7 %copy-start.49 = (f32[128]{0:T(128)S(1)}, f32[128]{0:T(128)}, u32[]{:S(2)}) copy-start(f32[128]{0:T(128)} %copy-done.48) | copy-start | bytes 1540
  869.5 159.7 %copy-start.60 = (f32[128]{0:T(128)S(1)}, f32[128]{0:T(128)}, u32[]{:S(2)}) copy-start(f32[128]{0:T(128)} %copy-done.59) | copy-start | bytes 1540
  (68 other events, 264.7 us)
Sparse Core Ops, SparseCore 0:
  10.3 19.4 all-gather.8
  32.5 60.4 all-gather.10
  95.1 39.2 all-gather.12
  296.9 30.0 reduce-scatter.14
  329.0 59.9 all-gather.16
  391.1 14.9 all-gather.14
  407.7 16.7 all-gather.20
  426.7 43.8 all-gather.18
  480.3 23.2 reduce-scatter.18
  507.4 16.6 all-gather.22
  835.7 61.2 reduce-scatter.32
  900.7 60.8 reduce-scatter.30
  964.4 23.9 reduce-scatter.20
  990.8 31.4 reduce-scatter.16
  1026.1 117.9 reduce-scatter.22
  1148.5 71.3 reduce-scatter.28
  1224.3 67.1 reduce-scatter.24
  1296.1 109.3 reduce-scatter.26
where the time goes:
time: 1430 us; the launch traced here: 1410 us
  waiting for transfers between devices  714 us (50%)
  other arithmetic  270 us (19%)
  matrix products  241 us (17%)
  blocking collectives  93.1 us (7%)
  local copies, waits for them, and re-layouts  76 us (5%)
  between operations  15.4 us (1%)
    another operation x48, other arithmetic, group_step(): solved = jax.scipy.linalg.solve_triangular(system, right_side, lower=True)  165 us
    reduce_scatter x1, waiting for transfers between devices, per_device(): lax.psum_scatter(local_gate_up, 'dp', scatter_dimension=0, tiled=True)  114 us
    reduce_scatter x1, waiting for transfers between devices, per_device(): lax.psum_scatter(local_mix, 'dp', scatter_dimension=0, tiled=True)  113 us
    unnamed x20, waiting for transfers between devices  92.1 us
    reduce_scatter x1, waiting for transfers between devices, per_device(): lax.psum_scatter(local_down, 'dp', scatter_dimension=1, tiled=True)  73.2 us
    reduce_scatter x1, waiting for transfers between devices, per_device(): lax.psum_scatter(local_out, 'dp', scatter_dimension=1, tiled=True)  71.6 us
    all_gather x1, waiting for transfers between devices, per_device(): lax.all_gather(w_gate_up, 'dp', axis=0, tiled=True)  58.1 us
    reduce_scatter x2, waiting for transfers between devices, sum_grads(): lax.psum_scatter(partial_sum.astype(jnp.bfloat16), 'tensor', scatter_dime...  48.6 us
  transfers between devices with their start and end apart: 18, of which 15 were waited for; matrix products, arithmetic and copies ran while one was open for 18% of the time, Pallas kernels for 0%

commit v1 on v0

--- a/solution.py
+++ b/solution.py
@@ -10,6 +10,8 @@
 highest = lax.Precision.HIGHEST
 NORM_EPS = 1e-05
 UNIT_EPS = 1e-06
+bf16 = jnp.bfloat16
+f32 = jnp.float32
 
 
 def scale_norm(matrix, scale_gain):
@@ -103,34 +105,117 @@
     return jax.nn.silu(gate_up[:, 0]) * gate_up[:, 1]
 
 
-def gather_rows(row_block):
-    return lax.all_gather(row_block, "tensor", axis=0, tiled=True)
-
-
-def sum_rows(partial_sum):
-    return lax.psum_scatter(partial_sum, "tensor", scatter_dimension=0, tiled=True)
-
-
-def gather_grads(row_block):
-    return lax.all_gather(row_block, "tensor", axis=0, tiled=True)
-
-
-def sum_grads(partial_sum):
-    return lax.psum_scatter(
-        partial_sum.astype(jnp.bfloat16), "tensor", scatter_dimension=0, tiled=True
-    ).astype(jnp.float32)
-
-
-def contract_rows(left, right):
+def rows_dot(left, right, kind=f32):
     return lax.dot_general(
-        left, right, (((0,), (0,)), ((), ())), preferred_element_type=jnp.float32
-    )
-
-
-def contract_cols(left, right):
-    return lax.dot_general(
-        left, right, (((1,), (1,)), ((), ())), preferred_element_type=jnp.float32
-    )
+        left, right, (((0,), (0,)), ((), ())), preferred_element_type=f32
+    ).astype(kind)
+
+
+def cols_dot(left, right):
+    return lax.dot_general(left, right, (((1,), (1,)), ((), ())), preferred_element_type=f32)
+
+
+def dot(left, right):
+    return jnp.dot(left, right, preferred_element_type=f32)
+
+
+def swap(array, axis, size, offset):
+    return lax.ppermute(array, axis, [(i, i ^ offset) for i in range(size)])
+
+
+class Dp:
+    def __init__(self, size):
+        self.size = size
+        self.near = size == 8
+        self.half = size // 2
+        self.offsets = [2 * p for p in range(self.half)] + [2 * p + 1 for p in range(self.half)]
+        self.places = [self.offsets.index(k) for k in range(size)]
+
+    def blocks_to_order(self, array):
+        if not self.near:
+            return array
+        parts = array.reshape(array.shape[:-1] + (self.size, -1))
+        index = lax.axis_index("dp") ^ jnp.array(self.offsets, jnp.int32)
+        return jnp.take(parts, index, axis=-2).reshape(array.shape)
+
+    def blocks_from_order(self, array):
+        if not self.near:
+            return array
+        parts = array.reshape(array.shape[:-1] + (self.size, -1))
+        index = jnp.array(self.places, jnp.int32)[lax.axis_index("dp") ^ jnp.arange(self.size, dtype=jnp.int32)]
+        return jnp.take(parts, index, axis=-2).reshape(array.shape)
+
+    def gather_start(self, shard):
+        return [shard] + [swap(shard, "dp", self.size, 2 * p) for p in range(1, self.half)]
+
+    def gather_end(self, evens):
+        return evens + [swap(e, "dp", self.size, 1) for e in evens]
+
+    def gather(self, shard):
+        if not self.near:
+            whole = lax.all_gather(shard, "dp", axis=0, tiled=False)
+            return [whole[k] for k in range(self.size)]
+        return self.gather_end(self.gather_start(shard))
+
+    def scatter(self, evens, odds, axis):
+        if not self.near:
+            return lax.psum_scatter(
+                jnp.concatenate([evens, odds.astype(evens.dtype)], axis),
+                "dp",
+                scatter_dimension=axis,
+                tiled=True,
+            )
+        kind = odds.dtype
+        summed = evens + swap(odds, "dp", self.size, 1).astype(f32)
+        parts = jnp.split(summed, self.half, axis)
+        total = parts[0]
+        for p in range(1, self.half):
+            total = total + swap(parts[p].astype(kind), "dp", self.size, 2 * p).astype(f32)
+        return total
+
+
+def gather_rows(rows, size):
+    blocks = {0: rows}
+    step = size // 2
+    while step:
+        for k in sorted(blocks):
+            blocks[k ^ step] = swap(blocks[k], "tensor", size, step)
+        step //= 2
+    return [blocks[k] for k in range(size)]
+
+
+def sum_rows(blocks, kind):
+    size = len(blocks)
+    blocks = dict(enumerate(blocks))
+    step = 1
+    while step < size:
+        keep = {k: blocks[k] for k in blocks if not k & step}
+        blocks = {
+            k: keep[k] + swap(blocks[k ^ step].astype(kind), "tensor", size, step).astype(f32)
+            for k in keep
+        }
+        step *= 2
+    return blocks[0]
+
+
+def in_time(blocks):
+    length = blocks[0].shape[0]
+    whole = jnp.zeros((len(blocks) * length,) + blocks[0].shape[1:], blocks[0].dtype)
+    me = lax.axis_index("tensor")
+    for k, block in enumerate(blocks):
+        whole = lax.dynamic_update_slice_in_dim(whole, block, (me ^ k) * length, 0)
+    return whole
+
+
+def from_time(whole, size):
+    length = whole.shape[0] // size
+    me = lax.axis_index("tensor")
+    return [lax.dynamic_slice_in_dim(whole, (me ^ k) * length, length, 0) for k in range(size)]
+
+
+def after(arrays, others):
+    kept, _ = lax.optimization_barrier((arrays, others))
+    return kept
 
 
 def per_device(
@@ -148,94 +233,108 @@
     w_down,
     out_grad,
 ):
-    full_mix, full_rates, full_taps, full_out = (
-        lax.all_gather(w_mix, "dp", axis=0, tiled=True),
-        lax.all_gather(w_rates, "dp", axis=0, tiled=True),
-        lax.all_gather(conv_taps, "dp", axis=2, tiled=True),
-        lax.all_gather(w_out, "dp", axis=1, tiled=True),
-    )
-    resid_in = layer_in.astype(jnp.float32)
+    dp = Dp(lax.axis_size("dp"))
+    ranks = lax.axis_size("tensor")
+    depth, heads_here, head_width = w_mix.shape
+    hidden_here = w_gate_up.shape[2]
+    channels = conv_taps.shape[2] * dp.size
+    taps_shape = conv_taps.shape
+
+    mix_shard = w_mix.reshape(depth, heads_here * head_width)
+    gate_up_shard = w_gate_up.reshape(depth, 2 * hidden_here)
+    small_shard = jnp.concatenate([w_rates.reshape(-1), conv_taps.reshape(-1)])
+    small_size = w_rates.size
+    small_slots = dp.gather(small_shard.reshape(8, -1))
+    mix_slots = dp.gather(mix_shard)
+    mix_full = jnp.concatenate(mix_slots, 0)
+    small_flat = [s.reshape(-1) for s in small_slots]
+    rates_full = jnp.concatenate([s[:small_size].reshape(depth, -1) for s in small_flat], 0)
+    taps_order = jnp.concatenate([s[small_size:].reshape(taps_shape) for s in small_flat], 2)
+    taps_full = dp.blocks_from_order(taps_order).astype(f32)
+
+    resid_in = dp.blocks_to_order(layer_in).astype(f32)
+    mixer_gain = dp.blocks_to_order(mixer_gain)
+    ffn_gain = dp.blocks_to_order(ffn_gain)
+    out_grad = dp.blocks_to_order(out_grad)
+
     normed, norm_back = jax.vjp(scale_norm, resid_in, mixer_gain)
-    normed_all = gather_rows(normed.astype(jnp.bfloat16))
-    project = jnp.einsum("sd,dhc->shc", normed_all, full_mix, preferred_element_type=jnp.float32)
-    rates = jnp.einsum("sd,dhc->shc", normed_all, full_rates, preferred_element_type=jnp.float32)
-    first_head = lax.axis_index("tensor") * full_mix.shape[1]
+    normed_all = in_time(gather_rows(normed.astype(bf16), ranks))
+    out_shard, gate_up_shard, down_shard = after((w_out, gate_up_shard, w_down), mix_full)
+    out_full = jnp.concatenate(dp.gather(out_shard), 1)
+    gate_up_full = jnp.concatenate(dp.gather(gate_up_shard), 0)
+    down_full = jnp.concatenate(dp.gather(down_shard), 1)
+
+    project = dot(normed_all, mix_full).reshape(-1, heads_here, head_width)
+    rates = dot(normed_all, rates_full).reshape(-1, heads_here, 2)
+    first_head = lax.axis_index("tensor") * heads_here
 
     def core_local(project_in, rates_in, taps_in, log_rates, decay_bias, gain_in):
         return mixer_core(project_in, rates_in, taps_in, log_rates, decay_bias, gain_in, first_head)
 
-    gated, core_back = jax.vjp(
-        core_local, project, rates, full_taps.astype(jnp.float32), a_log, dt_bias, head_gain
-    )
-    gated_low = gated.astype(jnp.bfloat16)
-    mixer_out = sum_rows(jnp.dot(gated_low, full_out, preferred_element_type=jnp.float32))
+    gated, core_back = jax.vjp(core_local, project, rates, taps_full, a_log, dt_bias, head_gain)
+    gated_low = gated.astype(bf16)
+    mixer_out = sum_rows(from_time(dot(gated_low, out_full), ranks), bf16)
     resid = resid_in + mixer_out
-    full_gate_up, full_down = (
-        lax.all_gather(w_gate_up, "dp", axis=0, tiled=True),
-        lax.all_gather(w_down, "dp", axis=1, tiled=True),
-    )
     ffn_in, ffn_back = jax.vjp(scale_norm, resid, ffn_gain)
-    ffn_all = gather_rows(ffn_in.astype(jnp.bfloat16))
-    gate_up = jnp.einsum("sd,dgf->sgf", ffn_all, full_gate_up, preferred_element_type=jnp.float32)
+    ffn_all = jnp.concatenate(gather_rows(ffn_in.astype(bf16), ranks), 0)
+    top_grad = jnp.concatenate(gather_rows(out_grad, ranks), 0)
+    gate_up = dot(ffn_all, gate_up_full).reshape(-1, 2, hidden_here)
     hidden, act_back = jax.vjp(gate_product, gate_up)
-    hidden_low = hidden.astype(jnp.bfloat16)
-    ffn_out = sum_rows(jnp.dot(hidden_low, full_down, preferred_element_type=jnp.float32))
-    layer_out = (resid + ffn_out).astype(jnp.bfloat16)
-    top_grad = gather_grads(out_grad)
-    local_down = contract_rows(hidden_low, top_grad)
-    grad_hidden = contract_cols(top_grad, full_down)
+    hidden_low = hidden.astype(bf16)
+    ffn_out = sum_rows(jnp.split(dot(hidden_low, down_full), ranks, 0), bf16)
+    layer_out = dp.blocks_from_order((resid + ffn_out).astype(bf16))
+    half = top_grad.shape[1] // 2
+    grad_hidden = cols_dot(top_grad, down_full)
     (grad_gate_up,) = act_back(grad_hidden)
-    grad_gate_low = grad_gate_up.astype(jnp.bfloat16)
-    local_gate_up = jnp.einsum(
-        "sd,sgf->dgf", ffn_all, grad_gate_low, preferred_element_type=jnp.float32
-    )
-    grad_ffn_in = sum_grads(
-        jnp.einsum("sgf,dgf->sd", grad_gate_low, full_gate_up, preferred_element_type=jnp.float32)
-    )
+    grad_gate_low = grad_gate_up.astype(bf16).reshape(-1, 2 * hidden_here)
+    grad_ffn_in = sum_rows(jnp.split(cols_dot(grad_gate_low, gate_up_full), ranks, 0), bf16)
     grad_resid_norm, grad_ffn_gain = ffn_back(grad_ffn_in)
-    grad_w_gate_up, grad_w_down = (
-        lax.psum_scatter(local_gate_up, "dp", scatter_dimension=0, tiled=True),
-        lax.psum_scatter(local_down, "dp", scatter_dimension=1, tiled=True),
-    )
-    grad_resid = out_grad.astype(jnp.float32) + grad_resid_norm
-    mix_grad = gather_grads(grad_resid.astype(jnp.bfloat16))
-    local_out = contract_rows(gated_low, mix_grad)
-    grad_gated = contract_cols(mix_grad, full_out)
+    grad_resid = out_grad.astype(f32) + grad_resid_norm
+    mix_grad = in_time(gather_rows(grad_resid.astype(bf16), ranks))
+    grad_w_gate_up = dp.scatter(
+        rows_dot(ffn_all[:, :half], grad_gate_low), rows_dot(ffn_all[:, half:], grad_gate_low, bf16), 0
+    )
+    grad_w_down = dp.scatter(
+        rows_dot(hidden_low, top_grad[:, :half]), rows_dot(hidden_low, top_grad[:, half:], bf16), 1
+    )
+    grad_gated = cols_dot(mix_grad, out_full)
+    grad_w_out = dp.scatter(
+        rows_dot(gated_low, mix_grad[:, :half]), rows_dot(gated_low, mix_grad[:, half:], bf16), 1
+    )
     grad_project, grad_rates, local_taps, grad_log_rates, grad_decay_bias, grad_gain_here = (
         core_back(grad_gated)
     )
-    project_low = grad_project.astype(jnp.bfloat16)
-    rates_low = grad_rates.astype(jnp.bfloat16)
-    local_mix = jnp.einsum(
-        "sd,shc->dhc", normed_all, project_low, preferred_element_type=jnp.float32
-    )
-    local_rates = jnp.einsum(
-        "sd,shc->dhc", normed_all, rates_low, preferred_element_type=jnp.float32
-    )
-    back_terms = jnp.einsum(
-        "shc,dhc->sd", project_low, full_mix, preferred_element_type=jnp.float32
-    )
-    back_terms = back_terms + jnp.einsum(
-        "shc,dhc->sd", rates_low, full_rates, preferred_element_type=jnp.float32
-    )
-    grad_normed = sum_grads(back_terms)
+    project_low = grad_project.astype(bf16).reshape(-1, heads_here * head_width)
+    rates_low = grad_rates.astype(bf16).reshape(-1, heads_here * 2)
+    back_terms = cols_dot(project_low, mix_full) + cols_dot(rates_low, rates_full)
+    grad_w_mix = dp.scatter(
+        rows_dot(normed_all[:, :half], project_low), rows_dot(normed_all[:, half:], project_low, bf16), 0
+    )
+    grad_normed = sum_rows(from_time(back_terms, ranks), bf16)
+    local_rates = rows_dot(normed_all, rates_low).reshape(dp.size, -1)
+    local_taps = dp.blocks_to_order(local_taps).reshape(taps_shape[:2] + (dp.size, -1))
+    local_taps = jnp.moveaxis(local_taps, 2, 0).reshape(dp.size, -1)
+    local_small = jnp.concatenate([local_rates, local_taps], 1)
+    summed_small = dp.scatter(local_small[: dp.half], local_small[dp.half :], 0).reshape(-1)
+    grad_w_rates = summed_small[:small_size].reshape(w_rates.shape)
+    grad_conv_taps = summed_small[small_size:].reshape(taps_shape)
     grad_input_norm, grad_gain_first = norm_back(grad_normed)
-    in_grad = grad_resid + grad_input_norm
+    in_grad = dp.blocks_from_order(grad_resid + grad_input_norm)
     grad_mixer_gain, grad_ffn_total, grad_head_gain, grad_a_log, grad_dt_bias = lax.psum(
-        (grad_gain_first, grad_ffn_gain, grad_gain_here, grad_log_rates, grad_decay_bias),
+        (
+            dp.blocks_from_order(grad_gain_first),
+            dp.blocks_from_order(grad_ffn_gain),
+            grad_gain_here,
+            grad_log_rates,
+            grad_decay_bias,
+        ),
         ("dp", "tensor"),
-    )
-    grad_w_mix, grad_w_rates, grad_conv_taps, grad_w_out = (
-        lax.psum_scatter(local_mix, "dp", scatter_dimension=0, tiled=True),
-        lax.psum_scatter(local_rates, "dp", scatter_dimension=0, tiled=True),
-        lax.psum_scatter(local_taps, "dp", scatter_dimension=2, tiled=True),
-        lax.psum_scatter(local_out, "dp", scatter_dimension=1, tiled=True),
     )
     return (
         layer_out,
         in_grad,
         grad_mixer_gain,
-        grad_w_mix,
+        grad_w_mix.reshape(w_mix.shape),
         grad_w_rates,
         grad_conv_taps,
         grad_a_log,
@@ -243,7 +342,7 @@
         grad_head_gain,
         grad_w_out,
         grad_ffn_total,
-        grad_w_gate_up,
+        grad_w_gate_up.reshape(w_gate_up.shape),
         grad_w_down,
     )
 

time: 1430 us -> 1040 us (0.73)
  waiting for transfers between devices: 714 us -> 200 us
  starting transfers between devices: 1.25 us -> 81.2 us
  local copies, waits for them, and re-layouts: 76 us -> 145 us
  blocking collectives: 93.1 us -> 38.4 us
  other arithmetic: 270 us -> 314 us
    reduce_scatter x8 -> x0, waiting for transfers between devices: 450 us -> none  [the longest x1 114 us: per_device(): lax.psum_scatter(local_gate_up, 'dp', scatter_dimension=0, tiled=True)]
    ppermute x0 -> x79, waiting for transfers between devices: none -> 200 us  [swap(): return lax.ppermute(array, axis, [(i, i ^ offset) for i in range(size)])]
    all_gather x8 -> x0, waiting for transfers between devices: 172 us -> none  [the longest x1 58.1 us: per_device(): lax.all_gather(w_gate_up, 'dp', axis=0, tiled=True)]
    unnamed x20 -> x0, waiting for transfers between devices: 92.1 us -> none
    ppermute x0 -> x79, starting transfers between devices: none -> 81.2 us  [swap(): return lax.ppermute(array, axis, [(i, i ^ offset) for i in range(size)])]
    all_gather x2 -> x0, blocking collectives: 53.6 us -> none  [the longest x1 32.7 us: per_device(): lax.all_gather(conv_taps, 'dp', axis=2, tiled=True)]
    unnamed x142 -> x221, local copies, waits for them, and re-layouts: 19.3 us -> 38.7 us
    another operation x48, other arithmetic: 165 us -> 181 us  [group_step(): solved = jax.scipy.linalg.solve_triangular(system, right_side, lower=True)]
  transfers between devices with their start and end apart: 18 -> 79, of which waited for: 15 -> 33; matrix products, arithmetic and copies ran while one was open for 18% -> 64% of each run, Pallas kernels for 0% -> 0%
where the time goes in v1:
time: 1040 us; the launch traced here: 1020 us
  other arithmetic  314 us (30%)
  matrix products  239 us (23%)
  waiting for transfers between devices  200 us (19%)
  local copies, waits for them, and re-layouts  145 us (14%)
  starting transfers between devices  81.2 us (8%)
  blocking collectives  38.4 us (4%)
    ppermute x79, waiting for transfers between devices, swap(): return lax.ppermute(array, axis, [(i, i ^ offset) for i in range(size)])  200 us
    another operation x48, other arithmetic, group_step(): solved = jax.scipy.linalg.solve_triangular(system, right_side, lower=True)  181 us
    ppermute x79, starting transfers between devices, swap(): return lax.ppermute(array, axis, [(i, i ^ offset) for i in range(size)])  81.2 us
    unnamed x221, local copies, waits for them, and re-layouts  38.7 us
    psum x1, blocking collectives, per_device(): lax.psum((dp.blocks_from_order(grad_gain_first), dp.blocks_from_order(gra...  38.4 us
    dynamic_update_slice x48, other arithmetic, mixer_core(): final_state, outputs = lax.scan(group_step, initial, blocks)  38.3 us
    dot_general x24, matrix products, group_step(): jnp.einsum('hcd,hde->hce', queries, state_now, precision=highest)  35.6 us
    dot_general x24, matrix products, group_step(): jnp.einsum('hid,hjd->hij', queries, key_rows, precision=highest) * decay_map  29.9 us
  transfers between devices with their start and end apart: 79, of which 33 were waited for; matrix products, arithmetic and copies ran while one was open for 64% of the time, Pallas kernels for 0%

profile of v1, /device:TPU:0, one launch (start us, length us, event | category | flops | bytes accessed | tf_op | source)
XLA Modules:
  0.0 1021.6 jit_solution(6913263290509508047)
XLA Ops:
  24.0 3.6 collective-permute-start.11
  29.4 3.0 collective-permute-done.7
  33.0 3.0 collective-permute-done.8
  46.8 3.3 collective-permute-done.48
  67.0 6.7 collective-permute-done.15
  75.4 5.6 collective-permute-done.16
  81.8 5.3 fusion.253
  87.1 5.7 reshape.885
  103.1 3.0 collective-permute-start.18
  113.8 237.1 %while.88 = (s32[]{:T(128)}, f32[2,128,256]{2,1,0:T(8,128)S(1)}, f32[8,2,64,256]{3,2,0,1:T(8,128)S(1)}, f32[8,2,64,64]{3,2,1,0:T(8,128)}, f32[8,2,64,64]{3,2,1,0...) while((s32[]{:T(128)}, f32[2,128,256]{2,1,0:T(8,128)S(1)}, ...), condition=%wide.region_5.8_spmd.clone.clone, body=%wide.region_3.7_spmd.clone.clone.sunk | while | flops 239907328 | bytes 5322673 | solution.py:98
  121.3 11.2 %custom-call.88 = f32[2,1,64,64]{2,3,1,0:T(8,128)} custom-call(f32[2,1,64,64]{3,2,1,0:T(8,128)} %select_bitcast_fusion.10), custom_call_target="InvertDiagBlocksLowerTriangular" | custom-call | tf_op jit(solution)/shard_map/jvp()/while/body/eval_jaxpr/jit(_solve_triangular)/vmap()/triangular_solve | solution.py:47
  150.9 11.2 %custom-call.88 = f32[2,1,64,64]{2,3,1,0:T(8,128)} custom-call(f32[2,1,64,64]{3,2,1,0:T(8,128)} %select_bitcast_fusion.10), custom_call_target="InvertDiagBlocksLowerTriangular" | custom-call | tf_op jit(solution)/shard_map/jvp()/while/body/eval_jaxpr/jit(_solve_triangular)/vmap()/triangular_solve | solution.py:47
  180.4 11.2 %custom-call.88 = f32[2,1,64,64]{2,3,1,0:T(8,128)} custom-call(f32[2,1,64,64]{3,2,1,0:T(8,128)} %select_bitcast_fusion.10), custom_call_target="InvertDiagBlocksLowerTriangular" | custom-call | tf_op jit(solution)/shard_map/jvp()/while/body/eval_jaxpr/jit(_solve_triangular)/vmap()/triangular_solve | solution.py:47
  210.1 11.2 %custom-call.88 = f32[2,1,64,64]{2,3,1,0:T(8,128)} custom-call(f32[2,1,64,64]{3,2,1,0:T(8,128)} %select_bitcast_fusion.10), custom_call_target="InvertDiagBlocksLowerTriangular" | custom-call | tf_op jit(solution)/shard_map/jvp()/while/body/eval_jaxpr/jit(_solve_triangular)/vmap()/triangular_solve | solution.py:47
  239.7 11.2 %custom-call.88 = f32[2,1,64,64]{2,3,1,0:T(8,128)} custom-call(f32[2,1,64,64]{3,2,1,0:T(8,128)} %select_bitcast_fusion.10), custom_call_target="InvertDiagBlocksLowerTriangular" | custom-call | tf_op jit(solution)/shard_map/jvp()/while/body/eval_jaxpr/jit(_solve_triangular)/vmap()/triangular_solve | solution.py:47
  269.2 11.2 %custom-call.88 = f32[2,1,64,64]{2,3,1,0:T(8,128)} custom-call(f32[2,1,64,64]{3,2,1,0:T(8,128)} %select_bitcast_fusion.10), custom_call_target="InvertDiagBlocksLowerTriangular" | custom-call | tf_op jit(solution)/shard_map/jvp()/while/body/eval_jaxpr/jit(_solve_triangular)/vmap()/triangular_solve | solution.py:47
  298.9 11.2 %custom-call.88 = f32[2,1,64,64]{2,3,1,0:T(8,128)} custom-call(f32[2,1,64,64]{3,2,1,0:T(8,128)} %select_bitcast_fusion.10), custom_call_target="InvertDiagBlocksLowerTriangular" | custom-call | tf_op jit(solution)/shard_map/jvp()/while/body/eval_jaxpr/jit(_solve_triangular)/vmap()/triangular_solve | solution.py:47
  328.6 11.2 %custom-call.88 = f32[2,1,64,64]{2,3,1,0:T(8,128)} custom-call(f32[2,1,64,64]{3,2,1,0:T(8,128)} %select_bitcast_fusion.10), custom_call_target="InvertDiagBlocksLowerTriangular" | custom-call | tf_op jit(solution)/shard_map/jvp()/while/body/eval_jaxpr/jit(_solve_triangular)/vmap()/triangular_solve | solution.py:47
  369.3 9.9 collective-permute-done.37
  381.5 20.1 %collective-permute-done.38 = bf16[704,128]{1,0:T(8,128)(2,1)S(1)} collective-permute-done((bf16[704,128]{1,0:T(8,128)(2,1)S(1)}, bf16[704,128]{1,0:T(8,128)(2,1)S(1)}, u32[]{:S(2)}, u32[]{:S(2)}) %collective-permute-start.38) | collective-permute-done | bytes 180256 | tf_op jit(solution)/shard_map/ppermute | solution.py:123
  425.0 4.9 collective-permute-done.41
  435.3 4.4 collective-permute-done.26
  442.4 4.5 collective-permute-done.28
  446.8 3.1 collective-permute-done.35
  450.0 7.1 collective-permute-done.36
  472.9 4.6 collective-permute-done.52
  477.4 4.4 collective-permute-done.46
  488.9 27.5 %collective-permute-done.75 = bf16[704,512]{1,0:T(8,128)(2,1)} collective-permute-done((bf16[704,512]{1,0:T(8,128)(2,1)}, bf16[704,512]{1,0:T(8,128)(2,1)}, u32[]{:S(2)}, u32[]{:S(2)}) %collective-permute-start.75) | collective-permute-done | bytes 720928 | tf_op jit(solution)/shard_map/ppermute | solution.py:123
  525.0 3.0 collective-permute-done.78
  528.1 7.6 collective-permute-done.77
  541.8 3.1 multiply_reduce_fusion.4
  549.6 285.2 %while.89 = (s32[]{:T(128)}, f32[2,128,256]{2,1,0:T(8,128)S(1)}, f32[8,2,64,128]{3,2,0,1:T(8,128)}, f32[8,2,64,128]{3,2,0,1:T(8,128)}, f32[8,2,64,256]{3,2,0,1:T...) while((s32[]{:T(128)}, f32[2,128,256]{2,1,0:T(8,128)S(1)}, ...), condition=%wide.region_21.24_spmd.clone.clone, body=%wide.region_10.23_spmd.clone.clone.sunk | while | flops 485823360 | bytes 8181820 | solution.py:98
  555.2 9.8 custom-call.89
  590.9 9.8 custom-call.89
  626.6 9.8 custom-call.89
  662.2 9.8 custom-call.89
  697.8 9.8 custom-call.89
  733.4 9.8 custom-call.89
  769.1 9.8 custom-call.89
  804.7 9.8 custom-call.89
  844.5 3.2 multiply_reduce_fusion.2
  855.7 5.1 convolution_add_fusion.11
  879.7 4.6 fusion.250
  898.8 22.0 %collective-permute-done.67 = bf16[512,512]{1,0:T(8,128)(2,1)} collective-permute-done((bf16[512,512]{1,0:T(8,128)(2,1)}, bf16[512,512]{1,0:T(8,128)(2,1)}, u32[]{:S(2)}, u32[]{:S(2)}) %collective-permute-start.67) | collective-permute-done | bytes 524320 | tf_op jit(solution)/shard_map/ppermute | solution.py:123
  928.0 38.4 %all-reduce.21 = (f32[1024]{0:T(1024)}, f32[8]{0:T(128)}, f32[8]{0:T(128)}, f32[256]{0:T(256)}, f32[1024]{0:T(1024)}) all-reduce(f32[1024]{0:T(1024)S(1)} %get-tuple-element.2183, f32[8]{0:T(128)S(1)} %multiply_dynamic-update-slice_fusion.1, f32[8]{0:T(128)S(1)} %dynamic_update_slice.260, ...), channel_id=1, replica_groups=mesh['dp'=8,'tensor'=4] {'dp','tensor'}, use_global_device_ids=true, to_apply=%region_26.29 | all-reduce | flops 2320 | bytes 18560 | tf_op jit(solution)/shard_map/psum | solution.py:323
  970.8 4.2 fusion.248
  979.5 22.5 %collective-permute-done.73 = bf16[128,1408]{1,0:T(8,128)(2,1)S(1)} collective-permute-done((bf16[128,1408]{1,0:T(8,128)(2,1)}, bf16[128,1408]{1,0:T(8,128)(2,1)S(1)}, u32[]{:S(2)}, u32[]{:S(2)}) %collective-permute-start.73) | collective-permute-done | bytes 360480 | tf_op jit(solution)/shard_map/ppermute | solution.py:123
  1004.5 14.2 %collective-permute-done.61 = bf16[128,1536]{1,0:T(8,128)(2,1)S(1)} collective-permute-done((bf16[128,1536]{1,0:T(8,128)(2,1)S(1)}, bf16[128,1536]{1,0:T(8,128)(2,1)S(1)}, u32[]{:S(2)}, u32[]{:S(2)}) %collective-permute-start.61) | collective-permute-done | bytes 393248 | tf_op jit(solution)/shard_map/ppermute | solution.py:123
  (1026 shorter events, 591.8 us)
Async XLA Ops:
  9.7 33.0 %collective-permute-start = (bf16[128,1024]{1,0:T(8,128)(2,1)}, bf16[128,1024]{1,0:T(8,128)(2,1)}, u32[]{:S(2)}, u32[]{:S(2)}) collective-permute-start(bf16[128,1024]{1,0:T(8,128)(2,1)} %get-tuple-element.2080), channel_id=1, source_target_pairs={{0,1},{1,0},{2,3},{3,2},{4,5},{5,4},{6,7},{7,6},{8,9},{9,8},{10,11... | collective-permute-start | bytes 786440 | tf_op jit(solution)/shard_map/ppermute | solution.py:123
  10.1 34.2 %collective-permute-start.1 = (bf16[128,1024]{1,0:T(8,128)(2,1)}, bf16[128,1024]{1,0:T(8,128)(2,1)}, u32[]{:S(2)}, u32[]{:S(2)}) collective-permute-start(bf16[128,1024]{1,0:T(8,128)(2,1)} %get-tuple-element.2080), channel_id=1, source_target_pairs={{0,2},{1,3},{2,0},{3,1},{4,6},{5,7},{6,4},{7,5},{8,10},{9,11},{10,... | collective-permute-start | bytes 786440 | tf_op jit(solution)/shard_map/ppermute | solution.py:123
  23.2 28.6 %collective-permute-start.10 = (bf16[128,1536]{1,0:T(8,128)(2,1)S(1)}, bf16[128,1536]{1,0:T(8,128)(2,1)S(1)}, u32[]{:S(2)}, u32[]{:S(2)}) collective-permute-start(bf16[128,1536]{1,0:T(8,128)(2,1)S(1)} %bitcast.660), channel_id=1, source_target_pairs={{0,8},{4,12},{8,0},{12,4},{16,24},{20,28},{24,16},{28,20},{1,9},{5... | collective-permute-start | bytes 1179656 | tf_op jit(solution)/shard_map/ppermute | solution.py:123
  24.0 29.1 %collective-permute-start.11 = (bf16[128,1536]{1,0:T(8,128)(2,1)S(1)}, bf16[128,1536]{1,0:T(8,128)(2,1)S(1)}, u32[]{:S(2)}, u32[]{:S(2)}) collective-permute-start(bf16[128,1536]{1,0:T(8,128)(2,1)S(1)} %bitcast.661), channel_id=1, source_target_pairs={{0,16},{4,20},{8,24},{12,28},{16,0},{20,4},{24,8},{28,12},{1,17},{... | collective-permute-start | bytes 1179656 | tf_op jit(solution)/shard_map/ppermute | solution.py:123
  42.6 12.8 %collective-permute-start.12 = (bf16[128,1536]{1,0:T(8,128)(2,1)S(1)}, bf16[128,1536]{1,0:T(8,128)(2,1)S(1)}, u32[]{:S(2)}, u32[]{:S(2)}) collective-permute-start(bf16[128,1536]{1,0:T(8,128)(2,1)S(1)} %bitcast.662), channel_id=1, source_target_pairs={{0,24},{4,28},{8,16},{12,20},{16,8},{20,12},{24,0},{28,4},{1,25},{... | collective-permute-start | bytes 1179656 | tf_op jit(solution)/shard_map/ppermute | solution.py:123
  44.3 12.5 %collective-permute-start.13 = (bf16[128,1536]{1,0:T(8,128)(2,1)S(1)}, bf16[128,1536]{1,0:T(8,128)(2,1)S(1)}, u32[]{:S(2)}, u32[]{:S(2)}) collective-permute-start(bf16[128,1536]{1,0:T(8,128)(2,1)S(1)} %bitcast.663), channel_id=1, source_target_pairs={{0,4},{4,0},{8,12},{12,8},{16,20},{20,16},{24,28},{28,24},{1,5},{5... | collective-permute-start | bytes 1179656 | tf_op jit(solution)/shard_map/ppermute | solution.py:123
  53.1 12.1 %collective-permute-start.14 = (bf16[128,1536]{1,0:T(8,128)(2,1)S(1)}, bf16[128,1536]{1,0:T(8,128)(2,1)}, u32[]{:S(2)}, u32[]{:S(2)}) collective-permute-start(bf16[128,1536]{1,0:T(8,128)(2,1)S(1)} %collective-permute-done.10), channel_id=1, source_target_pairs={{0,4},{4,0},{8,12},{12,8},{16,20},{20,16},{24,28},{28,24},{1,5},{5... | collective-permute-start | bytes 1179656 | tf_op jit(solution)/shard_map/ppermute | solution.py:123
  55.5 18.1 %collective-permute-start.15 = (bf16[128,1536]{1,0:T(8,128)(2,1)S(1)}, bf16[128,1536]{1,0:T(8,128)(2,1)}, u32[]{:S(2)}, u32[]{:S(2)}) collective-permute-start(bf16[128,1536]{1,0:T(8,128)(2,1)S(1)} %collective-permute-done.11), channel_id=1, source_target_pairs={{0,4},{4,0},{8,12},{12,8},{16,20},{20,16},{24,28},{28,24},{1,5},{5... | collective-permute-start | bytes 1179656 | tf_op jit(solution)/shard_map/ppermute | solution.py:123
  56.8 24.2 %collective-permute-start.16 = (bf16[128,1536]{1,0:T(8,128)(2,1)S(1)}, bf16[128,1536]{1,0:T(8,128)(2,1)S(1)}, u32[]{:S(2)}, u32[]{:S(2)}) collective-permute-start(bf16[128,1536]{1,0:T(8,128)(2,1)S(1)} %collective-permute-done.12), channel_id=1, source_target_pairs={{0,4},{4,0},{8,12},{12,8},{16,20},{20,16},{24,28},{28,24},{1,5},{5... | collective-permute-start | bytes 1179656 | tf_op jit(solution)/shard_map/ppermute | solution.py:123
  103.1 252.6 %collective-permute-start.17 = (bf16[512,128]{1,0:T(8,128)(2,1)}, bf16[512,128]{1,0:T(8,128)(2,1)}, u32[]{:S(2)}, u32[]{:S(2)}) collective-permute-start(bf16[512,128]{1,0:T(8,128)(2,1)} %param.39), channel_id=1, source_target_pairs={{0,8},{4,12},{8,0},{12,4},{16,24},{20,28},{24,16},{28,20},{1,9},{5... | collective-permute-start | bytes 393224 | tf_op jit(solution)/shard_map/ppermute | solution.py:123
  103.1 257.0 %collective-permute-start.18 = (bf16[512,128]{1,0:T(8,128)(2,1)}, bf16[512,128]{1,0:T(8,128)(2,1)}, u32[]{:S(2)}, u32[]{:S(2)}) collective-permute-start(bf16[512,128]{1,0:T(8,128)(2,1)} %param.39), channel_id=1, source_target_pairs={{0,16},{4,20},{8,24},{12,28},{16,0},{20,4},{24,8},{28,12},{1,17},{... | collective-permute-start | bytes 393224 | tf_op jit(solution)/shard_map/ppermute | solution.py:123
  106.2 257.2 %collective-permute-start.19 = (bf16[512,128]{1,0:T(8,128)(2,1)}, bf16[512,128]{1,0:T(8,128)(2,1)}, u32[]{:S(2)}, u32[]{:S(2)}) collective-permute-start(bf16[512,128]{1,0:T(8,128)(2,1)} %param.39), channel_id=1, source_target_pairs={{0,24},{4,28},{8,16},{12,20},{16,8},{20,12},{24,0},{28,4},{1,25},{... | collective-permute-start | bytes 393224 | tf_op jit(solution)/shard_map/ppermute | solution.py:123
  107.5 257.5 %collective-permute-start.20 = (bf16[512,128]{1,0:T(8,128)(2,1)}, bf16[512,128]{1,0:T(8,128)(2,1)}, u32[]{:S(2)}, u32[]{:S(2)}) collective-permute-start(bf16[512,128]{1,0:T(8,128)(2,1)} %param.39), channel_id=1, source_target_pairs={{0,4},{4,0},{8,12},{12,8},{16,20},{20,16},{24,28},{28,24},{1,5},{5... | collective-permute-start | bytes 393224 | tf_op jit(solution)/shard_map/ppermute | solution.py:123
  110.1 311.2 %collective-permute-start.30 = (bf16[128,1408]{0,1:T(8,128)(2,1)}, bf16[128,1408]{0,1:T(8,128)(2,1)}, u32[]{:S(2)}, u32[]{:S(2)}) collective-permute-start(bf16[128,1408]{0,1:T(8,128)(2,1)} %bitcast.25), channel_id=1, source_target_pairs={{0,8},{4,12},{8,0},{12,4},{16,24},{20,28},{24,16},{28,20},{1,9},{5... | collective-permute-start | bytes 1081352 | tf_op jit(solution)/shard_map/ppermute | solution.py:123
  355.8 67.8 %collective-permute-start.31 = (bf16[128,1408]{0,1:T(8,128)(2,1)}, bf16[128,1408]{0,1:T(8,128)(2,1)S(1)}, u32[]{:S(2)}, u32[]{:S(2)}) collective-permute-start(bf16[128,1408]{0,1:T(8,128)(2,1)} %bitcast.25), channel_id=1, source_target_pairs={{0,16},{4,20},{8,24},{12,28},{16,0},{20,4},{24,8},{28,12},{1,17},{... | collective-permute-start | bytes 1081352 | tf_op jit(solution)/shard_map/ppermute | solution.py:123
  360.1 64.6 %collective-permute-start.32 = (bf16[128,1408]{0,1:T(8,128)(2,1)}, bf16[128,1408]{0,1:T(8,128)(2,1)S(1)}, u32[]{:S(2)}, u32[]{:S(2)}) collective-permute-start(bf16[128,1408]{0,1:T(8,128)(2,1)} %bitcast.25), channel_id=1, source_target_pairs={{0,24},{4,28},{8,16},{12,20},{16,8},{20,12},{24,0},{28,4},{1,25},{... | collective-permute-start | bytes 1081352 | tf_op jit(solution)/shard_map/ppermute | solution.py:123
  363.4 15.8 %collective-permute-start.37 = (bf16[704,128]{1,0:T(8,128)(2,1)S(1)}, bf16[704,128]{1,0:T(8,128)(2,1)S(1)}, u32[]{:S(2)}, u32[]{:S(2)}) collective-permute-start(bf16[704,128]{1,0:T(8,128)(2,1)S(1)} %copy-done.34), channel_id=1, source_target_pairs={{0,8},{4,12},{8,0},{12,4},{16,24},{20,28},{24,16},{28,20},{1,9},{5... | collective-permute-start | bytes 540680 | tf_op jit(solution)/shard_map/ppermute | solution.py:123
  365.0 36.7 %collective-permute-start.38 = (bf16[704,128]{1,0:T(8,128)(2,1)S(1)}, bf16[704,128]{1,0:T(8,128)(2,1)S(1)}, u32[]{:S(2)}, u32[]{:S(2)}) collective-permute-start(bf16[704,128]{1,0:T(8,128)(2,1)S(1)} %copy-done.34), channel_id=1, source_target_pairs={{0,16},{4,20},{8,24},{12,28},{16,0},{20,4},{24,8},{28,12},{1,17},{... | collective-permute-start | bytes 540680 | tf_op jit(solution)/shard_map/ppermute | solution.py:123
  379.2 24.1 %collective-permute-start.39 = (bf16[704,128]{1,0:T(8,128)(2,1)S(1)}, bf16[704,128]{1,0:T(8,128)(2,1)S(1)}, u32[]{:S(2)}, u32[]{:S(2)}) collective-permute-start(bf16[704,128]{1,0:T(8,128)(2,1)S(1)} %copy-done.34), channel_id=1, source_target_pairs={{0,24},{4,28},{8,16},{12,20},{16,8},{20,12},{24,0},{28,4},{1,25},{... | collective-permute-start | bytes 540680 | tf_op jit(solution)/shard_map/ppermute | solution.py:123
  414.4 18.6 %collective-permute-start.33 = (bf16[128,1408]{0,1:T(8,128)(2,1)}, bf16[128,1408]{0,1:T(8,128)(2,1)S(1)}, u32[]{:S(2)}, u32[]{:S(2)}) collective-permute-start(bf16[128,1408]{0,1:T(8,128)(2,1)} %bitcast.25), channel_id=1, source_target_pairs={{0,4},{4,0},{8,12},{12,8},{16,20},{20,16},{24,28},{28,24},{1,5},{5... | collective-permute-start | bytes 1081352 | tf_op jit(solution)/shard_map/ppermute | solution.py:123
  417.5 12.4 %collective-permute-start.41 = (bf16[704,128]{1,0:T(8,128)(2,1)S(1)}, bf16[704,128]{1,0:T(8,128)(2,1)S(1)}, u32[]{:S(2)}, u32[]{:S(2)}) collective-permute-start(bf16[704,128]{1,0:T(8,128)(2,1)S(1)} %collective-permute-done.37), channel_id=1, source_target_pairs={{0,4},{4,0},{8,12},{12,8},{16,20},{20,16},{24,28},{28,24},{1,5},{5... | collective-permute-start | bytes 540680 | tf_op jit(solution)/shard_map/ppermute | solution.py:123
  421.3 10.7 %collective-permute-start.42 = (bf16[704,128]{1,0:T(8,128)(2,1)S(1)}, bf16[704,128]{1,0:T(8,128)(2,1)S(1)}, u32[]{:S(2)}, u32[]{:S(2)}) collective-permute-start(bf16[704,128]{1,0:T(8,128)(2,1)S(1)} %collective-permute-done.38), channel_id=1, source_target_pairs={{0,4},{4,0},{8,12},{12,8},{16,20},{20,16},{24,28},{28,24},{1,5},{5... | collective-permute-start | bytes 540680 | tf_op jit(solution)/shard_map/ppermute | solution.py:123
  423.6 17.4 %collective-permute-start.43 = (bf16[704,128]{1,0:T(8,128)(2,1)S(1)}, bf16[704,128]{1,0:T(8,128)(2,1)S(1)}, u32[]{:S(2)}, u32[]{:S(2)}) collective-permute-start(bf16[704,128]{1,0:T(8,128)(2,1)S(1)} %collective-permute-done.39), channel_id=1, source_target_pairs={{0,4},{4,0},{8,12},{12,8},{16,20},{20,16},{24,28},{28,24},{1,5},{5... | collective-permute-start | bytes 540680 | tf_op jit(solution)/shard_map/ppermute | solution.py:123
  429.9 12.2 %collective-permute-start.34 = (bf16[128,1408]{0,1:T(8,128)(2,1)}, bf16[128,1408]{0,1:T(8,128)(2,1)S(1)}, u32[]{:S(2)}, u32[]{:S(2)}) collective-permute-start(bf16[128,1408]{0,1:T(8,128)(2,1)} %collective-permute-done.30), channel_id=1, source_target_pairs={{0,4},{4,0},{8,12},{12,8},{16,20},{20,16},{24,28},{28,24},{1,5},{5... | collective-permute-start | bytes 1081352 | tf_op jit(solution)/shard_map/ppermute | solution.py:123
  433.0 16.9 %collective-permute-start.35 = (bf16[128,1408]{0,1:T(8,128)(2,1)S(1)}, bf16[128,1408]{0,1:T(8,128)(2,1)S(1)}, u32[]{:S(2)}, u32[]{:S(2)}) collective-permute-start(bf16[128,1408]{0,1:T(8,128)(2,1)S(1)} %collective-permute-done.31), channel_id=1, source_target_pairs={{0,4},{4,0},{8,12},{12,8},{16,20},{20,16},{24,28},{28,24},{1,5},{5... | collective-permute-start | bytes 1081352 | tf_op jit(solution)/shard_map/ppermute | solution.py:123
  434.3 22.8 %collective-permute-start.36 = (bf16[128,1408]{0,1:T(8,128)(2,1)S(1)}, bf16[128,1408]{0,1:T(8,128)(2,1)S(1)}, u32[]{:S(2)}, u32[]{:S(2)}) collective-permute-start(bf16[128,1408]{0,1:T(8,128)(2,1)S(1)} %collective-permute-done.32), channel_id=1, source_target_pairs={{0,4},{4,0},{8,12},{12,8},{16,20},{20,16},{24,28},{28,24},{1,5},{5... | collective-permute-start | bytes 1081352 | tf_op jit(solution)/shard_map/ppermute | solution.py:123
  442.3 14.9 %collective-permute-start.27 = (bf16[128,1024]{1,0:T(8,128)(2,1)S(1)}, bf16[128,1024]{1,0:T(8,128)(2,1)S(1)}, u32[]{:S(2)}, u32[]{:S(2)}) collective-permute-start(bf16[128,1024]{1,0:T(8,128)(2,1)S(1)} %multiply_convert_fusion.2), channel_id=1, source_target_pairs={{0,1},{1,0},{2,3},{3,2},{4,5},{5,4},{6,7},{7,6},{8,9},{9,8},{10,11... | collective-permute-start | bytes 786440 | tf_op jit(solution)/shard_map/ppermute | solution.py:123
  467.1 412.6 %collective-permute-start.71 = (bf16[512,1408]{1,0:T(8,128)(2,1)}, bf16[512,1408]{1,0:T(8,128)(2,1)}, u32[]{:S(2)}, u32[]{:S(2)}) collective-permute-start(bf16[512,1408]{1,0:T(8,128)(2,1)} %convolution_convert_fusion), channel_id=1, source_target_pairs={{0,4},{4,0},{8,12},{12,8},{16,20},{20,16},{24,28},{28,24},{1,5},{5... | collective-permute-start | bytes 4325384 | tf_op jit(solution)/shard_map/ppermute | solution.py:123
  469.4 12.5 %collective-permute-start.46 = (bf16[128,1024]{1,0:T(8,128)(2,1)S(1)}, bf16[128,1024]{1,0:T(8,128)(2,1)S(1)}, u32[]{:S(2)}, u32[]{:S(2)}) collective-permute-start(bf16[128,1024]{1,0:T(8,128)(2,1)S(1)} %fusion.193), channel_id=1, source_target_pairs={{0,2},{1,3},{2,0},{3,1},{4,6},{5,7},{6,4},{7,5},{8,10},{9,11},{10,... | collective-permute-start | bytes 786440 | tf_op jit(solution)/shard_map/ppermute | solution.py:123
  471.8 44.7 %collective-permute-start.75 = (bf16[704,512]{1,0:T(8,128)(2,1)}, bf16[704,512]{1,0:T(8,128)(2,1)}, u32[]{:S(2)}, u32[]{:S(2)}) collective-permute-start(bf16[704,512]{1,0:T(8,128)(2,1)} %convolution_convert_fusion.2), channel_id=1, source_target_pairs={{0,4},{4,0},{8,12},{12,8},{16,20},{20,16},{24,28},{28,24},{1,5},{5... | collective-permute-start | bytes 2162696 | tf_op jit(solution)/shard_map/ppermute | solution.py:123
  484.7 36.1 %collective-permute-start.53 = (bf16[128,1024]{1,0:T(8,128)(2,1)}, bf16[128,1024]{1,0:T(8,128)(2,1)}, u32[]{:S(2)}, u32[]{:S(2)}) collective-permute-start(bf16[128,1024]{1,0:T(8,128)(2,1)} %get-tuple-element.2073), channel_id=1, source_target_pairs={{0,1},{1,0},{2,3},{3,2},{4,5},{5,4},{6,7},{7,6},{8,9},{9,8},{10,11... | collective-permute-start | bytes 786440 | tf_op jit(solution)/shard_map/ppermute | solution.py:123
  484.7 38.4 %collective-permute-start.54 = (bf16[128,1024]{1,0:T(8,128)(2,1)}, bf16[128,1024]{1,0:T(8,128)(2,1)}, u32[]{:S(2)}, u32[]{:S(2)}) collective-permute-start(bf16[128,1024]{1,0:T(8,128)(2,1)} %get-tuple-element.2073), channel_id=1, source_target_pairs={{0,2},{1,3},{2,0},{3,1},{4,6},{5,7},{6,4},{7,5},{8,10},{9,11},{10,... | collective-permute-start | bytes 786440 | tf_op jit(solution)/shard_map/ppermute | solution.py:123
  520.7 14.9 %collective-permute-start.77 = (bf16[704,128]{1,0:T(8,128)(2,1)S(1)}, bf16[704,128]{1,0:T(8,128)(2,1)S(1)}, u32[]{:S(2)}, u32[]{:S(2)}) collective-permute-start(bf16[704,128]{1,0:T(8,128)(2,1)S(1)} %get-tuple-element.2152), channel_id=1, source_target_pairs={{0,16},{4,20},{8,24},{12,28},{16,0},{20,4},{24,8},{28,12},{1,17},{... | collective-permute-start | bytes 540680 | tf_op jit(solution)/shard_map/ppermute | solution.py:123
  520.7 14.9 %collective-permute-start.76 = (bf16[704,128]{1,0:T(8,128)(2,1)S(1)}, bf16[704,128]{1,0:T(8,128)(2,1)S(1)}, u32[]{:S(2)}, u32[]{:S(2)}) collective-permute-start(bf16[704,128]{1,0:T(8,128)(2,1)S(1)} %get-tuple-element.2150), channel_id=1, source_target_pairs={{0,8},{4,12},{8,0},{12,4},{16,24},{20,28},{24,16},{28,20},{1,9},{5... | collective-permute-start | bytes 540680 | tf_op jit(solution)/shard_map/ppermute | solution.py:123
  523.1 13.4 %collective-permute-start.55 = (bf16[128,1024]{1,0:T(8,128)(2,1)}, bf16[128,1024]{1,0:T(8,128)(2,1)S(1)}, u32[]{:S(2)}, u32[]{:S(2)}) collective-permute-start(bf16[128,1024]{1,0:T(8,128)(2,1)} %collective-permute-done.54), channel_id=1, source_target_pairs={{0,1},{1,0},{2,3},{3,2},{4,5},{5,4},{6,7},{7,6},{8,9},{9,8},{10,11... | collective-permute-start | bytes 786440 | tf_op jit(solution)/shard_map/ppermute | solution.py:123
  866.4 10.8 %collective-permute-start.57 = (bf16[128,1024]{1,0:T(8,128)(2,1)}, bf16[128,1024]{1,0:T(8,128)(2,1)}, u32[]{:S(2)}, u32[]{:S(2)}) collective-permute-start(bf16[128,1024]{1,0:T(8,128)(2,1)} %get-tuple-element.2129), channel_id=1, source_target_pairs={{0,1},{1,0},{2,3},{3,2},{4,5},{5,4},{6,7},{7,6},{8,9},{9,8},{10,11... | collective-permute-start | bytes 786440 | tf_op jit(solution)/shard_map/ppermute | solution.py:123
  872.4 14.5 %collective-permute-start.56 = (bf16[128,1024]{1,0:T(8,128)(2,1)}, bf16[128,1024]{1,0:T(8,128)(2,1)}, u32[]{:S(2)}, u32[]{:S(2)}) collective-permute-start(bf16[128,1024]{1,0:T(8,128)(2,1)} %get-tuple-element.2128), channel_id=1, source_target_pairs={{0,1},{1,0},{2,3},{3,2},{4,5},{5,4},{6,7},{7,6},{8,9},{9,8},{10,11... | collective-permute-start | bytes 786440 | tf_op jit(solution)/shard_map/ppermute | solution.py:123
  873.5 97.3 %collective-permute-start.59 = (bf16[512,1536]{1,0:T(8,128)(2,1)}, bf16[512,1536]{1,0:T(8,128)(2,1)}, u32[]{:S(2)}, u32[]{:S(2)}) collective-permute-start(bf16[512,1536]{1,0:T(8,128)(2,1)} %convolution_convert_fusion.1), channel_id=1, source_target_pairs={{0,4},{4,0},{8,12},{12,8},{16,20},{20,16},{24,28},{28,24},{1,5},{5... | collective-permute-start | bytes 4718600 | tf_op jit(solution)/shard_map/ppermute | solution.py:123
  874.5 46.2 %collective-permute-start.67 = (bf16[512,512]{1,0:T(8,128)(2,1)}, bf16[512,512]{1,0:T(8,128)(2,1)}, u32[]{:S(2)}, u32[]{:S(2)}) collective-permute-start(bf16[512,512]{1,0:T(8,128)(2,1)} %convolution_convert_fusion.3), channel_id=1, source_target_pairs={{0,4},{4,0},{8,12},{12,8},{16,20},{20,16},{24,28},{28,24},{1,5},{5... | collective-permute-start | bytes 1572872 | tf_op jit(solution)/shard_map/ppermute | solution.py:123
  885.3 93.2 %collective-permute-start.74 = (bf16[128,1408]{1,0:T(8,128)(2,1)}, bf16[128,1408]{1,0:T(8,128)(2,1)}, u32[]{:S(2)}, u32[]{:S(2)}) collective-permute-start(bf16[128,1408]{1,0:T(8,128)(2,1)} %get-tuple-element.2144), channel_id=1, source_target_pairs={{0,24},{4,28},{8,16},{12,20},{16,8},{20,12},{24,0},{28,4},{1,25},{... | collective-permute-start | bytes 1081352 | tf_op jit(solution)/shard_map/ppermute | solution.py:123
  923.5 42.9 %collective-permute-start.70 = (bf16[512,128]{1,0:T(8,128)(2,1)S(1)}, bf16[512,128]{1,0:T(8,128)(2,1)S(1)}, u32[]{:S(2)}, u32[]{:S(2)}) collective-permute-start(bf16[512,128]{1,0:T(8,128)(2,1)S(1)} %get-tuple-element.2154), channel_id=1, source_target_pairs={{0,24},{4,28},{8,16},{12,20},{16,8},{20,12},{24,0},{28,4},{1,25},{... | collective-permute-start | bytes 393224 | tf_op jit(solution)/shard_map/ppermute | solution.py:123
  925.5 43.5 %collective-permute-start.69 = (bf16[512,128]{1,0:T(8,128)(2,1)S(1)}, bf16[512,128]{1,0:T(8,128)(2,1)S(1)}, u32[]{:S(2)}, u32[]{:S(2)}) collective-permute-start(bf16[512,128]{1,0:T(8,128)(2,1)S(1)} %get-tuple-element.2155), channel_id=1, source_target_pairs={{0,16},{4,20},{8,24},{12,28},{16,0},{20,4},{24,8},{28,12},{1,17},{... | collective-permute-start | bytes 393224 | tf_op jit(solution)/shard_map/ppermute | solution.py:123
  925.5 43.5 %collective-permute-start.68 = (bf16[512,128]{1,0:T(8,128)(2,1)S(1)}, bf16[512,128]{1,0:T(8,128)(2,1)S(1)}, u32[]{:S(2)}, u32[]{:S(2)}) collective-permute-start(bf16[512,128]{1,0:T(8,128)(2,1)S(1)} %get-tuple-element.2153), channel_id=1, source_target_pairs={{0,8},{4,12},{8,0},{12,4},{16,24},{20,28},{24,16},{28,20},{1,9},{5... | collective-permute-start | bytes 393224 | tf_op jit(solution)/shard_map/ppermute | solution.py:123
  966.4 35.6 %collective-permute-start.73 = (bf16[128,1408]{1,0:T(8,128)(2,1)}, bf16[128,1408]{1,0:T(8,128)(2,1)S(1)}, u32[]{:S(2)}, u32[]{:S(2)}) collective-permute-start(bf16[128,1408]{1,0:T(8,128)(2,1)} %get-tuple-element.2145), channel_id=1, source_target_pairs={{0,16},{4,20},{8,24},{12,28},{16,0},{20,4},{24,8},{28,12},{1,17},{... | collective-permute-start | bytes 1081352 | tf_op jit(solution)/shard_map/ppermute | solution.py:123
  969.0 33.0 %collective-permute-start.72 = (bf16[128,1408]{1,0:T(8,128)(2,1)}, bf16[128,1408]{1,0:T(8,128)(2,1)S(1)}, u32[]{:S(2)}, u32[]{:S(2)}) collective-permute-start(bf16[128,1408]{1,0:T(8,128)(2,1)} %get-tuple-element.2143), channel_id=1, source_target_pairs={{0,8},{4,12},{8,0},{12,4},{16,24},{20,28},{24,16},{28,20},{1,9},{5... | collective-permute-start | bytes 1081352 | tf_op jit(solution)/shard_map/ppermute | solution.py:123
  975.0 29.5 %collective-permute-start.62 = (bf16[128,1536]{1,0:T(8,128)(2,1)S(1)}, bf16[128,1536]{1,0:T(8,128)(2,1)S(1)}, u32[]{:S(2)}, u32[]{:S(2)}) collective-permute-start(bf16[128,1536]{1,0:T(8,128)(2,1)S(1)} %get-tuple-element.2141), channel_id=1, source_target_pairs={{0,24},{4,28},{8,16},{12,20},{16,8},{20,12},{24,0},{28,4},{1,25},{... | collective-permute-start | bytes 1179656 | tf_op jit(solution)/shard_map/ppermute | solution.py:123
  976.8 41.9 %collective-permute-start.61 = (bf16[128,1536]{1,0:T(8,128)(2,1)S(1)}, bf16[128,1536]{1,0:T(8,128)(2,1)S(1)}, u32[]{:S(2)}, u32[]{:S(2)}) collective-permute-start(bf16[128,1536]{1,0:T(8,128)(2,1)S(1)} %get-tuple-element.2142), channel_id=1, source_target_pairs={{0,16},{4,20},{8,24},{12,28},{16,0},{20,4},{24,8},{28,12},{1,17},{... | collective-permute-start | bytes 1179656 | tf_op jit(solution)/shard_map/ppermute | solution.py:123
  978.6 40.2 %collective-permute-start.60 = (bf16[128,1536]{1,0:T(8,128)(2,1)S(1)}, bf16[128,1536]{1,0:T(8,128)(2,1)S(1)}, u32[]{:S(2)}, u32[]{:S(2)}) collective-permute-start(bf16[128,1536]{1,0:T(8,128)(2,1)S(1)} %get-tuple-element.2140), channel_id=1, source_target_pairs={{0,8},{4,12},{8,0},{12,4},{16,24},{20,28},{24,16},{28,20},{1,9},{5... | collective-permute-start | bytes 1179656 | tf_op jit(solution)/shard_map/ppermute | solution.py:123
  (112 other events, 3003.4 us)

commit v2 on v1

--- a/solution.py
+++ b/solution.py
@@ -1,10 +1,11 @@
 import jax
 import jax.numpy as jnp
 from jax import lax
+from jax.experimental import pallas as pl
+from jax.experimental.pallas import tpu as pltpu
 from jax.sharding import PartitionSpec as P
 
 CONV = 4
-GROUP = 64
 
 
 highest = lax.Precision.HIGHEST
@@ -22,85 +23,6 @@
     )
 
 
-def unit_rows(matrix):
-    return matrix * lax.rsqrt(jnp.sum(matrix * matrix, axis=-1, keepdims=True) + UNIT_EPS)
-
-
-def group_step(state_now, block):
-    queries, key_rows, val_rows, log_decay, strength = block
-    width = log_decay.shape[1]
-    cumulative = jnp.cumsum(log_decay, axis=1)
-    row_ids = lax.broadcasted_iota(jnp.int32, (width, width), 0)
-    col_ids = lax.broadcasted_iota(jnp.int32, (width, width), 1)
-    lower_mask = row_ids >= col_ids
-    strict_mask = row_ids > col_ids
-    spread = cumulative[:, :, None] - cumulative[:, None, :]
-    decay_map = jnp.where(lower_mask, jnp.exp(jnp.where(lower_mask, spread, 0.0)), 0.0)
-    key_dots = jnp.einsum("hid,hjd->hij", key_rows, key_rows, precision=highest)
-    system = jnp.where(strict_mask, strength[:, :, None] * key_dots * decay_map, 0.0) + jnp.eye(
-        width, dtype=jnp.float32
-    )
-    start_decay = jnp.exp(cumulative)
-    right_side = jnp.concatenate(
-        [(strength * start_decay)[:, :, None] * key_rows, strength[:, :, None] * val_rows], axis=2
-    )
-    solved = jax.scipy.linalg.solve_triangular(system, right_side, lower=True)
-    key_width = key_rows.shape[2]
-    carried = solved[:, :, key_width:] - jnp.einsum(
-        "hcd,hde->hce", solved[:, :, :key_width], state_now, precision=highest
-    )
-    scores = jnp.einsum("hid,hjd->hij", queries, key_rows, precision=highest) * decay_map
-    output = start_decay[:, :, None] * jnp.einsum(
-        "hcd,hde->hce", queries, state_now, precision=highest
-    )
-    output = output + jnp.einsum("hij,hje->hie", scores, carried, precision=highest)
-    final_decay = cumulative[:, -1:]
-    remaining = jnp.exp(final_decay - cumulative)
-    state_next = jnp.exp(final_decay)[:, :, None] * state_now
-    state_next = state_next + jnp.einsum(
-        "hjd,hje->hde", key_rows * remaining[:, :, None], carried, precision=highest
-    )
-    return (state_next, output)
-
-
-def to_blocks(matrix):
-    length = matrix.shape[0]
-    shaped = matrix.reshape((length // GROUP, GROUP) + matrix.shape[1:])
-    return jnp.moveaxis(shaped, 2, 1)
-
-
-def mixer_core(project, rates, taps, a_log, dt_bias, head_gain, first_head):
-    heads_here = project.shape[1]
-    channels = taps.shape[2]
-    value_width = head_gain.shape[0]
-    key_width = (channels - value_width) // 2
-    length = project.shape[0]
-    padded = jnp.pad(project[:, :, :channels], ((CONV - 1, 0), (0, 0), (0, 0)))
-    mixed = taps[0] * padded[0:length]
-    for offset in range(1, CONV):
-        mixed = mixed + taps[offset] * padded[offset : offset + length]
-    mixed = jax.nn.silu(mixed)
-    queries = unit_rows(mixed[:, :, :key_width]) * key_width ** (-0.5)
-    key_rows = unit_rows(mixed[:, :, key_width : 2 * key_width])
-    val_rows = mixed[:, :, 2 * key_width :]
-    log_rate = lax.dynamic_slice_in_dim(a_log, first_head, heads_here)
-    bias_here = lax.dynamic_slice_in_dim(dt_bias, first_head, heads_here)
-    log_decay = -jnp.exp(log_rate) * jax.nn.softplus(rates[:, :, 0] + bias_here)
-    strength = jax.nn.sigmoid(rates[:, :, 1])
-    initial = jnp.zeros((heads_here, key_width, value_width), jnp.float32)
-    blocks = (
-        to_blocks(queries),
-        to_blocks(key_rows),
-        to_blocks(val_rows),
-        to_blocks(log_decay),
-        to_blocks(strength),
-    )
-    final_state, outputs = lax.scan(group_step, initial, blocks)
-    outputs = jnp.moveaxis(outputs, 1, 2).reshape(length, heads_here, value_width)
-    gated = scale_norm(outputs, head_gain) * jax.nn.silu(project[:, :, channels:])
-    return gated.reshape(length, heads_here * value_width)
-
-
 def gate_product(gate_up):
     return jax.nn.silu(gate_up[:, 0]) * gate_up[:, 1]
 
@@ -117,6 +39,490 @@
 
 def dot(left, right):
     return jnp.dot(left, right, preferred_element_type=f32)
+
+
+CHUNK = 128
+LANES = 128
+
+
+def mul(left, right, over=(1, 0), exact=False):
+    dims = (((over[0],), (over[1],)), ((), ()))
+    if exact:
+        return lax.dot_general(left, right, dims, precision=highest, preferred_element_type=f32)
+    return lax.dot_general(left.astype(bf16), right.astype(bf16), dims, preferred_element_type=f32)
+
+
+def square_ids():
+    shape = (CHUNK, CHUNK)
+    return lax.broadcasted_iota(jnp.int32, shape, 0), lax.broadcasted_iota(jnp.int32, shape, 1)
+
+
+def sigmoid(v):
+    return 1.0 / (1.0 + jnp.exp(-v))
+
+
+def softplus(v):
+    return jnp.maximum(v, 0.0) + jnp.log1p(jnp.exp(-jnp.abs(v)))
+
+
+def row_sum(v):
+    return jnp.sum(v, axis=1, keepdims=True)
+
+
+def unit_inverse(lower):
+    rows, cols = square_ids()
+    inverse = jnp.where(rows == cols, 1.0, 0.0)
+    block = 1
+    while block < CHUNK:
+        corner = (
+            (rows // (2 * block) == cols // (2 * block))
+            & ((rows // block) % 2 == 1)
+            & ((cols // block) % 2 == 0)
+        )
+        part = jnp.where(corner, lower, 0.0)
+        if block == 1:
+            inverse = inverse - part
+        else:
+            inverse = inverse - mul(mul(inverse, part), inverse)
+        block *= 2
+    return inverse
+
+
+def shifted(ref, start, back, columns):
+    if start == 0 and back:
+        rows = lax.broadcasted_iota(jnp.int32, (CHUNK, columns.stop - columns.start), 0)
+        return jnp.where(rows >= back, pltpu.roll(ref[0:CHUNK, columns], back, 0), 0.0)
+    return ref[start - back : start - back + CHUNK, columns]
+
+
+def short_conv(project_ref, taps_ref, start, columns, tap_columns):
+    total = None
+    for tap in range(CONV):
+        term = taps_ref[tap : tap + 1, tap_columns] * shifted(
+            project_ref, start, CONV - 1 - tap, columns
+        )
+        total = term if total is None else total + term
+    return total
+
+
+def decays(rates, log_rates, bias):
+    log_decay = -jnp.exp(log_rates) * softplus(rates + bias)
+    place = lax.broadcasted_iota(jnp.int32, rates.shape, 0)
+    total = log_decay
+    step = 1
+    while step < CHUNK:
+        total = total + jnp.where(place >= step, pltpu.roll(total, step, 0), 0.0)
+        step *= 2
+    return log_decay, total
+
+
+def chunk_terms(head, project_ref, taps_ref, start, total, total_rows, strength, key_width, value_width):
+    width = 2 * key_width + 2 * value_width
+    base, tap_base = head * width, head * (2 * key_width + value_width)
+    terms = {}
+    parts = (("q", 0, key_width), ("k", key_width, key_width), ("v", 2 * key_width, value_width))
+    for name, at, size in parts:
+        pre = short_conv(
+            project_ref,
+            taps_ref,
+            start,
+            slice(base + at, base + at + size),
+            slice(tap_base + at, tap_base + at + size),
+        )
+        gate = sigmoid(pre)
+        mixed = pre * gate
+        if name != "v":
+            scale = lax.rsqrt(row_sum(mixed * mixed) + UNIT_EPS)
+            mixed = mixed * scale
+            terms[name + "_scale"] = scale
+        terms[name + "_slope"] = (pre, gate)
+        terms[name] = mixed
+    terms["unit_q"] = terms["q"]
+    terms["q"] = terms["q"] * key_width ** (-0.5)
+    lane = 2 * head
+    sums = total[:, lane : lane + 1]
+    across = total_rows[lane : lane + 1, :]
+    rows, cols = square_ids()
+    decay = jnp.where(rows >= cols, jnp.exp(jnp.minimum(sums - across, 0.0)), 0.0)
+    final = total[CHUNK - 1 : CHUNK, lane : lane + 1]
+    terms["b"] = strength[:, lane + 1 : lane + 2]
+    terms["since"] = jnp.exp(sums)
+    terms["remaining"] = jnp.exp(final - sums)
+    terms["through"] = jnp.exp(final)
+    terms["decay"] = decay
+    terms["dots"] = mul(terms["k"], terms["k"], (1, 1)) * jnp.where(rows > cols, decay, 0.0)
+    terms["scores"] = mul(terms["q"], terms["k"], (1, 1)) * decay
+    return terms
+
+
+def mixer_forward(
+    normed_ref,
+    mix_ref,
+    rates_w_ref,
+    taps_ref,
+    log_rates_ref,
+    bias_ref,
+    gain_ref,
+    gated_ref,
+    project_ref,
+    rates_ref,
+    out_ref,
+    states_ref,
+    carried_ref,
+    inverse_ref,
+    q_scr,
+    kr_scr,
+    p_scr,
+    w_scr,
+    u_scr,
+):
+    length = normed_ref.shape[0]
+    value_width = gain_ref.shape[1]
+    heads = out_ref.shape[1] // value_width
+    width = project_ref.shape[1] // heads
+    key_width = (width - 2 * value_width) // 2
+    chunks = length // CHUNK
+    for head in range(heads):
+        columns = slice(head * width, (head + 1) * width)
+        project_ref[:, columns] = dot(normed_ref[...], mix_ref[:, columns])
+    rates_ref[...] = dot(normed_ref[...], rates_w_ref[...])
+    through = {}
+    for chunk in range(chunks):
+        start = chunk * CHUNK
+        rows = slice(start, start + CHUNK)
+        rates = rates_ref[rows, :]
+        _, total = decays(rates, log_rates_ref[...], bias_ref[...])
+        strength = sigmoid(rates)
+        total_rows = jnp.transpose(total)
+        for head in range(heads):
+            t = chunk_terms(
+                head, project_ref, taps_ref, start, total, total_rows, strength, key_width, value_width
+            )
+            inverse = unit_inverse(t["b"] * t["dots"])
+            inverse_ref[chunk, head] = inverse
+            side = jnp.concatenate([(t["b"] * t["since"]) * t["k"], t["b"] * t["v"]], 1)
+            solved = mul(inverse, side)
+            w_scr[chunk, head] = solved[:, :key_width].astype(bf16)
+            u_scr[chunk, head] = solved[:, key_width:]
+            q_scr[chunk, head] = (t["q"] * t["since"]).astype(bf16)
+            kr_scr[chunk, head] = (t["k"] * t["remaining"]).astype(bf16)
+            p_scr[chunk, head] = t["scores"].astype(bf16)
+            through[chunk, head] = t["through"]
+    state = [jnp.zeros((key_width, value_width), f32) for _ in range(heads)]
+    for chunk in range(chunks):
+        rows = slice(chunk * CHUNK, (chunk + 1) * CHUNK)
+        for head in range(heads):
+            columns = slice(head * value_width, (head + 1) * value_width)
+            states_ref[chunk, head] = state[head]
+            low = state[head].astype(bf16)
+            carried = u_scr[chunk, head] - mul(w_scr[chunk, head], low)
+            carried_ref[rows, columns] = carried
+            carried = carried.astype(bf16)
+            out_ref[rows, columns] = mul(q_scr[chunk, head], low) + mul(p_scr[chunk, head], carried)
+            state[head] = through[chunk, head] * state[head] + mul(
+                kr_scr[chunk, head], carried, (0, 0)
+            )
+    for chunk in range(chunks):
+        rows = slice(chunk * CHUNK, (chunk + 1) * CHUNK)
+        for head in range(heads):
+            columns = slice(head * value_width, (head + 1) * value_width)
+            out = out_ref[rows, columns]
+            gate = project_ref[rows, (head + 1) * width - value_width : (head + 1) * width]
+            scale = lax.rsqrt(row_sum(out * out) / value_width + NORM_EPS)
+            gated_ref[rows, columns] = (
+                out * scale * gain_ref[...] * (gate * sigmoid(gate))
+            ).astype(bf16)
+
+
+def mixer_backward(
+    grad_ref,
+    w_out_ref,
+    taps_ref,
+    log_rates_ref,
+    bias_ref,
+    gain_ref,
+    project_ref,
+    rates_ref,
+    out_ref,
+    states_ref,
+    carried_ref,
+    inverse_ref,
+    grad_project_ref,
+    grad_rates_ref,
+    grad_taps_ref,
+    grad_gain_ref,
+    grad_lanes_ref,
+    grad_out_scr,
+    back_scr,
+    grad_carried_scr,
+    q_scr,
+    kr_scr,
+    p_scr,
+    w_scr,
+    conv_scr,
+    mixed_scr,
+):
+    length = grad_ref.shape[0]
+    value_width = gain_ref.shape[1]
+    heads = out_ref.shape[1] // value_width
+    width = project_ref.shape[1] // heads
+    key_width = (width - 2 * value_width) // 2
+    channels = 2 * key_width + value_width
+    chunks = length // CHUNK
+    grad_out_scr[...] = lax.dot_general(
+        grad_ref[...], w_out_ref[...], (((1,), (1,)), ((), ())), preferred_element_type=f32
+    )
+    gain = gain_ref[...]
+    gain_total = jnp.zeros((1, value_width), f32)
+    terms = {}
+
+    def gather_terms(chunk):
+        start = chunk * CHUNK
+        rates = rates_ref[start : start + CHUNK, :]
+        _, total = decays(rates, log_rates_ref[...], bias_ref[...])
+        strength = sigmoid(rates)
+        total_rows = jnp.transpose(total)
+        return [
+            chunk_terms(
+                head, project_ref, taps_ref, start, total, total_rows, strength, key_width, value_width
+            )
+            for head in range(heads)
+        ]
+
+    through = {}
+    for chunk in range(chunks):
+        rows = slice(chunk * CHUNK, (chunk + 1) * CHUNK)
+        terms = gather_terms(chunk)
+        for head in range(heads):
+            columns = slice(head * value_width, (head + 1) * value_width)
+            gate_columns = slice((head + 1) * width - value_width, (head + 1) * width)
+            t = terms[head]
+            out = out_ref[rows, columns]
+            gate = project_ref[rows, gate_columns]
+            grad = grad_out_scr[rows, columns]
+            scale = lax.rsqrt(row_sum(out * out) / value_width + NORM_EPS)
+            unit = out * scale
+            sig = sigmoid(gate)
+            act = gate * sig
+            gain_total = gain_total + jnp.sum(grad * unit * act, axis=0, keepdims=True)
+            grad_project_ref[rows, gate_columns] = (
+                grad * gain * unit * (sig * (1.0 + gate * (1.0 - sig)))
+            ).astype(bf16)
+            inner = grad * act * gain
+            grad_out_scr[rows, columns] = scale * (
+                inner - unit * (row_sum(inner * unit) / value_width)
+            )
+            w_scr[chunk, head] = mul(
+                inverse_ref[chunk, head], (t["b"] * t["since"]) * t["k"]
+            ).astype(bf16)
+            q_scr[chunk, head] = (t["q"] * t["since"]).astype(bf16)
+            kr_scr[chunk, head] = (t["k"] * t["remaining"]).astype(bf16)
+            p_scr[chunk, head] = t["scores"].astype(bf16)
+            through[chunk, head] = t["through"]
+    grad_gain_ref[...] = gain_total
+
+    back = [jnp.zeros((key_width, value_width), f32) for _ in range(heads)]
+    for chunk in reversed(range(chunks)):
+        rows = slice(chunk * CHUNK, (chunk + 1) * CHUNK)
+        for head in range(heads):
+            columns = slice(head * value_width, (head + 1) * value_width)
+            back_scr[chunk, head] = back[head]
+            grad_out = grad_out_scr[rows, columns].astype(bf16)
+            grad_carried = mul(p_scr[chunk, head], grad_out, (0, 0)) + mul(
+                kr_scr[chunk, head], back[head]
+            )
+            grad_carried_scr[rows, columns] = grad_carried
+            back[head] = (
+                through[chunk, head] * back[head]
+                + mul(q_scr[chunk, head], grad_out, (0, 0))
+                - mul(w_scr[chunk, head], grad_carried, (0, 0))
+            )
+
+    rows_at, cols_at = square_ids()
+    lane = lax.broadcasted_iota(jnp.int32, (CHUNK, LANES), 1)
+    place = lax.broadcasted_iota(jnp.int32, (CHUNK, LANES), 0)
+    log_total = jnp.zeros((1, LANES), f32)
+    bias_total = jnp.zeros((1, LANES), f32)
+    for chunk in range(chunks):
+        rows = slice(chunk * CHUNK, (chunk + 1) * CHUNK)
+        terms = gather_terms(chunk)
+        sums_grad = jnp.zeros((CHUNK, LANES), f32)
+        strength_grad = jnp.zeros((CHUNK, LANES), f32)
+        for head in range(heads):
+            columns = slice(head * value_width, (head + 1) * value_width)
+            t = terms[head]
+            b, since, remaining, decay = t["b"], t["since"], t["remaining"], t["decay"]
+            q, k, v = t["q"], t["k"], t["v"]
+            state = states_ref[chunk, head]
+            back_now = back_scr[chunk, head]
+            carried = carried_ref[rows, columns]
+            grad_out = grad_out_scr[rows, columns]
+            grad_side = mul(inverse_ref[chunk, head], grad_carried_scr[rows, columns], (0, 0))
+            strict = jnp.where(rows_at > cols_at, -mul(grad_side, carried, (1, 1)), 0.0)
+            grad_scores = mul(grad_out, carried, (1, 1))
+            side_state = mul(grad_side, state, (1, 1))
+            out_state = since * mul(grad_out, state, (1, 1))
+            carried_back = remaining * mul(carried, back_now, (1, 1))
+            key_side = since * row_sum(k * side_state)
+            strict_dots = strict * t["dots"]
+            grad_strength = row_sum(grad_side * v) - key_side + row_sum(strict_dots)
+            pulls = grad_scores * t["scores"] + b * strict_dots
+            key_back = row_sum(k * carried_back)
+            grad_sums = (
+                row_sum(pulls - jnp.transpose(pulls))
+                - b * key_side
+                + row_sum(q * out_state)
+                - key_back
+            )
+            final = jnp.sum(key_back, axis=0, keepdims=True) + t["through"] * jnp.sum(
+                row_sum(back_now * state), axis=0, keepdims=True
+            )
+            scores_low = (grad_scores * decay).astype(bf16)
+            strict_low = (strict * (b * decay)).astype(bf16)
+            k_low, q_low = k.astype(bf16), q.astype(bf16)
+            grad_q = out_state + mul(scores_low, k_low)
+            grad_k = (
+                carried_back
+                - (b * since) * side_state
+                + mul(scores_low, q_low, (0, 0))
+                + mul(strict_low, k_low)
+                + mul(strict_low, k_low, (0, 0))
+            )
+            grad_v = b * grad_side
+            sums_grad = sums_grad + jnp.where(
+                lane == 2 * head, grad_sums + jnp.where(place == CHUNK - 1, final, 0.0), 0.0
+            )
+            strength_grad = strength_grad + jnp.where(lane == 2 * head + 1, grad_strength, 0.0)
+            grad_q = grad_q * key_width ** (-0.5)
+            unit = t["unit_q"]
+            grad_q = t["q_scale"] * (grad_q - unit * row_sum(grad_q * unit))
+            grad_k = t["k_scale"] * (grad_k - k * row_sum(grad_k * k))
+            at = head * channels
+            for name, grad, size in (
+                ("q", grad_q, key_width),
+                ("k", grad_k, key_width),
+                ("v", grad_v, value_width),
+            ):
+                pre, sig = t[name + "_slope"]
+                mixed_scr[rows, at : at + size] = grad * (sig * (1.0 + pre * (1.0 - sig)))
+                at += size
+        step = 1
+        while step < CHUNK:
+            sums_grad = sums_grad + jnp.where(
+                place < CHUNK - step, pltpu.roll(sums_grad, CHUNK - step, 0), 0.0
+            )
+            step *= 2
+        rates = rates_ref[rows, :]
+        log_decay, _ = decays(rates, log_rates_ref[...], bias_ref[...])
+        strength = sigmoid(rates)
+        inputs_grad = sums_grad * (-jnp.exp(log_rates_ref[...])) * sigmoid(rates + bias_ref[...])
+        log_total = log_total + jnp.sum(sums_grad * log_decay, axis=0, keepdims=True)
+        bias_total = bias_total + jnp.sum(inputs_grad, axis=0, keepdims=True)
+        grad_rates_ref[rows, :] = (
+            inputs_grad + strength_grad * strength * (1.0 - strength)
+        ).astype(bf16)
+    grad_lanes_ref[0:1, :] = log_total
+    grad_lanes_ref[1:2, :] = bias_total
+
+    mixed_scr[length : length + 8, :] = jnp.zeros((8, mixed_scr.shape[1]), f32)
+    tap_totals = [jnp.zeros((1, heads * channels), f32) for _ in range(CONV)]
+    for head in range(heads):
+        columns = slice(head * channels, (head + 1) * channels)
+        source = slice(head * width, head * width + channels)
+        taps_here = [jnp.zeros((1, channels), f32) for _ in range(CONV)]
+        for chunk in range(chunks):
+            start = chunk * CHUNK
+            total = None
+            now = mixed_scr[start : start + CHUNK, columns]
+            for tap in range(CONV):
+                ahead = CONV - 1 - tap
+                term = taps_ref[tap : tap + 1, columns] * (
+                    mixed_scr[start + ahead : start + ahead + CHUNK, columns]
+                )
+                total = term if total is None else total + term
+                taps_here[tap] = taps_here[tap] + jnp.sum(
+                    now * shifted(project_ref, start, ahead, source), axis=0, keepdims=True
+                )
+            grad_project_ref[start : start + CHUNK, source] = total.astype(bf16)
+        for tap in range(CONV):
+            grad_taps_ref[tap : tap + 1, columns] = taps_here[tap]
+
+
+def whole(count):
+    return [pl.BlockSpec(memory_space=pltpu.VMEM)] * count
+
+
+def run_forward(normed, mix, rates_w, taps, log_rates, bias, gain):
+    length, value_width = normed.shape[0], gain.shape[1]
+    columns = mix.shape[1]
+    channels = taps.shape[1]
+    heads = (columns - channels) // value_width
+    key_width = (channels // heads - value_width) // 2
+    chunks = length // CHUNK
+    shape = jax.ShapeDtypeStruct
+    values = heads * value_width
+    pair = (chunks, heads)
+    return pl.pallas_call(
+        mixer_forward,
+        out_shape=(
+            shape((length, values), bf16),
+            shape((length, columns), f32),
+            shape((length, LANES), f32),
+            shape((length, values), f32),
+            shape(pair + (key_width, value_width), f32),
+            shape((length, values), f32),
+            shape(pair + (CHUNK, CHUNK), f32),
+        ),
+        in_specs=whole(7),
+        out_specs=tuple(whole(7)),
+        scratch_shapes=[
+            pltpu.VMEM(pair + (CHUNK, key_width), bf16),
+            pltpu.VMEM(pair + (CHUNK, key_width), bf16),
+            pltpu.VMEM(pair + (CHUNK, CHUNK), bf16),
+            pltpu.VMEM(pair + (CHUNK, key_width), bf16),
+            pltpu.VMEM(pair + (CHUNK, value_width), f32),
+        ],
+        compiler_params=pltpu.CompilerParams(vmem_limit_bytes=52 * 2**20),
+        name="mixer_forward",
+    )(normed, mix, rates_w, taps, log_rates, bias, gain)
+
+
+def run_backward(grad, w_out, taps, log_rates, bias, gain, kept):
+    length, value_width = grad.shape[0], gain.shape[1]
+    project = kept[0]
+    columns = project.shape[1]
+    channels = taps.shape[1]
+    heads = (columns - channels) // value_width
+    key_width = (channels // heads - value_width) // 2
+    chunks = length // CHUNK
+    shape = jax.ShapeDtypeStruct
+    values = heads * value_width
+    pair = (chunks, heads)
+    return pl.pallas_call(
+        mixer_backward,
+        out_shape=(
+            shape((length, columns), bf16),
+            shape((length, LANES), bf16),
+            shape((CONV, channels), f32),
+            shape((1, value_width), f32),
+            shape((2, LANES), f32),
+        ),
+        in_specs=whole(6 + len(kept)),
+        out_specs=tuple(whole(5)),
+        scratch_shapes=[
+            pltpu.VMEM((length, values), f32),
+            pltpu.VMEM(pair + (key_width, value_width), f32),
+            pltpu.VMEM((length, values), f32),
+            pltpu.VMEM(pair + (CHUNK, key_width), bf16),
+            pltpu.VMEM(pair + (CHUNK, key_width), bf16),
+            pltpu.VMEM(pair + (CHUNK, CHUNK), bf16),
+            pltpu.VMEM(pair + (CHUNK, key_width), bf16),
+            pltpu.VMEM((8, LANES), f32),
+            pltpu.VMEM((length + 8, channels), f32),
+        ],
+        compiler_params=pltpu.CompilerParams(vmem_limit_bytes=52 * 2**20),
+        name="mixer_backward",
+    )(grad, w_out, taps, log_rates, bias, gain, *kept)
 
 
 def swap(array, axis, size, offset):
@@ -264,15 +670,25 @@
     gate_up_full = jnp.concatenate(dp.gather(gate_up_shard), 0)
     down_full = jnp.concatenate(dp.gather(down_shard), 1)
 
-    project = dot(normed_all, mix_full).reshape(-1, heads_here, head_width)
-    rates = dot(normed_all, rates_full).reshape(-1, heads_here, 2)
     first_head = lax.axis_index("tensor") * heads_here
 
-    def core_local(project_in, rates_in, taps_in, log_rates, decay_bias, gain_in):
-        return mixer_core(project_in, rates_in, taps_in, log_rates, decay_bias, gain_in, first_head)
-
-    gated, core_back = jax.vjp(core_local, project, rates, taps_full, a_log, dt_bias, head_gain)
-    gated_low = gated.astype(bf16)
+    def on_lanes(per_head):
+        here = lax.dynamic_slice_in_dim(per_head, first_head, heads_here)
+        pairs = jnp.stack([here, jnp.zeros_like(here)], 1).reshape(1, -1)
+        return jnp.pad(pairs, ((0, 0), (0, LANES - pairs.shape[1])))
+
+    def off_lanes(row):
+        here = row[: 2 * heads_here : 2]
+        return lax.dynamic_update_slice_in_dim(jnp.zeros_like(a_log), here, first_head, 0)
+
+    rates_wide = jnp.pad(rates_full, ((0, 0), (0, LANES - rates_full.shape[1])))
+    small_args = (
+        taps_full.reshape(CONV, -1),
+        on_lanes(a_log),
+        on_lanes(dt_bias),
+        head_gain.reshape(1, -1),
+    )
+    gated_low, *kept = run_forward(normed_all, mix_full, rates_wide, *small_args)
     mixer_out = sum_rows(from_time(dot(gated_low, out_full), ranks), bf16)
     resid = resid_in + mixer_out
     ffn_in, ffn_back = jax.vjp(scale_norm, resid, ffn_gain)
@@ -297,15 +713,16 @@
     grad_w_down = dp.scatter(
         rows_dot(hidden_low, top_grad[:, :half]), rows_dot(hidden_low, top_grad[:, half:], bf16), 1
     )
-    grad_gated = cols_dot(mix_grad, out_full)
     grad_w_out = dp.scatter(
         rows_dot(gated_low, mix_grad[:, :half]), rows_dot(gated_low, mix_grad[:, half:], bf16), 1
     )
-    grad_project, grad_rates, local_taps, grad_log_rates, grad_decay_bias, grad_gain_here = (
-        core_back(grad_gated)
-    )
-    project_low = grad_project.astype(bf16).reshape(-1, heads_here * head_width)
-    rates_low = grad_rates.astype(bf16).reshape(-1, heads_here * 2)
+    project_low, rates_low, local_taps, grad_gain_here, grad_lanes = run_backward(
+        mix_grad, out_full, *small_args, kept
+    )
+    rates_low = rates_low[:, : rates_full.shape[1]]
+    local_taps = local_taps.reshape(CONV, heads_here, -1)
+    grad_gain_here = grad_gain_here.reshape(-1)
+    grad_log_rates, grad_decay_bias = off_lanes(grad_lanes[0]), off_lanes(grad_lanes[1])
     back_terms = cols_dot(project_low, mix_full) + cols_dot(rates_low, rates_full)
     grad_w_mix = dp.scatter(
         rows_dot(normed_all[:, :half], project_low), rows_dot(normed_all[:, half:], project_low, bf16), 0

time: 1040 us -> 506 us (0.49)
  other arithmetic: 314 us -> 14.1 us
  matrix products: 239 us -> 31.7 us
  local copies, waits for them, and re-layouts: 145 us -> 44.3 us
  Pallas kernels: 0 us -> 41.8 us
  waiting for transfers between devices: 200 us -> 234 us
    another operation x89 -> x0, other arithmetic: 193 us -> none  [the longest x48 181 us: group_step(): solved = jax.scipy.linalg.solve_triangular(system, right_side, lower=True)]
    dot_general x152 -> x0, matrix products: 166 us -> none  [the longest x24 35.6 us: group_step(): jnp.einsum('hcd,hde->hce', queries, state_now, precision=highest)]
    pallas_call x0 -> x2, Pallas kernels: none -> 41.8 us  [the longest x1 21 us: run_forward(): pl.pallas_call(mixer_forward, out_shape=(shape((length, values), bf16), s...]
    dynamic_update_slice x49 -> x0, other arithmetic: 38.5 us -> none  [the longest x48 38.3 us: mixer_core(): final_state, outputs = lax.scan(group_step, initial, blocks)]
    ppermute x79, waiting for transfers between devices: 200 us -> 234 us  [swap(): return lax.ppermute(array, axis, [(i, i ^ offset) for i in range(size)])]
    reduce_sum x36 -> x0, other arithmetic: 29.9 us -> none  [the longest x8 8.75 us: group_step(): start_decay[:, :, None]]
    another operation x24 -> x0, matrix products: 28 us -> none  [group_step(): solved = jax.scipy.linalg.solve_triangular(system, right_side, lower=True)]
    unnamed x221 -> x111, local copies, waits for them, and re-layouts: 38.7 us -> 17.1 us
  transfers between devices with their start and end apart: 79 -> 79, of which waited for: 33 -> 38; matrix products, arithmetic and copies ran while one was open for 64% -> 15% of each run, Pallas kernels for 0% -> 8%
where the time goes in v2:
time: 506 us; the launch traced here: 496 us
  waiting for transfers between devices  234 us (46%)
  starting transfers between devices  90 us (18%)
  local copies, waits for them, and re-layouts  44.3 us (9%)
  Pallas kernels  41.8 us (8%)
  blocking collectives  37.9 us (7%)
  matrix products  31.7 us (6%)
  other arithmetic  14.1 us (3%)
    ppermute x79, waiting for transfers between devices, swap(): return lax.ppermute(array, axis, [(i, i ^ offset) for i in range(size)])  234 us
    ppermute x79, starting transfers between devices, swap(): return lax.ppermute(array, axis, [(i, i ^ offset) for i in range(size)])  90 us
    psum x1, blocking collectives, per_device(): lax.psum((dp.blocks_from_order(grad_gain_first), dp.blocks_from_order(gra...  37.9 us
    dot_general x9, matrix products, rows_dot(): lax.dot_general(left, right, (((0,), (0,)), ((), ())), preferred_element_...  21.4 us
    pallas_call x1, Pallas kernels, run_forward(): pl.pallas_call(mixer_forward, out_shape=(shape((length, values), bf16), s...  21 us
    pallas_call x1, Pallas kernels, run_backward(): pl.pallas_call(mixer_backward, out_shape=(shape((length, columns), bf16),...  20.8 us
    unnamed x111, local copies, waits for them, and re-layouts  17.1 us
  transfers between devices with their start and end apart: 79, of which 38 were waited for; matrix products, arithmetic and copies ran while one was open for 15% of the time, Pallas kernels for 8%

profile of v2, /device:TPU:0, one launch (start us, length us, event | category | flops | bytes accessed | tf_op | source)
XLA Modules:
  0.0 496.4 jit_solution(15395337652825660672)
XLA Ops:
  9.3 2.5 collective-permute-start.1
  13.5 2.6 collective-permute-start.4
  20.3 11.3 %collective-permute-done.10 = bf16[8,128]{1,0:T(8,128)(2,1)S(1)} collective-permute-done((bf16[8,128]{1,0:T(8,128)(2,1)S(1)}, bf16[8,128]{1,0:T(8,128)(2,1)S(1)}, u32[]{:S(2)}, u32[]{:S(2)}) %collective-permute-start.10) | collective-permute-done | bytes 2080 | tf_op jit(solution)/shard_map/ppermute | solution.py:529
  31.6 2.8 collective-permute-start.11
  36.1 2.5 collective-permute-start.12
  38.5 2.9 collective-permute-done.12
  60.3 2.6 collective-permute-start.5
  78.4 6.1 %collective-permute-done.7 = bf16[128,1536]{1,0:T(8,128)(2,1)S(1)} collective-permute-done((bf16[128,1536]{1,0:T(8,128)(2,1)S(1)}, bf16[128,1536]{1,0:T(8,128)(2,1)S(1)}, u32[]{:S(2)}, u32[]{:S(2)}) %collective-permute-start.7) | collective-permute-done | bytes 393248 | tf_op jit(solution)/shard_map/ppermute | solution.py:529
  85.2 7.6 %collective-permute-done.8 = bf16[128,1536]{1,0:T(8,128)(2,1)S(1)} collective-permute-done((bf16[128,1536]{1,0:T(8,128)(2,1)S(1)}, bf16[128,1536]{1,0:T(8,128)(2,1)S(1)}, u32[]{:S(2)}, u32[]{:S(2)}) %collective-permute-start.8) | collective-permute-done | bytes 393248 | tf_op jit(solution)/shard_map/ppermute | solution.py:529
  93.7 6.2 %collective-permute-done.9 = bf16[128,1536]{1,0:T(8,128)(2,1)S(1)} collective-permute-done((bf16[128,1536]{1,0:T(8,128)(2,1)S(1)}, bf16[128,1536]{1,0:T(8,128)(2,1)S(1)}, u32[]{:S(2)}, u32[]{:S(2)}) %collective-permute-start.9) | collective-permute-done | bytes 393248 | tf_op jit(solution)/shard_map/ppermute | solution.py:529
  102.5 2.6 collective-permute-start.19
  107.5 21.0 %mixer_forward.1 = (bf16[512,512]{1,0:T(8,128)(2,1)S(1)}, f32[512,1536]{1,0:T(8,128)}, f32[512,128]{1,0:T(8,128)S(1)}, f32[512,512]{1,0:T(8,128)}, f32[4,2,128,2...) custom-call(bf16[512,1024]{1,0:T(8,128)(2,1)} %copy-done.3, ...), custom_call_target="tpu_custom_call" | custom-call | tf_op jit(solution)/shard_map/mixer_forward/pallas_call | solution.py:465
  130.4 2.5 collective-permute-start.32
  135.2 15.7 %collective-permute-done.37 = bf16[704,128]{1,0:T(8,128)(2,1)S(1)} collective-permute-done((bf16[704,128]{1,0:T(8,128)(2,1)S(1)}, bf16[704,128]{1,0:T(8,128)(2,1)S(1)}, u32[]{:S(2)}, u32[]{:S(2)}) %collective-permute-start.37) | collective-permute-done | bytes 180256 | tf_op jit(solution)/shard_map/ppermute | solution.py:529
  150.8 2.5 collective-permute-start.39
  153.4 20.0 %collective-permute-done.38 = bf16[704,128]{1,0:T(8,128)(2,1)S(1)} collective-permute-done((bf16[704,128]{1,0:T(8,128)(2,1)S(1)}, bf16[704,128]{1,0:T(8,128)(2,1)S(1)}, u32[]{:S(2)}, u32[]{:S(2)}) %collective-permute-start.38) | collective-permute-done | bytes 180256 | tf_op jit(solution)/shard_map/ppermute | solution.py:529
  175.6 4.4 collective-permute-done.40
  180.6 2.3 collective-permute-done.21
  183.4 2.9 collective-permute-done.22
  186.9 2.3 collective-permute-done.23
  194.1 7.4 %collective-permute-done.41 = bf16[704,128]{1,0:T(8,128)(2,1)S(1)} collective-permute-done((bf16[704,128]{1,0:T(8,128)(2,1)S(1)}, bf16[704,128]{1,0:T(8,128)(2,1)S(1)}, u32[]{:S(2)}, u32[]{:S(2)}) %collective-permute-start.41) | collective-permute-done | bytes 180256 | tf_op jit(solution)/shard_map/ppermute | solution.py:529
  207.3 3.4 collective-permute-done.26
  213.8 3.7 collective-permute-done.28
  217.5 3.8 collective-permute-done.35
  221.4 7.0 %collective-permute-done.36 = bf16[128,1408]{0,1:T(8,128)(2,1)S(1)} collective-permute-done((bf16[128,1408]{0,1:T(8,128)(2,1)S(1)}, bf16[128,1408]{0,1:T(8,128)(2,1)S(1)}, u32[]{:S(2)}, u32[]{:S(2)}) %collective-permute-start.36) | collective-permute-done | bytes 360480 | tf_op jit(solution)/shard_map/ppermute | solution.py:529
  236.2 2.1 convolution_convert_fusion
  244.3 4.0 collective-permute-done.52
  248.2 4.4 collective-permute-done.46
  258.0 29.6 %collective-permute-done.75 = bf16[704,512]{1,0:T(8,128)(2,1)} collective-permute-done((bf16[704,512]{1,0:T(8,128)(2,1)}, bf16[704,512]{1,0:T(8,128)(2,1)}, u32[]{:S(2)}, u32[]{:S(2)}) %collective-permute-start.75) | collective-permute-done | bytes 720928 | tf_op jit(solution)/shard_map/ppermute | solution.py:529
  291.6 2.7 collective-permute-start.76
  295.3 4.0 collective-permute-done.78
  299.3 7.6 %collective-permute-done.77 = bf16[704,128]{1,0:T(8,128)(2,1)S(1)} collective-permute-done((bf16[704,128]{1,0:T(8,128)(2,1)S(1)}, bf16[704,128]{1,0:T(8,128)(2,1)S(1)}, u32[]{:S(2)}, u32[]{:S(2)}) %collective-permute-start.77) | collective-permute-done | bytes 180256 | tf_op jit(solution)/shard_map/ppermute | solution.py:529
  307.7 20.8 %mixer_backward.1 = (bf16[512,1536]{1,0:T(8,128)(2,1)}, bf16[512,128]{1,0:T(8,128)(2,1)S(1)}, f32[4,1024]{1,0:T(4,128)S(1)}, f32[1,256]{1,0:T(1,128)S(1)}, f32[2,128]{1,0:T(2,128)S(1)}) custom-call(bf16[512,1024]{1,0:T(8,128)(2,1)S(1)} %constant_dynamic-update-slice_fusion.54.grad_ref, bf16[512,1024]{1,0:T(8,128)(2,1)} %copy-done.8, ...), custom_call_target="tpu_custom_call" | custom-call | tf_op jit(solution)/shard_map/mixer_backward/pallas_call | solution.py:501
  331.5 2.2 convolution_convert_fusion.1
  333.7 3.2 convolution_add_fusion.2
  341.9 2.1 collective-permute-start.66
  344.0 2.4 collective-permute-start.64
  354.8 4.6 fusion.62
  364.7 2.4 gather_fusion.2
  371.9 23.8 %collective-permute-done.67 = bf16[512,512]{1,0:T(8,128)(2,1)} collective-permute-done((bf16[512,512]{1,0:T(8,128)(2,1)}, bf16[512,512]{1,0:T(8,128)(2,1)}, u32[]{:S(2)}, u32[]{:S(2)}) %collective-permute-start.67) | collective-permute-done | bytes 524320 | tf_op jit(solution)/shard_map/ppermute | solution.py:529
  395.7 2.6 fusion.61
  398.4 2.1 collective-permute-start.70
  400.5 2.4 collective-permute-start.68
  402.9 37.9 %all-reduce.7 = (f32[1024]{0:T(1024)}, f32[8]{0:T(128)}, f32[8]{0:T(128)}, f32[256]{0:T(256)}, f32[1024]{0:T(1024)}) all-reduce(f32[1024]{0:T(1024)S(1)} %get-tuple-element.175, f32[8]{0:T(128)S(1)} %dynamic_update_slice.38, f32[8]{0:T(128)S(1)} %dynamic_update_slice.39, ...), channel_id=1, replica_groups=mesh['dp'=8,'tensor'=4] {'dp','tensor'}, use_global_device_ids=true, to_apply=%region_5.8 | all-reduce | flops 2320 | bytes 18560 | tf_op jit(solution)/shard_map/psum | solution.py:740
  440.9 2.6 collective-permute-start.73
  445.2 4.6 fusion.60
  454.4 22.1 %collective-permute-done.73 = bf16[128,1408]{1,0:T(8,128)(2,1)S(1)} collective-permute-done((bf16[128,1408]{1,0:T(8,128)(2,1)}, bf16[128,1408]{1,0:T(8,128)(2,1)S(1)}, u32[]{:S(2)}, u32[]{:S(2)}) %collective-permute-start.73) | collective-permute-done | bytes 360480 | tf_op jit(solution)/shard_map/ppermute | solution.py:529
  478.9 14.2 %collective-permute-done.61 = bf16[128,1536]{1,0:T(8,128)(2,1)S(1)} collective-permute-done((bf16[128,1536]{1,0:T(8,128)(2,1)S(1)}, bf16[128,1536]{1,0:T(8,128)(2,1)S(1)}, u32[]{:S(2)}, u32[]{:S(2)}) %collective-permute-start.61) | collective-permute-done | bytes 393248 | tf_op jit(solution)/shard_map/ppermute | solution.py:529
  (379 shorter events, 141.1 us)
Async XLA Ops:
  8.9 51.4 %collective-permute-start = (bf16[128,1024]{1,0:T(8,128)(2,1)}, bf16[128,1024]{1,0:T(8,128)(2,1)}, u32[]{:S(2)}, u32[]{:S(2)}) collective-permute-start(bf16[128,1024]{1,0:T(8,128)(2,1)} %get-tuple-element.128), channel_id=1, source_target_pairs={{0,1},{1,0},{2,3},{3,2},{4,5},{5,4},{6,7},{7,6},{8,9},{9,8},{10,11... | collective-permute-start | bytes 786440 | tf_op jit(solution)/shard_map/ppermute | solution.py:529
  9.3 54.6 %collective-permute-start.1 = (bf16[128,1024]{1,0:T(8,128)(2,1)}, bf16[128,1024]{1,0:T(8,128)(2,1)}, u32[]{:S(2)}, u32[]{:S(2)}) collective-permute-start(bf16[128,1024]{1,0:T(8,128)(2,1)} %get-tuple-element.128), channel_id=1, source_target_pairs={{0,2},{1,3},{2,0},{3,1},{4,6},{5,7},{6,4},{7,5},{8,10},{9,11},{10,... | collective-permute-start | bytes 786440 | tf_op jit(solution)/shard_map/ppermute | solution.py:529
  11.9 55.7 %collective-permute-start.3 = (bf16[128,1536]{1,0:T(8,128)(2,1)S(1)}, bf16[128,1536]{1,0:T(8,128)(2,1)S(1)}, u32[]{:S(2)}, u32[]{:S(2)}) collective-permute-start(bf16[128,1536]{1,0:T(8,128)(2,1)S(1)} %bitcast.141), channel_id=1, source_target_pairs={{0,8},{4,12},{8,0},{12,4},{16,24},{20,28},{24,16},{28,20},{1,9},{5... | collective-permute-start | bytes 1179656 | tf_op jit(solution)/shard_map/ppermute | solution.py:529
  13.5 55.3 %collective-permute-start.4 = (bf16[128,1536]{1,0:T(8,128)(2,1)S(1)}, bf16[128,1536]{1,0:T(8,128)(2,1)S(1)}, u32[]{:S(2)}, u32[]{:S(2)}) collective-permute-start(bf16[128,1536]{1,0:T(8,128)(2,1)S(1)} %bitcast.142), channel_id=1, source_target_pairs={{0,16},{4,20},{8,24},{12,28},{16,0},{20,4},{24,8},{28,12},{1,17},{... | collective-permute-start | bytes 1179656 | tf_op jit(solution)/shard_map/ppermute | solution.py:529
  16.5 15.0 %collective-permute-start.10 = (bf16[8,128]{1,0:T(8,128)(2,1)S(1)}, bf16[8,128]{1,0:T(8,128)(2,1)S(1)}, u32[]{:S(2)}, u32[]{:S(2)}) collective-permute-start(bf16[8,128]{1,0:T(8,128)(2,1)S(1)} %pad_maximum_fusion.1), channel_id=1, source_target_pairs={{0,8},{4,12},{8,0},{12,4},{16,24},{20,28},{24,16},{28,20},{1,9},{5... | collective-permute-start | bytes 6152 | tf_op jit(solution)/shard_map/ppermute | solution.py:529
  60.3 12.8 %collective-permute-start.5 = (bf16[128,1536]{1,0:T(8,128)(2,1)S(1)}, bf16[128,1536]{1,0:T(8,128)(2,1)S(1)}, u32[]{:S(2)}, u32[]{:S(2)}) collective-permute-start(bf16[128,1536]{1,0:T(8,128)(2,1)S(1)} %bitcast.144), channel_id=1, source_target_pairs={{0,24},{4,28},{8,16},{12,20},{16,8},{20,12},{24,0},{28,4},{1,25},{... | collective-permute-start | bytes 1179656 | tf_op jit(solution)/shard_map/ppermute | solution.py:529
  63.9 12.1 %collective-permute-start.6 = (bf16[128,1536]{1,0:T(8,128)(2,1)S(1)}, bf16[128,1536]{1,0:T(8,128)(2,1)S(1)}, u32[]{:S(2)}, u32[]{:S(2)}) collective-permute-start(bf16[128,1536]{1,0:T(8,128)(2,1)S(1)} %bitcast.145), channel_id=1, source_target_pairs={{0,4},{4,0},{8,12},{12,8},{16,20},{20,16},{24,28},{28,24},{1,5},{5... | collective-permute-start | bytes 1179656 | tf_op jit(solution)/shard_map/ppermute | solution.py:529
  68.9 15.6 %collective-permute-start.7 = (bf16[128,1536]{1,0:T(8,128)(2,1)S(1)}, bf16[128,1536]{1,0:T(8,128)(2,1)S(1)}, u32[]{:S(2)}, u32[]{:S(2)}) collective-permute-start(bf16[128,1536]{1,0:T(8,128)(2,1)S(1)} %collective-permute-done.3), channel_id=1, source_target_pairs={{0,4},{4,0},{8,12},{12,8},{16,20},{20,16},{24,28},{28,24},{1,5},{5... | collective-permute-start | bytes 1179656 | tf_op jit(solution)/shard_map/ppermute | solution.py:529
  73.1 19.8 %collective-permute-start.8 = (bf16[128,1536]{1,0:T(8,128)(2,1)S(1)}, bf16[128,1536]{1,0:T(8,128)(2,1)S(1)}, u32[]{:S(2)}, u32[]{:S(2)}) collective-permute-start(bf16[128,1536]{1,0:T(8,128)(2,1)S(1)} %collective-permute-done.4), channel_id=1, source_target_pairs={{0,4},{4,0},{8,12},{12,8},{16,20},{20,16},{24,28},{28,24},{1,5},{5... | collective-permute-start | bytes 1179656 | tf_op jit(solution)/shard_map/ppermute | solution.py:529
  76.0 23.8 %collective-permute-start.9 = (bf16[128,1536]{1,0:T(8,128)(2,1)S(1)}, bf16[128,1536]{1,0:T(8,128)(2,1)S(1)}, u32[]{:S(2)}, u32[]{:S(2)}) collective-permute-start(bf16[128,1536]{1,0:T(8,128)(2,1)S(1)} %collective-permute-done.5), channel_id=1, source_target_pairs={{0,4},{4,0},{8,12},{12,8},{16,20},{20,16},{24,28},{28,24},{1,5},{5... | collective-permute-start | bytes 1179656 | tf_op jit(solution)/shard_map/ppermute | solution.py:529
  100.7 27.8 %collective-permute-start.17 = (bf16[512,128]{1,0:T(8,128)(2,1)S(1)}, bf16[512,128]{1,0:T(8,128)(2,1)S(1)}, u32[]{:S(2)}, u32[]{:S(2)}) collective-permute-start(bf16[512,128]{1,0:T(8,128)(2,1)S(1)} %copy-done.22), channel_id=1, source_target_pairs={{0,8},{4,12},{8,0},{12,4},{16,24},{20,28},{24,16},{28,20},{1,9},{5... | collective-permute-start | bytes 393224 | tf_op jit(solution)/shard_map/ppermute | solution.py:529
  100.7 29.7 %collective-permute-start.18 = (bf16[512,128]{1,0:T(8,128)(2,1)S(1)}, bf16[512,128]{1,0:T(8,128)(2,1)S(1)}, u32[]{:S(2)}, u32[]{:S(2)}) collective-permute-start(bf16[512,128]{1,0:T(8,128)(2,1)S(1)} %copy-done.22), channel_id=1, source_target_pairs={{0,16},{4,20},{8,24},{12,28},{16,0},{20,4},{24,8},{28,12},{1,17},{... | collective-permute-start | bytes 393224 | tf_op jit(solution)/shard_map/ppermute | solution.py:529
  102.5 30.5 %collective-permute-start.19 = (bf16[512,128]{1,0:T(8,128)(2,1)S(1)}, bf16[512,128]{1,0:T(8,128)(2,1)S(1)}, u32[]{:S(2)}, u32[]{:S(2)}) collective-permute-start(bf16[512,128]{1,0:T(8,128)(2,1)S(1)} %copy-done.22), channel_id=1, source_target_pairs={{0,24},{4,28},{8,16},{12,20},{16,8},{20,12},{24,0},{28,4},{1,25},{... | collective-permute-start | bytes 393224 | tf_op jit(solution)/shard_map/ppermute | solution.py:529
  105.1 28.0 %collective-permute-start.20 = (bf16[512,128]{1,0:T(8,128)(2,1)S(1)}, bf16[512,128]{1,0:T(8,128)(2,1)S(1)}, u32[]{:S(2)}, u32[]{:S(2)}) collective-permute-start(bf16[512,128]{1,0:T(8,128)(2,1)S(1)} %copy-done.22), channel_id=1, source_target_pairs={{0,4},{4,0},{8,12},{12,8},{16,20},{20,16},{24,28},{28,24},{1,5},{5... | collective-permute-start | bytes 393224 | tf_op jit(solution)/shard_map/ppermute | solution.py:529
  107.4 83.4 %collective-permute-start.30 = (bf16[128,1408]{0,1:T(8,128)(2,1)S(1)}, bf16[128,1408]{0,1:T(8,128)(2,1)S(1)}, u32[]{:S(2)}, u32[]{:S(2)}) collective-permute-start(bf16[128,1408]{0,1:T(8,128)(2,1)S(1)} %bitcast.153), channel_id=1, source_target_pairs={{0,8},{4,12},{8,0},{12,4},{16,24},{20,28},{24,16},{28,20},{1,9},{5... | collective-permute-start | bytes 1081352 | tf_op jit(solution)/shard_map/ppermute | solution.py:529
  128.5 64.0 %collective-permute-start.31 = (bf16[128,1408]{0,1:T(8,128)(2,1)S(1)}, bf16[128,1408]{0,1:T(8,128)(2,1)S(1)}, u32[]{:S(2)}, u32[]{:S(2)}) collective-permute-start(bf16[128,1408]{0,1:T(8,128)(2,1)S(1)} %bitcast.154), channel_id=1, source_target_pairs={{0,16},{4,20},{8,24},{12,28},{16,0},{20,4},{24,8},{28,12},{1,17},{... | collective-permute-start | bytes 1081352 | tf_op jit(solution)/shard_map/ppermute | solution.py:529
  130.4 63.4 %collective-permute-start.32 = (bf16[128,1408]{0,1:T(8,128)(2,1)S(1)}, bf16[128,1408]{0,1:T(8,128)(2,1)S(1)}, u32[]{:S(2)}, u32[]{:S(2)}) collective-permute-start(bf16[128,1408]{0,1:T(8,128)(2,1)S(1)} %bitcast.155), channel_id=1, source_target_pairs={{0,24},{4,28},{8,16},{12,20},{16,8},{20,12},{24,0},{28,4},{1,25},{... | collective-permute-start | bytes 1081352 | tf_op jit(solution)/shard_map/ppermute | solution.py:529
  133.0 17.8 %collective-permute-start.37 = (bf16[704,128]{1,0:T(8,128)(2,1)S(1)}, bf16[704,128]{1,0:T(8,128)(2,1)S(1)}, u32[]{:S(2)}, u32[]{:S(2)}) collective-permute-start(bf16[704,128]{1,0:T(8,128)(2,1)S(1)} %copy-done.21), channel_id=1, source_target_pairs={{0,8},{4,12},{8,0},{12,4},{16,24},{20,28},{24,16},{28,20},{1,9},{5... | collective-permute-start | bytes 540680 | tf_op jit(solution)/shard_map/ppermute | solution.py:529
  133.2 40.2 %collective-permute-start.38 = (bf16[704,128]{1,0:T(8,128)(2,1)S(1)}, bf16[704,128]{1,0:T(8,128)(2,1)S(1)}, u32[]{:S(2)}, u32[]{:S(2)}) collective-permute-start(bf16[704,128]{1,0:T(8,128)(2,1)S(1)} %copy-done.21), channel_id=1, source_target_pairs={{0,16},{4,20},{8,24},{12,28},{16,0},{20,4},{24,8},{28,12},{1,17},{... | collective-permute-start | bytes 540680 | tf_op jit(solution)/shard_map/ppermute | solution.py:529
  150.8 23.1 %collective-permute-start.39 = (bf16[704,128]{1,0:T(8,128)(2,1)S(1)}, bf16[704,128]{1,0:T(8,128)(2,1)S(1)}, u32[]{:S(2)}, u32[]{:S(2)}) collective-permute-start(bf16[704,128]{1,0:T(8,128)(2,1)S(1)} %copy-done.21), channel_id=1, source_target_pairs={{0,24},{4,28},{8,16},{12,20},{16,8},{20,12},{24,0},{28,4},{1,25},{... | collective-permute-start | bytes 540680 | tf_op jit(solution)/shard_map/ppermute | solution.py:529
  186.3 18.7 %collective-permute-start.33 = (bf16[128,1408]{0,1:T(8,128)(2,1)S(1)}, bf16[128,1408]{0,1:T(8,128)(2,1)S(1)}, u32[]{:S(2)}, u32[]{:S(2)}) collective-permute-start(bf16[128,1408]{0,1:T(8,128)(2,1)S(1)} %bitcast.156), channel_id=1, source_target_pairs={{0,4},{4,0},{8,12},{12,8},{16,20},{20,16},{24,28},{28,24},{1,5},{5... | collective-permute-start | bytes 1081352 | tf_op jit(solution)/shard_map/ppermute | solution.py:529
  189.3 12.2 %collective-permute-start.41 = (bf16[704,128]{1,0:T(8,128)(2,1)S(1)}, bf16[704,128]{1,0:T(8,128)(2,1)S(1)}, u32[]{:S(2)}, u32[]{:S(2)}) collective-permute-start(bf16[704,128]{1,0:T(8,128)(2,1)S(1)} %collective-permute-done.37), channel_id=1, source_target_pairs={{0,4},{4,0},{8,12},{12,8},{16,20},{20,16},{24,28},{28,24},{1,5},{5... | collective-permute-start | bytes 540680 | tf_op jit(solution)/shard_map/ppermute | solution.py:529
  190.8 12.6 %collective-permute-start.42 = (bf16[704,128]{1,0:T(8,128)(2,1)S(1)}, bf16[704,128]{1,0:T(8,128)(2,1)S(1)}, u32[]{:S(2)}, u32[]{:S(2)}) collective-permute-start(bf16[704,128]{1,0:T(8,128)(2,1)S(1)} %collective-permute-done.38), channel_id=1, source_target_pairs={{0,4},{4,0},{8,12},{12,8},{16,20},{20,16},{24,28},{28,24},{1,5},{5... | collective-permute-start | bytes 540680 | tf_op jit(solution)/shard_map/ppermute | solution.py:529
  192.5 20.2 %collective-permute-start.43 = (bf16[704,128]{1,0:T(8,128)(2,1)S(1)}, bf16[704,128]{1,0:T(8,128)(2,1)S(1)}, u32[]{:S(2)}, u32[]{:S(2)}) collective-permute-start(bf16[704,128]{1,0:T(8,128)(2,1)S(1)} %collective-permute-done.39), channel_id=1, source_target_pairs={{0,4},{4,0},{8,12},{12,8},{16,20},{20,16},{24,28},{28,24},{1,5},{5... | collective-permute-start | bytes 540680 | tf_op jit(solution)/shard_map/ppermute | solution.py:529
  201.5 12.1 %collective-permute-start.34 = (bf16[128,1408]{0,1:T(8,128)(2,1)S(1)}, bf16[128,1408]{0,1:T(8,128)(2,1)S(1)}, u32[]{:S(2)}, u32[]{:S(2)}) collective-permute-start(bf16[128,1408]{0,1:T(8,128)(2,1)S(1)} %collective-permute-done.30), channel_id=1, source_target_pairs={{0,4},{4,0},{8,12},{12,8},{16,20},{20,16},{24,28},{28,24},{1,5},{5... | collective-permute-start | bytes 1081352 | tf_op jit(solution)/shard_map/ppermute | solution.py:529
  205.0 16.3 %collective-permute-start.35 = (bf16[128,1408]{0,1:T(8,128)(2,1)S(1)}, bf16[128,1408]{0,1:T(8,128)(2,1)S(1)}, u32[]{:S(2)}, u32[]{:S(2)}) collective-permute-start(bf16[128,1408]{0,1:T(8,128)(2,1)S(1)} %collective-permute-done.31), channel_id=1, source_target_pairs={{0,4},{4,0},{8,12},{12,8},{16,20},{20,16},{24,28},{28,24},{1,5},{5... | collective-permute-start | bytes 1081352 | tf_op jit(solution)/shard_map/ppermute | solution.py:529
  205.7 22.8 %collective-permute-start.36 = (bf16[128,1408]{0,1:T(8,128)(2,1)S(1)}, bf16[128,1408]{0,1:T(8,128)(2,1)S(1)}, u32[]{:S(2)}, u32[]{:S(2)}) collective-permute-start(bf16[128,1408]{0,1:T(8,128)(2,1)S(1)} %collective-permute-done.32), channel_id=1, source_target_pairs={{0,4},{4,0},{8,12},{12,8},{16,20},{20,16},{24,28},{28,24},{1,5},{5... | collective-permute-start | bytes 1081352 | tf_op jit(solution)/shard_map/ppermute | solution.py:529
  213.7 14.9 %collective-permute-start.27 = (bf16[128,1024]{1,0:T(8,128)(2,1)S(1)}, bf16[128,1024]{1,0:T(8,128)(2,1)S(1)}, u32[]{:S(2)}, u32[]{:S(2)}) collective-permute-start(bf16[128,1024]{1,0:T(8,128)(2,1)S(1)} %multiply_convert_fusion.1), channel_id=1, source_target_pairs={{0,1},{1,0},{2,3},{3,2},{4,5},{5,4},{6,7},{7,6},{8,9},{9,8},{10,11... | collective-permute-start | bytes 786440 | tf_op jit(solution)/shard_map/ppermute | solution.py:529
  238.3 116.5 %collective-permute-start.71 = (bf16[512,1408]{1,0:T(8,128)(2,1)}, bf16[512,1408]{1,0:T(8,128)(2,1)}, u32[]{:S(2)}, u32[]{:S(2)}) collective-permute-start(bf16[512,1408]{1,0:T(8,128)(2,1)} %convolution_convert_fusion), channel_id=1, source_target_pairs={{0,4},{4,0},{8,12},{12,8},{16,20},{20,16},{24,28},{28,24},{1,5},{5... | collective-permute-start | bytes 4325384 | tf_op jit(solution)/shard_map/ppermute | solution.py:529
  240.6 12.0 %collective-permute-start.46 = (bf16[128,1024]{1,0:T(8,128)(2,1)S(1)}, bf16[128,1024]{1,0:T(8,128)(2,1)S(1)}, u32[]{:S(2)}, u32[]{:S(2)}) collective-permute-start(bf16[128,1024]{1,0:T(8,128)(2,1)S(1)} %fusion.23), channel_id=1, source_target_pairs={{0,2},{1,3},{2,0},{3,1},{4,6},{5,7},{6,4},{7,5},{8,10},{9,11},{10,... | collective-permute-start | bytes 786440 | tf_op jit(solution)/shard_map/ppermute | solution.py:529
  242.8 44.9 %collective-permute-start.75 = (bf16[704,512]{1,0:T(8,128)(2,1)}, bf16[704,512]{1,0:T(8,128)(2,1)}, u32[]{:S(2)}, u32[]{:S(2)}) collective-permute-start(bf16[704,512]{1,0:T(8,128)(2,1)} %convolution_convert_fusion.2), channel_id=1, source_target_pairs={{0,4},{4,0},{8,12},{12,8},{16,20},{20,16},{24,28},{28,24},{1,5},{5... | collective-permute-start | bytes 2162696 | tf_op jit(solution)/shard_map/ppermute | solution.py:529
  254.2 37.4 %collective-permute-start.53 = (bf16[128,1024]{1,0:T(8,128)(2,1)S(1)}, bf16[128,1024]{1,0:T(8,128)(2,1)}, u32[]{:S(2)}, u32[]{:S(2)}) collective-permute-start(bf16[128,1024]{1,0:T(8,128)(2,1)S(1)} %get-tuple-element.123), channel_id=1, source_target_pairs={{0,1},{1,0},{2,3},{3,2},{4,5},{5,4},{6,7},{7,6},{8,9},{9,8},{10,11... | collective-permute-start | bytes 786440 | tf_op jit(solution)/shard_map/ppermute | solution.py:529
  254.2 40.1 %collective-permute-start.54 = (bf16[128,1024]{1,0:T(8,128)(2,1)S(1)}, bf16[128,1024]{1,0:T(8,128)(2,1)S(1)}, u32[]{:S(2)}, u32[]{:S(2)}) collective-permute-start(bf16[128,1024]{1,0:T(8,128)(2,1)S(1)} %get-tuple-element.123), channel_id=1, source_target_pairs={{0,2},{1,3},{2,0},{3,1},{4,6},{5,7},{6,4},{7,5},{8,10},{9,11},{10,... | collective-permute-start | bytes 786440 | tf_op jit(solution)/shard_map/ppermute | solution.py:529
  291.4 15.5 %collective-permute-start.77 = (bf16[704,128]{1,0:T(8,128)(2,1)S(1)}, bf16[704,128]{1,0:T(8,128)(2,1)S(1)}, u32[]{:S(2)}, u32[]{:S(2)}) collective-permute-start(bf16[704,128]{1,0:T(8,128)(2,1)S(1)} %get-tuple-element.150), channel_id=1, source_target_pairs={{0,16},{4,20},{8,24},{12,28},{16,0},{20,4},{24,8},{28,12},{1,17},{... | collective-permute-start | bytes 540680 | tf_op jit(solution)/shard_map/ppermute | solution.py:529
  291.6 15.3 %collective-permute-start.76 = (bf16[704,128]{1,0:T(8,128)(2,1)S(1)}, bf16[704,128]{1,0:T(8,128)(2,1)S(1)}, u32[]{:S(2)}, u32[]{:S(2)}) collective-permute-start(bf16[704,128]{1,0:T(8,128)(2,1)S(1)} %get-tuple-element.148), channel_id=1, source_target_pairs={{0,8},{4,12},{8,0},{12,4},{16,24},{20,28},{24,16},{28,20},{1,9},{5... | collective-permute-start | bytes 540680 | tf_op jit(solution)/shard_map/ppermute | solution.py:529
  294.3 13.4 %collective-permute-start.55 = (bf16[128,1024]{1,0:T(8,128)(2,1)S(1)}, bf16[128,1024]{1,0:T(8,128)(2,1)S(1)}, u32[]{:S(2)}, u32[]{:S(2)}) collective-permute-start(bf16[128,1024]{1,0:T(8,128)(2,1)S(1)} %collective-permute-done.54), channel_id=1, source_target_pairs={{0,1},{1,0},{2,3},{3,2},{4,5},{5,4},{6,7},{7,6},{8,9},{9,8},{10,11... | collective-permute-start | bytes 786440 | tf_op jit(solution)/shard_map/ppermute | solution.py:529
  347.4 14.9 %collective-permute-start.56 = (bf16[128,1024]{1,0:T(8,128)(2,1)}, bf16[128,1024]{1,0:T(8,128)(2,1)}, u32[]{:S(2)}, u32[]{:S(2)}) collective-permute-start(bf16[128,1024]{1,0:T(8,128)(2,1)} %get-tuple-element.134), channel_id=1, source_target_pairs={{0,1},{1,0},{2,3},{3,2},{4,5},{5,4},{6,7},{7,6},{8,9},{9,8},{10,11... | collective-permute-start | bytes 786440 | tf_op jit(solution)/shard_map/ppermute | solution.py:529
  348.5 96.7 %collective-permute-start.59 = (bf16[512,1536]{1,0:T(8,128)(2,1)}, bf16[512,1536]{1,0:T(8,128)(2,1)}, u32[]{:S(2)}, u32[]{:S(2)}) collective-permute-start(bf16[512,1536]{1,0:T(8,128)(2,1)} %convolution_convert_fusion.1), channel_id=1, source_target_pairs={{0,4},{4,0},{8,12},{12,8},{16,20},{20,16},{24,28},{28,24},{1,5},{5... | collective-permute-start | bytes 4718600 | tf_op jit(solution)/shard_map/ppermute | solution.py:529
  349.0 46.7 %collective-permute-start.67 = (bf16[512,512]{1,0:T(8,128)(2,1)}, bf16[512,512]{1,0:T(8,128)(2,1)}, u32[]{:S(2)}, u32[]{:S(2)}) collective-permute-start(bf16[512,512]{1,0:T(8,128)(2,1)} %convolution_convert_fusion.3), channel_id=1, source_target_pairs={{0,4},{4,0},{8,12},{12,8},{16,20},{20,16},{24,28},{28,24},{1,5},{5... | collective-permute-start | bytes 1572872 | tf_op jit(solution)/shard_map/ppermute | solution.py:529
  360.5 93.0 %collective-permute-start.74 = (bf16[128,1408]{1,0:T(8,128)(2,1)}, bf16[128,1408]{1,0:T(8,128)(2,1)}, u32[]{:S(2)}, u32[]{:S(2)}) collective-permute-start(bf16[128,1408]{1,0:T(8,128)(2,1)} %get-tuple-element.142), channel_id=1, source_target_pairs={{0,24},{4,28},{8,16},{12,20},{16,8},{20,12},{24,0},{28,4},{1,25},{... | collective-permute-start | bytes 1081352 | tf_op jit(solution)/shard_map/ppermute | solution.py:529
  398.4 42.4 %collective-permute-start.70 = (bf16[512,128]{1,0:T(8,128)(2,1)S(1)}, bf16[512,128]{1,0:T(8,128)(2,1)S(1)}, u32[]{:S(2)}, u32[]{:S(2)}) collective-permute-start(bf16[512,128]{1,0:T(8,128)(2,1)S(1)} %get-tuple-element.152), channel_id=1, source_target_pairs={{0,24},{4,28},{8,16},{12,20},{16,8},{20,12},{24,0},{28,4},{1,25},{... | collective-permute-start | bytes 393224 | tf_op jit(solution)/shard_map/ppermute | solution.py:529
  400.5 42.9 %collective-permute-start.69 = (bf16[512,128]{1,0:T(8,128)(2,1)S(1)}, bf16[512,128]{1,0:T(8,128)(2,1)S(1)}, u32[]{:S(2)}, u32[]{:S(2)}) collective-permute-start(bf16[512,128]{1,0:T(8,128)(2,1)S(1)} %get-tuple-element.153), channel_id=1, source_target_pairs={{0,16},{4,20},{8,24},{12,28},{16,0},{20,4},{24,8},{28,12},{1,17},{... | collective-permute-start | bytes 393224 | tf_op jit(solution)/shard_map/ppermute | solution.py:529
  400.5 43.0 %collective-permute-start.68 = (bf16[512,128]{1,0:T(8,128)(2,1)S(1)}, bf16[512,128]{1,0:T(8,128)(2,1)S(1)}, u32[]{:S(2)}, u32[]{:S(2)}) collective-permute-start(bf16[512,128]{1,0:T(8,128)(2,1)S(1)} %get-tuple-element.151), channel_id=1, source_target_pairs={{0,8},{4,12},{8,0},{12,4},{16,24},{20,28},{24,16},{28,20},{1,9},{5... | collective-permute-start | bytes 393224 | tf_op jit(solution)/shard_map/ppermute | solution.py:529
  440.9 35.6 %collective-permute-start.73 = (bf16[128,1408]{1,0:T(8,128)(2,1)}, bf16[128,1408]{1,0:T(8,128)(2,1)S(1)}, u32[]{:S(2)}, u32[]{:S(2)}) collective-permute-start(bf16[128,1408]{1,0:T(8,128)(2,1)} %get-tuple-element.143), channel_id=1, source_target_pairs={{0,16},{4,20},{8,24},{12,28},{16,0},{20,4},{24,8},{28,12},{1,17},{... | collective-permute-start | bytes 1081352 | tf_op jit(solution)/shard_map/ppermute | solution.py:529
  443.4 33.0 %collective-permute-start.72 = (bf16[128,1408]{1,0:T(8,128)(2,1)}, bf16[128,1408]{1,0:T(8,128)(2,1)S(1)}, u32[]{:S(2)}, u32[]{:S(2)}) collective-permute-start(bf16[128,1408]{1,0:T(8,128)(2,1)} %get-tuple-element.141), channel_id=1, source_target_pairs={{0,8},{4,12},{8,0},{12,4},{16,24},{20,28},{24,16},{28,20},{1,9},{5... | collective-permute-start | bytes 1081352 | tf_op jit(solution)/shard_map/ppermute | solution.py:529
  449.9 29.0 %collective-permute-start.62 = (bf16[128,1536]{1,0:T(8,128)(2,1)S(1)}, bf16[128,1536]{1,0:T(8,128)(2,1)S(1)}, u32[]{:S(2)}, u32[]{:S(2)}) collective-permute-start(bf16[128,1536]{1,0:T(8,128)(2,1)S(1)} %get-tuple-element.139), channel_id=1, source_target_pairs={{0,24},{4,28},{8,16},{12,20},{16,8},{20,12},{24,0},{28,4},{1,25},{... | collective-permute-start | bytes 1179656 | tf_op jit(solution)/shard_map/ppermute | solution.py:529
  451.8 41.4 %collective-permute-start.61 = (bf16[128,1536]{1,0:T(8,128)(2,1)S(1)}, bf16[128,1536]{1,0:T(8,128)(2,1)S(1)}, u32[]{:S(2)}, u32[]{:S(2)}) collective-permute-start(bf16[128,1536]{1,0:T(8,128)(2,1)S(1)} %get-tuple-element.140), channel_id=1, source_target_pairs={{0,16},{4,20},{8,24},{12,28},{16,0},{20,4},{24,8},{28,12},{1,17},{... | collective-permute-start | bytes 1179656 | tf_op jit(solution)/shard_map/ppermute | solution.py:529
  453.4 39.8 %collective-permute-start.60 = (bf16[128,1536]{1,0:T(8,128)(2,1)S(1)}, bf16[128,1536]{1,0:T(8,128)(2,1)S(1)}, u32[]{:S(2)}, u32[]{:S(2)}) collective-permute-start(bf16[128,1536]{1,0:T(8,128)(2,1)S(1)} %get-tuple-element.138), channel_id=1, source_target_pairs={{0,8},{4,12},{8,0},{12,4},{16,24},{20,28},{24,16},{28,20},{1,9},{5... | collective-permute-start | bytes 1179656 | tf_op jit(solution)/shard_map/ppermute | solution.py:529
  (59 other events, 848.8 us)

commit v3 on v2

v3 whole, which is shorter than its diff:
```python
import jax
import jax.numpy as jnp
from jax import lax
from jax.experimental import pallas as pl
from jax.experimental.pallas import tpu as pltpu
from jax.sharding import PartitionSpec as P

CONV = 4


highest = lax.Precision.HIGHEST
NORM_EPS = 1e-05
UNIT_EPS = 1e-06
bf16 = jnp.bfloat16
f32 = jnp.float32


def rows_dot(left, right, kind=f32):
    return lax.dot_general(
        left, right, (((0,), (0,)), ((), ())), preferred_element_type=f32
    ).astype(kind)


def cols_dot(left, right):
    return lax.dot_general(left, right, (((1,), (1,)), ((), ())), preferred_element_type=f32)


def dot(left, right):
    return jnp.dot(left, right, preferred_element_type=f32)


CHUNK = 128
LANES = 128


def mul(left, right, over=(1, 0), exact=False):
    dims = (((over[0],), (over[1],)), ((), ()))
    if exact:
        return lax.dot_general(left, right, dims, precision=highest, preferred_element_type=f32)
    return lax.dot_general(left.astype(bf16), right.astype(bf16), dims, preferred_element_type=f32)


def square_ids():
    shape = (CHUNK, CHUNK)
    return lax.broadcasted_iota(jnp.int32, shape, 0), lax.broadcasted_iota(jnp.int32, shape, 1)


def sigmoid(v):
    return 1.0 / (1.0 + jnp.exp(-v))


def softplus(v):
    return jnp.maximum(v, 0.0) + jnp.log1p(jnp.exp(-jnp.abs(v)))


def row_sum(v):
    return jnp.sum(v, axis=1, keepdims=True)


def unit_inverse(lower):
    rows, cols = square_ids()
    inverse = jnp.where(rows == cols, 1.0, 0.0)
    block = 1
    while block < CHUNK:
        corner = (
            (rows // (2 * block) == cols // (2 * block))
            & ((rows // block) % 2 == 1)
            & ((cols // block) % 2 == 0)
        )
        part = jnp.where(corner, lower, 0.0)
        if block == 1:
            inverse = inverse - part
        else:
            inverse = inverse - mul(mul(inverse, part), inverse)
        block *= 2
    return inverse


def shifted(ref, start, back, columns):
    if start == 0 and back:
        rows = lax.broadcasted_iota(jnp.int32, (CHUNK, columns.stop - columns.start), 0)
        return jnp.where(rows >= back, pltpu.roll(ref[0:CHUNK, columns], back, 0), 0.0)
    return ref[start - back : start - back + CHUNK, columns]


def short_conv(project_ref, taps_ref, start, head, heads, columns, tap_columns):
    total = None
    for tap in range(CONV):
        row = tap * heads + head
        term = taps_ref[row : row + 1, tap_columns] * shifted(
            project_ref, start, CONV - 1 - tap, columns
        )
        total = term if total is None else total + term
    return total


def decays(rates, log_rates, bias):
    log_decay = -jnp.exp(log_rates) * softplus(rates + bias)
    place = lax.broadcasted_iota(jnp.int32, rates.shape, 0)
    total = log_decay
    step = 1
    while step < CHUNK:
        total = total + jnp.where(place >= step, pltpu.roll(total, step, 0), 0.0)
        step *= 2
    return log_decay, total


def chunk_terms(head, project_ref, taps_ref, start, total, total_rows, strength, key_width, value_width):
    width = 2 * key_width + 2 * value_width
    base = head * width
    heads = project_ref.shape[1] // width
    terms = {}
    parts = (("q", 0, key_width), ("k", key_width, key_width), ("v", 2 * key_width, value_width))
    for name, at, size in parts:
        pre = short_conv(
            project_ref,
            taps_ref,
            start,
            head,
            heads,
            slice(base + at, base + at + size),
            slice(at, at + size),
        )
        gate = sigmoid(pre)
        mixed = pre * gate
        if name != "v":
            scale = lax.rsqrt(row_sum(mixed * mixed) + UNIT_EPS)
            mixed = mixed * scale
            terms[name + "_scale"] = scale
        terms[name + "_slope"] = (pre, gate)
        terms[name] = mixed
    terms["unit_q"] = terms["q"]
    terms["q"] = terms["q"] * key_width ** (-0.5)
    lane = 2 * head
    sums = total[:, lane : lane + 1]
    across = total_rows[lane : lane + 1, :]
    rows, cols = square_ids()
    decay = jnp.where(rows >= cols, jnp.exp(jnp.minimum(sums - across, 0.0)), 0.0)
    final = total[CHUNK - 1 : CHUNK, lane : lane + 1]
    terms["b"] = strength[:, lane + 1 : lane + 2]
    terms["since"] = jnp.exp(sums)
    terms["remaining"] = jnp.exp(final - sums)
    terms["through"] = jnp.exp(final)
    terms["decay"] = decay
    terms["dots"] = mul(terms["k"], terms["k"], (1, 1)) * jnp.where(rows > cols, decay, 0.0)
    terms["scores"] = mul(terms["q"], terms["k"], (1, 1)) * decay
    return terms


def stack_rows(refs, target, column):
    at = 0
    for ref in refs:
        rows = ref.shape[0]
        columns = min(ref.shape[1], target.shape[1] - column)
        target[at : at + rows, column : column + columns] = ref[:, :columns]
        at += rows


def rows_in_time(ids_ref, refs, target):
    size = target.shape[0] // len(refs)
    for k, ref in enumerate(refs):
        at = pl.multiple_of((ids_ref[0] ^ k) * size, size)
        target[pl.ds(at, size), :] = ref[0:size, :]


def order_of(ids_ref, place):
    return ids_ref[1 + place]


def taps_from_blocks(ids_ref, mix_ref, shape):
    rows, channels = shape
    count = mix_ref.shape[0] // LANES
    part = channels // count
    lane = lax.broadcasted_iota(jnp.int32, shape, 1)
    total = jnp.zeros(shape, f32)
    for place in range(count):
        block = mix_ref[place * LANES : place * LANES + 16, mix_ref.shape[1] - LANES :]
        block = block.astype(f32)[0:rows, LANES - part :]
        wide = jnp.concatenate([block] * count, 1)
        total = total + jnp.where(lane // part == order_of(ids_ref, place), wide, 0.0)
    return total


def taps_to_blocks(ids_ref, taps_ref, target, first):
    rows, channels = taps_ref.shape
    count = target.shape[0] // LANES
    part = channels // (2 * count)
    for place in range(count):
        owner = order_of(ids_ref, first + place)
        block = jnp.zeros((rows, part), f32)
        for other in range(2 * count):
            block = block + jnp.where(
                owner == other, taps_ref[:, other * part : (other + 1) * part], 0.0
            )
        block = jnp.concatenate([jnp.zeros((rows, LANES - part), f32), block], 1)
        block = jnp.concatenate([block, jnp.zeros((16 - rows, LANES), f32)], 0)
        at = (slice(place * LANES, place * LANES + 16), slice(target.shape[1] - LANES, target.shape[1]))
        target[at] = (target[at].astype(f32) + block).astype(target.dtype)


def rows_to_blocks(ids_ref, value, send_ref, keep_ref):
    size = value.shape[0] // 4
    for k in range(4):
        target = send_ref if k % 2 else keep_ref
        half = (k // 2) * size
        for block in range(4):

            @pl.when((ids_ref[0] ^ k) == block)
            def _(block=block, half=half, target=target):
                target[half : half + size, :] = value[block * size : (block + 1) * size, :].astype(
                    target.dtype
                )


def mixer_forward(near, refs):
    (ids_ref, taps_in_ref, log_rates_ref, bias_ref, gain_ref), row_refs, mix_refs, outs, scratch = refs
    gated_ref, project_ref, rates_ref, out_ref, states_ref, carried_ref, inverse_ref = outs[:7]
    normed_ref, mix_ref, taps_ref = outs[7:]
    q_scr, kr_scr, p_scr, w_scr, u_scr = scratch
    length = normed_ref.shape[0]
    value_width = gain_ref.shape[1]
    heads = out_ref.shape[1] // value_width
    width = project_ref.shape[1] // heads
    key_width = (width - 2 * value_width) // 2
    chunks = length // CHUNK
    rows_in_time(ids_ref, row_refs, normed_ref)
    stack_rows(mix_refs, mix_ref, 0)
    if near:
        taps_ref[...] = taps_from_blocks(ids_ref, mix_ref, taps_in_ref.shape)
    else:
        taps_ref[...] = taps_in_ref[...]
    for head in range(heads):
        columns = slice(head * width, (head + 1) * width)
        project_ref[:, columns] = dot(normed_ref[...], mix_ref[:, columns])
    rates_ref[...] = dot(normed_ref[...], mix_ref[:, heads * width :])
    through = {}
    for chunk in range(chunks):
        start = chunk * CHUNK
        rows = slice(start, start + CHUNK)
        rates = rates_ref[rows, :]
        _, total = decays(rates, log_rates_ref[...], bias_ref[...])
        strength = sigmoid(rates)
        total_rows = jnp.transpose(total)
        for head in range(heads):
            t = chunk_terms(
                head, project_ref, taps_ref, start, total, total_rows, strength, key_width, value_width
            )
            inverse = unit_inverse(t["b"] * t["dots"])
            inverse_ref[chunk, head] = inverse
            side = jnp.concatenate([(t["b"] * t["since"]) * t["k"], t["b"] * t["v"]], 1)
            solved = mul(inverse, side)
            w_scr[chunk, head] = solved[:, :key_width].astype(bf16)
            u_scr[chunk, head] = solved[:, key_width:]
            q_scr[chunk, head] = (t["q"] * t["since"]).astype(bf16)
            kr_scr[chunk, head] = t["k"] * t["remaining"]
            p_scr[chunk, head] = t["scores"].astype(bf16)
            through[chunk, head] = t["through"]
    state = [jnp.zeros((key_width, value_width), f32) for _ in range(heads)]
    for chunk in range(chunks):
        rows = slice(chunk * CHUNK, (chunk + 1) * CHUNK)
        for head in range(heads):
            columns = slice(head * value_width, (head + 1) * value_width)
            states_ref[chunk, head] = state[head]
            low = state[head].astype(bf16)
            carried = u_scr[chunk, head] - mul(w_scr[chunk, head], low)
            carried_ref[rows, columns] = carried
            out_ref[rows, columns] = mul(q_scr[chunk, head], low) + mul(p_scr[chunk, head], carried)
            state[head] = through[chunk, head] * state[head] + mul(
                kr_scr[chunk, head], carried, (0, 0), exact=True
            )
    for chunk in range(chunks):
        rows = slice(chunk * CHUNK, (chunk + 1) * CHUNK)
        for head in range(heads):
            columns = slice(head * value_width, (head + 1) * value_width)
            out = out_ref[rows, columns]
            gate = project_ref[rows, (head + 1) * width - value_width : (head + 1) * width]
            scale = lax.rsqrt(row_sum(out * out) / value_width + NORM_EPS)
            gated_ref[rows, columns] = (
                out * scale * gain_ref[...] * (gate * sigmoid(gate))
            ).astype(bf16)


def mixer_backward(near, refs):
    fixed, row_refs, w_out_refs, kept, outs, scratch = refs
    ids_ref, log_rates_ref, bias_ref, gain_ref = fixed
    (
        project_ref,
        rates_ref,
        out_ref,
        states_ref,
        carried_ref,
        inverse_ref,
        normed_ref,
        _,
        taps_ref,
    ) = kept
    grads_ref, grad_taps_ref, grad_gain_ref, grad_lanes_ref, send_a_ref, send_b_ref, grad_ref = outs
    (
        grad_out_scr,
        back_scr,
        grad_carried_scr,
        q_scr,
        kr_scr,
        p_scr,
        w_scr,
        w_out_scr,
        mixed_scr,
    ) = scratch
    grad_project_ref = grads_ref
    length = grad_ref.shape[0]
    value_width = gain_ref.shape[1]
    heads = out_ref.shape[1] // value_width
    width = project_ref.shape[1] // heads
    key_width = (width - 2 * value_width) // 2
    channels = 2 * key_width + value_width
    chunks = length // CHUNK
    rows_in_time(ids_ref, row_refs, grad_ref)
    stack_rows(w_out_refs, w_out_scr, 0)
    grad_out_scr[...] = dot(grad_ref[...], w_out_scr[...])
    gain = gain_ref[...]
    gain_total = jnp.zeros((1, value_width), f32)
    terms = {}

    def gather_terms(chunk):
        start = chunk * CHUNK
        rates = rates_ref[start : start + CHUNK, :]
        _, total = decays(rates, log_rates_ref[...], bias_ref[...])
        strength = sigmoid(rates)
        total_rows = jnp.transpose(total)
        return [
            chunk_terms(
                head, project_ref, taps_ref, start, total, total_rows, strength, key_width, value_width
            )
            for head in range(heads)
        ]

    through = {}
    for chunk in range(chunks):
        rows = slice(chunk * CHUNK, (chunk + 1) * CHUNK)
        terms = gather_terms(chunk)
        for head in range(heads):
            columns = slice(head * value_width, (head + 1) * value_width)
            gate_columns = slice((head + 1) * width - value_width, (head + 1) * width)
            t = terms[head]
            out = out_ref[rows, columns]
            gate = project_ref[rows, gate_columns]
            grad = grad_out_scr[rows, columns]
            scale = lax.rsqrt(row_sum(out * out) / value_width + NORM_EPS)
            unit = out * scale
            sig = sigmoid(gate)
            act = gate * sig
            gain_total = gain_total + jnp.sum(grad * unit * act, axis=0, keepdims=True)
            grad_project_ref[rows, gate_columns] = (
                grad * gain * unit * (sig * (1.0 + gate * (1.0 - sig)))
            ).astype(bf16)
            inner = grad * act * gain
            grad_out_scr[rows, columns] = scale * (
                inner - unit * (row_sum(inner * unit) / value_width)
            )
            w_scr[chunk, head] = mul(
                inverse_ref[chunk, head], (t["b"] * t["since"]) * t["k"]
            ).astype(bf16)
            q_scr[chunk, head] = (t["q"] * t["since"]).astype(bf16)
            kr_scr[chunk, head] = (t["k"] * t["remaining"]).astype(bf16)
            p_scr[chunk, head] = t["scores"].astype(bf16)
            through[chunk, head] = t["through"]
    grad_gain_ref[...] = gain_total

    back = [jnp.zeros((key_width, value_width), f32) for _ in range(heads)]
    for chunk in reversed(range(chunks)):
        rows = slice(chunk * CHUNK, (chunk + 1) * CHUNK)
        for head in range(heads):
            columns = slice(head * value_width, (head + 1) * value_width)
            back_scr[chunk, head] = back[head]
            grad_out = grad_out_scr[rows, columns].astype(bf16)
            grad_carried = mul(p_scr[chunk, head], grad_out, (0, 0)) + mul(
                kr_scr[chunk, head], back[head]
            )
            grad_carried_scr[rows, columns] = grad_carried
            back[head] = (
                through[chunk, head] * back[head]
                + mul(q_scr[chunk, head], grad_out, (0, 0))
                - mul(w_scr[chunk, head], grad_carried, (0, 0))
            )

    rows_at, cols_at = square_ids()
    lane = lax.broadcasted_iota(jnp.int32, (CHUNK, LANES), 1)
    place = lax.broadcasted_iota(jnp.int32, (CHUNK, LANES), 0)
    log_total = jnp.zeros((1, LANES), f32)
    bias_total = jnp.zeros((1, LANES), f32)
    for chunk in range(chunks):
        rows = slice(chunk * CHUNK, (chunk + 1) * CHUNK)
        terms = gather_terms(chunk)
        sums_grad = jnp.zeros((CHUNK, LANES), f32)
        strength_grad = jnp.zeros((CHUNK, LANES), f32)
        for head in range(heads):
            columns = slice(head * value_width, (head + 1) * value_width)
            t = terms[head]
            b, since, remaining, decay = t["b"], t["since"], t["remaining"], t["decay"]
            q, k, v = t["q"], t["k"], t["v"]
            state = states_ref[chunk, head]
            back_now = back_scr[chunk, head]
            carried = carried_ref[rows, columns]
            grad_out = grad_out_scr[rows, columns]
            grad_side = mul(inverse_ref[chunk, head], grad_carried_scr[rows, columns], (0, 0))
            strict = jnp.where(rows_at > cols_at, -mul(grad_side, carried, (1, 1)), 0.0)
            grad_scores = mul(grad_out, carried, (1, 1))
            side_state = mul(grad_side, state, (1, 1))
            out_state = since * mul(grad_out, state, (1, 1))
            carried_back = remaining * mul(carried, back_now, (1, 1))
            key_side = since * row_sum(k * side_state)
            strict_dots = strict * t["dots"]
            grad_strength = row_sum(grad_side * v) - key_side + row_sum(strict_dots)
            pulls = grad_scores * t["scores"] + b * strict_dots
            key_back = row_sum(k * carried_back)
            grad_sums = (
                row_sum(pulls - jnp.transpose(pulls))
                - b * key_side
                + row_sum(q * out_state)
                - key_back
            )
            final = jnp.sum(key_back, axis=0, keepdims=True) + t["through"] * jnp.sum(
                row_sum(back_now * state), axis=0, keepdims=True
            )
            scores_low = (grad_scores * decay).astype(bf16)
            strict_low = (strict * (b * decay)).astype(bf16)
            k_low, q_low = k.astype(bf16), q.astype(bf16)
            grad_q = out_state + mul(scores_low, k_low)
            grad_k = (
                carried_back
                - (b * since) * side_state
                + mul(scores_low, q_low, (0, 0))
                + mul(strict_low, k_low)
                + mul(strict_low, k_low, (0, 0))
            )
            grad_v = b * grad_side
            sums_grad = sums_grad + jnp.where(
                lane == 2 * head, grad_sums + jnp.where(place == CHUNK - 1, final, 0.0), 0.0
            )
            strength_grad = strength_grad + jnp.where(lane == 2 * head + 1, grad_strength, 0.0)
            grad_q = grad_q * key_width ** (-0.5)
            unit = t["unit_q"]
            grad_q = t["q_scale"] * (grad_q - unit * row_sum(grad_q * unit))
            grad_k = t["k_scale"] * (grad_k - k * row_sum(grad_k * k))
            at = head * channels
            for name, grad, size in (
                ("q", grad_q, key_width),
                ("k", grad_k, key_width),
                ("v", grad_v, value_width),
            ):
                pre, sig = t[name + "_slope"]
                mixed_scr[rows, at : at + size] = grad * (sig * (1.0 + pre * (1.0 - sig)))
                at += size
        step = 1
        while step < CHUNK:
            sums_grad = sums_grad + jnp.where(
                place < CHUNK - step, pltpu.roll(sums_grad, CHUNK - step, 0), 0.0
            )
            step *= 2
        rates = rates_ref[rows, :]
        log_decay, _ = decays(rates, log_rates_ref[...], bias_ref[...])
        strength = sigmoid(rates)
        inputs_grad = sums_grad * (-jnp.exp(log_rates_ref[...])) * sigmoid(rates + bias_ref[...])
        log_total = log_total + jnp.sum(sums_grad * log_decay, axis=0, keepdims=True)
        bias_total = bias_total + jnp.sum(inputs_grad, axis=0, keepdims=True)
        grads_ref[rows, heads * width :] = (
            inputs_grad + strength_grad * strength * (1.0 - strength)
        ).astype(bf16)
    grad_lanes_ref[0:1, :] = log_total
    grad_lanes_ref[1:2, :] = bias_total

    mixed_scr[length : length + 8, :] = jnp.zeros((8, mixed_scr.shape[1]), f32)
    for head in range(heads):
        columns = slice(head * channels, (head + 1) * channels)
        source = slice(head * width, head * width + channels)
        taps_here = [jnp.zeros((1, channels), f32) for _ in range(CONV)]
        for chunk in range(chunks):
            start = chunk * CHUNK
            total = None
            now = mixed_scr[start : start + CHUNK, columns]
            for tap in range(CONV):
                ahead = CONV - 1 - tap
                row = tap * heads + head
                term = taps_ref[row : row + 1, :] * (
                    mixed_scr[start + ahead : start + ahead + CHUNK, columns]
                )
                total = term if total is None else total + term
                taps_here[tap] = taps_here[tap] + jnp.sum(
                    now * shifted(project_ref, start, ahead, source), axis=0, keepdims=True
                )
            grads_ref[start : start + CHUNK, source] = total.astype(bf16)
        for tap in range(CONV):
            row = tap * heads + head
            grad_taps_ref[row : row + 1, :] = taps_here[tap]
    half = normed_ref.shape[1] // 2
    cut = send_a_ref.shape[1]
    send_a_ref[...] = rows_dot(normed_ref[:, half:], grads_ref[:, :cut], bf16)
    send_b_ref[...] = rows_dot(normed_ref[:, half:], grads_ref[:, cut:], bf16)
    if near:
        taps_to_blocks(ids_ref, grad_taps_ref, send_b_ref, half // LANES)


def mixer_products(near, refs):
    ids_ref, normed_ref, grads_ref, mix_ref, grad_taps_ref, keep_a_ref, keep_b_ref, back_send_ref, back_keep_ref = refs
    back = cols_dot(grads_ref[...], mix_ref[...])
    rows_to_blocks(ids_ref, back, back_send_ref, back_keep_ref)
    half = normed_ref.shape[1] // 2
    cut = keep_a_ref.shape[1]
    keep_a_ref[...] = rows_dot(normed_ref[:, :half], grads_ref[:, :cut])
    keep_b_ref[...] = rows_dot(normed_ref[:, :half], grads_ref[:, cut:])
    if near:
        taps_to_blocks(ids_ref, grad_taps_ref, keep_b_ref, 0)


def norm_scale(rows):
    return lax.rsqrt(jnp.mean(rows * rows, axis=1, keepdims=True) + NORM_EPS)


def prepare(ids_ref, rows_ref, grad_ref, mixer_gain_ref, ffn_gain_ref, resid_ref, both_ref, gains_ref):
    size = rows_ref.shape[0]
    count = rows_ref.shape[1] // LANES
    for place in range(count):
        at = pl.multiple_of(order_of(ids_ref, place) * LANES, LANES)
        here = slice(place * LANES, (place + 1) * LANES)
        resid_ref[:, here] = rows_ref[:, pl.ds(at, LANES)].astype(f32)
        both_ref[size:, here] = grad_ref[:, pl.ds(at, LANES)]
        gains_ref[0:1, here] = mixer_gain_ref[:, pl.ds(at, LANES)]
        gains_ref[1:2, here] = ffn_gain_ref[:, pl.ds(at, LANES)]
    resid = resid_ref[...]
    both_ref[0:size, :] = (resid * norm_scale(resid) * gains_ref[0:1, :]).astype(bf16)


def out_product(ids_ref, gated_ref, *refs):
    w_out_refs, (send_ref, keep_ref, w_out_scr) = refs[:-3], refs[-3:]
    stack_rows(w_out_refs, w_out_scr, 0)
    rows_to_blocks(ids_ref, cols_dot(gated_ref[...], w_out_scr[...]), send_ref, keep_ref)


def fold(keep_ref, got_ref, keep_out_ref, send_ref):
    size = send_ref.shape[0]
    keep_out_ref[...] = keep_ref[0:size, :] + got_ref[0:size, :].astype(f32)
    send_ref[...] = (keep_ref[size:, :] + got_ref[size:, :].astype(f32)).astype(bf16)


def middle_norm(keep_ref, got_ref, resid_in_ref, gains_ref, resid_ref, ffn_in_ref):
    resid = resid_in_ref[...] + keep_ref[...] + got_ref[...].astype(f32)
    resid_ref[...] = resid
    ffn_in_ref[...] = (resid * norm_scale(resid) * gains_ref[1:2, :]).astype(bf16)


def feed_forward(groups, refs):
    ffn_refs, grad_refs, weight_refs, outs, weights_scr = refs
    ffn_ref, top_ref, hidden_ref, grad_gate_ref, out_send, out_keep, back_send, back_keep = outs
    size = ffn_refs[0].shape[0]
    column = 0
    for group in weight_refs:
        stack_rows(group, weights_scr, column)
        column += group[0].shape[1]
    for k in range(4):
        ffn_ref[k * size : (k + 1) * size, :] = ffn_refs[k][...]
        top_ref[k * size : (k + 1) * size, :] = grad_refs[k][size:, :]
    hidden_size = hidden_ref.shape[1]
    first, second = groups
    gate_up_w = weights_scr[:, first:second]
    down_w = weights_scr[:, second : second + hidden_size]
    gate_up = dot(ffn_ref[...], gate_up_w)
    grad_hidden = dot(top_ref[...], down_w)
    gate, up = gate_up[:, :hidden_size], gate_up[:, hidden_size:]
    sig = sigmoid(gate)
    act = gate * sig
    hidden_ref[...] = (act * up).astype(bf16)
    grad_gate_ref[:, :hidden_size] = (grad_hidden * up * (sig * (1.0 + gate * (1.0 - sig)))).astype(bf16)
    grad_gate_ref[:, hidden_size:] = (grad_hidden * act).astype(bf16)
    back = cols_dot(grad_gate_ref[...], gate_up_w)
    out = cols_dot(hidden_ref[...], down_w)
    for value, send, keep in ((back, back_send, back_keep), (out, out_send, out_keep)):
        for k in range(4):
            target = send if k % 2 else keep
            half = (k // 2) * size
            target[half : half + size, :] = value[k * size : (k + 1) * size, :].astype(target.dtype)


def norm_reverse(grad, rows, gain):
    scale = norm_scale(rows)
    unit = rows * scale
    inner = grad * gain
    gain_grad = jnp.sum(grad * unit, axis=0, keepdims=True)
    return scale * (inner - unit * jnp.mean(inner * unit, axis=1, keepdims=True)), gain_grad


def middle_back(
    back_keep_ref, back_got_ref, resid_ref, both_ref, gains_ref, grad_ref, low_ref, gain_grad_ref
):
    grad_ffn_in = back_keep_ref[...] + back_got_ref[...].astype(f32)
    grad, gain_grad = norm_reverse(grad_ffn_in, resid_ref[...], gains_ref[1:2, :])
    grad = grad + both_ref[both_ref.shape[0] // 2 :, :].astype(f32)
    grad_ref[...] = grad
    low_ref[...] = grad.astype(bf16)
    gain_grad_ref[...] = gain_grad


def place_of(ids_ref, block, count):
    return ids_ref[1 + count + block]


def last_out(ids_ref, keep_ref, got_ref, resid_ref, out_ref, scr):
    scr[...] = resid_ref[...] + keep_ref[...] + got_ref[...].astype(f32)
    count = out_ref.shape[1] // LANES
    for block in range(count):
        at = pl.multiple_of(place_of(ids_ref, block, count) * LANES, LANES)
        out_ref[:, block * LANES : (block + 1) * LANES] = scr[:, pl.ds(at, LANES)].astype(bf16)


def last_grad(
    ids_ref, keep_ref, got_ref, resid_in_ref, gains_ref, grad_ref, gain_grad_ref, out_ref, gains_out_ref, scr, gain_scr
):
    grad_normed = keep_ref[...] + got_ref[...].astype(f32)
    grad, gain_grad = norm_reverse(grad_normed, resid_in_ref[...], gains_ref[0:1, :])
    scr[...] = grad + grad_ref[...]
    gain_scr[0:1, :] = gain_grad
    gain_scr[1:2, :] = gain_grad_ref[...]
    count = out_ref.shape[1] // LANES
    for block in range(count):
        at = pl.multiple_of(place_of(ids_ref, block, count) * LANES, LANES)
        here = slice(block * LANES, (block + 1) * LANES)
        out_ref[:, here] = scr[:, pl.ds(at, LANES)]
        gains_out_ref[:, here] = gain_scr[:, pl.ds(at, LANES)]


def call(kernel, outs, operands, scratch=(), name=None, scalar=True):
    specs = [pl.BlockSpec(memory_space=pltpu.VMEM)] * len(operands)
    if scalar:
        specs[0] = pl.BlockSpec(memory_space=pltpu.SMEM)
    return pl.pallas_call(
        kernel,
        out_shape=tuple(jax.ShapeDtypeStruct(shape, kind) for shape, kind in outs),
        in_specs=specs,
        out_specs=tuple([pl.BlockSpec(memory_space=pltpu.VMEM)] * len(outs)),
        scratch_shapes=[pltpu.VMEM(shape, kind) for shape, kind in scratch],
        compiler_params=pltpu.CompilerParams(vmem_limit_bytes=56 * 2**20),
        name=name,
    )(*operands)


def cut_list(items, sizes):
    parts, at = [], 0
    for size in sizes:
        parts.append(items[at : at + size])
        at += size
    return parts


def run_forward(near, ids, rows, mix, taps, log_rates, bias, gain):
    length = rows[0].shape[0] // 2 * len(rows)
    model, value_width = rows[0].shape[1], gain.shape[1]
    wide = mix[0].shape[1]
    columns = wide - LANES
    channels = taps.shape[1]
    heads = taps.shape[0] // CONV
    key_width = (channels - value_width) // 2
    pair = (length // CHUNK, heads)
    values = heads * value_width

    def kernel(*refs):
        mixer_forward(near, cut_list(refs, (5, len(rows), len(mix), 10, 5)))

    return call(
        kernel,
        (
            ((length, values), bf16),
            ((length, columns), f32),
            ((length, LANES), f32),
            ((length, values), f32),
            (pair + (key_width, value_width), f32),
            ((length, values), f32),
            (pair + (CHUNK, CHUNK), f32),
            ((length, model), bf16),
            ((model, wide), bf16),
            (taps.shape, f32),
        ),
        (ids, taps, log_rates, bias, gain, *rows, *mix),
        (
            (pair + (CHUNK, key_width), bf16),
            (pair + (CHUNK, key_width), f32),
            (pair + (CHUNK, CHUNK), bf16),
            (pair + (CHUNK, key_width), bf16),
            (pair + (CHUNK, value_width), f32),
        ),
        "mixer_forward",
    )


def run_backward(near, ids, rows, w_out, log_rates, bias, gain, kept):
    project, _, out, states, _, _, normed, mix, taps = kept
    length, model = normed.shape
    values, value_width = out.shape[1], gain.shape[1]
    wide = mix.shape[1]
    key_width, heads = states.shape[2], states.shape[1]
    pair = (length // CHUNK, heads)
    cut = wide // 2 // LANES * LANES + LANES

    def kernel(*refs):
        mixer_backward(near, cut_list(refs, (4, len(rows), len(w_out), len(kept), 7, 9)))

    return call(
        kernel,
        (
            ((length, wide), bf16),
            (taps.shape, f32),
            ((1, value_width), f32),
            ((2, LANES), f32),
            ((model // 2, cut), bf16),
            ((model // 2, wide - cut), bf16),
            ((length, model), bf16),
        ),
        (ids, log_rates, bias, gain, *rows, *w_out, *kept),
        (
            ((length, values), f32),
            (pair + (key_width, value_width), f32),
            ((length, values), f32),
            (pair + (CHUNK, key_width), bf16),
            (pair + (CHUNK, key_width), bf16),
            (pair + (CHUNK, CHUNK), bf16),
            (pair + (CHUNK, key_width), bf16),
            ((model, values), bf16),
            ((length + 8, heads * taps.shape[1]), f32),
        ),
        "mixer_backward",
    )


def swap(array, axis, size, offset):
    return lax.ppermute(array, axis, [(i, i ^ offset) for i in range(size)])


def after(arrays, others):
    kept, _ = lax.optimization_barrier((arrays, others))
    return kept


def per_device(
    layer_in,
    mixer_gain,
    w_mix,
    w_rates,
    conv_taps,
    a_log,
    dt_bias,
    head_gain,
    w_out,
    ffn_gain,
    w_gate_up,
    w_down,
    out_grad,
):
    size = lax.axis_size("dp")
    ranks = lax.axis_size("tensor")
    depth, heads, width = w_mix.shape
    model = layer_in.shape[1]
    hidden = w_gate_up.shape[2]
    value_size = w_out.shape[0]
    rows = layer_in.shape[0]
    taps_shape = conv_taps.shape
    part = taps_shape[2]
    near = size == 8 and depth == LANES and 2 * part == LANES
    half = size // 2
    rank, own = lax.axis_index("tensor"), lax.axis_index("dp")
    blocks = model // LANES
    if near:
        offsets = [2 * p for p in range(half)] + [2 * p + 1 for p in range(half)]
        order = own ^ jnp.array(offsets, jnp.int32)
        places = [offsets.index(k) for k in range(size)]
        index = own ^ jnp.arange(size, dtype=jnp.int32)
        place = jnp.where(index % 2 == 0, index // 2, half + index // 2)
        assert places == [k // 2 if k % 2 == 0 else half + k // 2 for k in range(size)]
    else:
        order = place = jnp.arange(blocks, dtype=jnp.int32)
    ids = jnp.concatenate([jnp.full((1,), rank, jnp.int32), order, place])

    def near_z(shard):
        return [shard] + [swap(shard, "dp", size, 2 * p) for p in range(1, half)]

    def near_x(shards):
        return [swap(shard, "dp", size, 1) for shard in shards]

    def far(shard):
        return lax.all_gather(shard, "dp", axis=0, tiled=True)

    def rows_y(block):
        return swap(block, "tensor", ranks, 2)

    def rows_core(block):
        return swap(block, "tensor", ranks, 1)

    def gather_rows(block):
        across = rows_y(block)
        return [block, rows_core(block), across, rows_core(across)]

    def sum_rows(send, keep, name):
        got = rows_core(send)
        shape = (rows, model)
        keep, send = call(fold, ((shape, f32), (shape, bf16)), (keep, got), name=name, scalar=False)
        return keep, rows_y(send)

    rates_tile = jnp.pad(w_rates.reshape(depth, 2 * heads), ((0, 0), (0, LANES - 2 * heads)))
    if near:
        taps_tile = conv_taps.reshape(CONV * heads, part)
        taps_tile = jnp.pad(taps_tile, ((0, depth - CONV * heads), (LANES - part, 0)))
        rates_tile = rates_tile + taps_tile
    mix_shard = jnp.concatenate([w_mix.reshape(depth, heads * width), rates_tile], 1)
    gate_up_shard = w_gate_up.reshape(depth, 2 * hidden)
    total = value_size + 3 * hidden
    filler = -total % (3 * LANES)
    rest_shard = jnp.concatenate(
        [w_out.T, gate_up_shard, w_down.T, jnp.zeros((depth, filler), bf16)], 1
    )
    step = (total + filler) // 3

    if near:
        mix_a, mix_b = mix_shard[: depth // 2], mix_shard[depth // 2 :]
        mix_az = near_z(mix_a)
    square = (rows, model)
    resid_in, both, gains = call(
        prepare,
        ((square, f32), ((2 * rows, model), bf16), ((2, model), f32)),
        (ids, layer_in, out_grad, mixer_gain.reshape(1, -1), ffn_gain.reshape(1, -1)),
        name="prepare",
    )
    if near:
        mix_b = after(mix_b, mix_az)
        mix_bz = near_z(mix_b)
        mix_ax = near_x(mix_az)
    both_all = gather_rows(both)
    if near:
        rest_0, rest_1, rest_2 = (rest_shard[:, g * step : (g + 1) * step] for g in range(3))
        rest_0 = after(rest_0, (mix_bz, mix_ax))
        rest_0z = near_z(rest_0)
        mix_bx = near_x(mix_bz)
        rest_1 = after(rest_1, (rest_0z, mix_bx))
        rest_1z = near_z(rest_1)
        rest_0x = near_x(rest_0z)
        mix_slots = [half_slot for pair in zip(mix_az + mix_ax, mix_bz + mix_bx) for half_slot in pair]
        taps = jnp.zeros((CONV * heads, part * size), f32)
    else:
        mix_slots = [far(mix_shard)]
        taps = lax.all_gather(conv_taps, "dp", axis=2, tiled=True).astype(f32)
        taps = taps.reshape(CONV * heads, part * size)
        rest_full = far(rest_shard)
        rest_slots = [[rest_full[:, g * step : (g + 1) * step]] for g in range(3)]

    first_head = rank * heads

    def on_lanes(per_head):
        here = lax.dynamic_slice_in_dim(per_head, first_head, heads)
        pairs = jnp.stack([here, jnp.zeros_like(here)], 1).reshape(1, -1)
        return jnp.pad(pairs, ((0, 0), (0, LANES - pairs.shape[1])))

    def off_lanes(row):
        here = row[: 2 * heads : 2]
        return lax.dynamic_update_slice_in_dim(jnp.zeros_like(a_log), here, first_head, 0)

    lanes = (on_lanes(a_log), on_lanes(dt_bias), head_gain.reshape(1, -1))
    gated, *kept = run_forward(near, ids, both_all, mix_slots, taps, *lanes)
    if near:
        gated, rest_2, rest_1z, rest_0x = lax.optimization_barrier((gated, rest_2, rest_1z, rest_0x))
        rest_2z = near_z(rest_2)
        rest_1x = near_x(rest_1z)
        rest_slots = [rest_0z + rest_0x]
    block_pair = (2 * rows, model)
    out_send, out_keep = call(
        out_product,
        ((block_pair, bf16), (block_pair, f32)),
        (ids, gated, *rest_slots[0]),
        (((model, value_size), bf16),),
        "out_product",
    )
    out_keep, out_got = sum_rows(out_send, out_keep, "out_fold")
    resid, ffn_in = call(
        middle_norm, ((square, f32), (square, bf16)), (out_keep, out_got, resid_in, gains), name="middle_norm", scalar=False
    )
    if near:
        ffn_in, rest_2z, rest_1x = lax.optimization_barrier((ffn_in, rest_2z, rest_1x))
        rest_2x = near_x(rest_2z)
        rest_slots += [rest_1z + rest_1x, rest_2z + rest_2x]
    ffn_all = gather_rows(ffn_in)
    tokens = rows * ranks
    counts = [len(group) for group in rest_slots]

    def ffn_kernel(*refs):
        ffn_refs, grad_refs, weights, outs, scratch = cut_list(refs, (4, 4, sum(counts), 8, 1))
        feed_forward(
            (value_size, value_size + 2 * hidden),
            (ffn_refs, grad_refs, cut_list(weights, counts), outs, scratch[0]),
        )

    ffn_rows, top_rows, hidden_low, grad_gate, ffn_send, ffn_keep, back_send, back_keep = call(
        ffn_kernel,
        (
            ((tokens, model), bf16),
            ((tokens, model), bf16),
            ((tokens, hidden), bf16),
            ((tokens, 2 * hidden), bf16),
            (block_pair, bf16),
            (block_pair, f32),
            (block_pair, bf16),
            (block_pair, f32),
        ),
        (*ffn_all, *both_all, *[slot for group in rest_slots for slot in group]),
        (((model, total + filler), bf16),),
        "feed_forward",
        scalar=False,
    )
    split = model // 2

    def scatter_x(send):
        return swap(send, "dp", size, 1) if near else send

    def scatter_z(keep, got):
        if not near:
            return keep, got
        summed = keep + got.astype(f32)
        low = summed.astype(bf16)
        return summed[:depth], [
            swap(low[p * depth : (p + 1) * depth], "dp", size, 2 * p) for p in range(1, half)
        ]

    def scatter_end(keep, got):
        if not near:
            return lax.psum_scatter(
                jnp.concatenate([keep, got.astype(f32)], 0), "dp", scatter_dimension=0, tiled=True
            )
        for block in got:
            keep = keep + block.astype(f32)
        return keep

    gate_x = scatter_x(rows_dot(ffn_rows[:, split:], grad_gate, bf16))
    back_keep, back_got = sum_rows(back_send, back_keep, "back_fold")
    down_x = scatter_x(rows_dot(top_rows[:, split:], hidden_low, bf16))
    grad_resid, mix_low, ffn_gain_grad = call(
        middle_back,
        ((square, f32), (square, bf16), ((1, model), f32)),
        (back_keep, back_got, resid, both, gains),
        name="middle_back",
        scalar=False,
    )
    mix_all = gather_rows(mix_low)
    gate_keep = rows_dot(ffn_rows[:, :split], grad_gate)
    down_keep = rows_dot(top_rows[:, :split], hidden_low)
    ffn_keep, ffn_got = sum_rows(ffn_send, ffn_keep, "ffn_fold")
    (layer_out,) = call(
        last_out, ((square, bf16),), (ids, ffn_keep, ffn_got, resid), ((square, f32),), "last_out"
    )
    gate_own, gate_z = scatter_z(gate_keep, gate_x)
    down_own, down_z = scatter_z(down_keep, down_x)
    grads, taps_grad, head_gain_grad, lanes_grad, mix_send_a, mix_send_b, grad_rows = run_backward(
        near, ids, mix_all, rest_slots[0], *lanes, kept
    )
    mix_xa, mix_xb = scatter_x(mix_send_a), scatter_x(mix_send_b)
    out_x = scatter_x(rows_dot(grad_rows[:, split:], gated, bf16))
    normed_rows, mix_full = kept[6], kept[7]
    cuts = (mix_send_a.shape[1], mix_send_b.shape[1])

    def products_kernel(*refs):
        mixer_products(near, refs)

    mix_keep_a, mix_keep_b, norm_send, norm_keep = call(
        products_kernel,
        (
            ((split, cuts[0]), f32),
            ((split, cuts[1]), f32),
            (block_pair, bf16),
            (block_pair, f32),
        ),
        (ids, normed_rows, grads, mix_full, taps_grad),
        name="mixer_products",
    )
    norm_keep, norm_got = sum_rows(norm_send, norm_keep, "norm_fold")
    out_keep = rows_dot(grad_rows[:, :split], gated)
    in_grad, gains_grad = call(
        last_grad,
        ((square, f32), ((2, model), f32)),
        (ids, norm_keep, norm_got, resid_in, gains, grad_resid, ffn_gain_grad),
        ((square, f32), ((2, model), f32)),
        "last_grad",
    )
    mix_own_a, mix_za = scatter_z(mix_keep_a, mix_xa)
    mix_own_b, mix_zb = scatter_z(mix_keep_b, mix_xb)
    out_own, out_z = scatter_z(out_keep, out_x)

    small = jnp.concatenate(
        [
            gains_grad.reshape(-1),
            head_gain_grad.reshape(-1),
            off_lanes(lanes_grad[0]),
            off_lanes(lanes_grad[1]),
        ]
    )
    length = small.size
    small = jnp.pad(small, (0, -length % (8 * LANES))).reshape(8, -1)
    for offset in (1, 2):
        small = small + swap(small, "tensor", ranks, offset)
    if near:
        for offset in (1, 2, 4):
            small = small + swap(small, "dp", size, offset)
    else:
        small = lax.psum(small, "dp")
    small = small.reshape(-1)[:length]
    grad_mixer_gain, grad_ffn_gain = small[:model], small[model : 2 * model]
    small = small[2 * model :]
    grad_head_gain, small = small[: head_gain.size], small[head_gain.size :]
    grad_a_log, grad_dt_bias = small[: a_log.size], small[a_log.size :]

    gate_total = scatter_end(gate_own, gate_z)
    down_total = scatter_end(down_own, down_z)
    out_total = scatter_end(out_own, out_z)
    mix_total = jnp.concatenate([scatter_end(mix_own_a, mix_za), scatter_end(mix_own_b, mix_zb)], 1)
    grad_w_rates = mix_total[:, heads * width : heads * width + 2 * heads].reshape(w_rates.shape)
    if near:
        grad_taps = mix_total[: CONV * heads, mix_total.shape[1] - part :].reshape(taps_shape)
    else:
        grad_taps = lax.psum_scatter(
            taps_grad.reshape(CONV, heads, -1), "dp", scatter_dimension=2, tiled=True
        )
    return (
        layer_out,
        in_grad,
        grad_mixer_gain,
        mix_total[:, : heads * width].reshape(w_mix.shape),
        grad_w_rates,
        grad_taps,
        grad_a_log,
        grad_dt_bias,
        grad_head_gain,
        out_total.T,
        grad_ffn_gain,
        gate_total.reshape(w_gate_up.shape),
        down_total.T,
    )


def solution(mesh):
    return jax.shard_map(
        per_device,
        mesh=mesh,
        in_specs=(
            P(("dp", "tensor"), None),
            P(),
            P("dp", "tensor", None),
            P("dp", "tensor", None),
            P(None, "tensor", "dp"),
            P(),
            P(),
            P(),
            P("tensor", "dp"),
            P(),
            P("dp", None, "tensor"),
            P("tensor", "dp"),
            P(("dp", "tensor"), None),
        ),
        out_specs=(
            P(("dp", "tensor"), None),
            P(("dp", "tensor"), None),
            P(),
            P("dp", "tensor", None),
            P("dp", "tensor", None),
            P(None, "tensor", "dp"),
            P(),
            P(),
            P(),
            P("tensor", "dp"),
            P(),
            P("dp", None, "tensor"),
            P("tensor", "dp"),
        ),
        check_vma=False,
    )
```

time: 506 us -> 407 us (0.80); the launches traced: 496 us -> 403 us
  waiting for transfers between devices: 234 us -> 150 us
  Pallas kernels: 41.8 us -> 90.5 us
  blocking collectives: 37.9 us -> 0 us
  matrix products: 31.7 us -> 12.6 us
  starting transfers between devices: 90 us -> 105 us
  local copies, waits for them, and re-layouts: 44.3 us -> 30.1 us
    ppermute x79 -> x77, waiting for transfers between devices: 234 us -> 150 us  [swap(): return lax.ppermute(array, axis, [(i, i ^ offset) for i in range(size)])]
    pallas_call x2 -> x14, Pallas kernels: 41.8 us -> 90.5 us  [call(): pl.pallas_call(kernel, out_shape=tuple((jax.ShapeDtypeStruct(shape, kind)...]
    psum x1 -> x0, blocking collectives: 37.9 us -> none  [per_device(): lax.psum((dp.blocks_from_order(grad_gain_first), dp.blocks_from_order(gra...]
    ppermute x79 -> x77, starting transfers between devices: 90 us -> 105 us  [swap(): return lax.ppermute(array, axis, [(i, i ^ offset) for i in range(size)])]
    gather x14 -> x0, local copies, waits for them, and re-layouts: 11 us -> none  [the longest x8 6.04 us: blocks_from_order(): return jnp.take(parts, index, axis=-2).reshape(array.shape)]
    dot_general x7 -> x0, matrix products: 10.3 us -> none  [the longest x4 6.91 us: cols_dot(): lax.dot_general(left, right, (((1,), (1,)), ((), ())), preferred_element_...]
    dot_general x9 -> x6, matrix products: 21.4 us -> 12.6 us  [rows_dot(): lax.dot_general(left, right, (((0,), (0,)), ((), ())), preferred_element_...]
    slice x11 -> x14, local copies, waits for them, and re-layouts: 0.26 us -> 7.74 us  [the longest x5 3.53 us: scatter_z(): low[p * depth:(p + 1) * depth]]
  transfers between devices with their start and end apart: 79 -> 77, of which waited for: 38 -> 32; matrix products, arithmetic and copies ran while one was open for 15% -> 10% of each run, Pallas kernels for 8% -> 18%
where the time goes in v3:
time: 407 us; the launch traced here: 403 us
  waiting for transfers between devices  150 us (37%)
  starting transfers between devices  105 us (26%)
  Pallas kernels  90.5 us (22%)
  local copies, waits for them, and re-layouts  30.1 us (7%)
  other arithmetic  12.7 us (3%)
  matrix products  12.6 us (3%)
    ppermute x77, waiting for transfers between devices, swap(): return lax.ppermute(array, axis, [(i, i ^ offset) for i in range(size)])  150 us
    ppermute x77, starting transfers between devices, swap(): return lax.ppermute(array, axis, [(i, i ^ offset) for i in range(size)])  105 us
    pallas_call x14, Pallas kernels, call(): pl.pallas_call(kernel, out_shape=tuple((jax.ShapeDtypeStruct(shape, kind)...  90.5 us
    dot_general x6, matrix products, rows_dot(): lax.dot_general(left, right, (((0,), (0,)), ((), ())), preferred_element_...  12.6 us
    unnamed x139, local copies, waits for them, and re-layouts  12.3 us
  transfers between devices with their start and end apart: 77, of which 32 were waited for; matrix products, arithmetic and copies ran while one was open for 10% of the time, Pallas kernels for 18%

profile of v3, /device:TPU:0, one launch (start us, length us, event | category | flops | bytes accessed | tf_op | source)
XLA Modules:
  0.0 402.7 jit_solution(17082036757822706568)
XLA Ops:
  3.4 3.1 collective-permute-start.3
  6.5 2.6 collective-permute-start.4
  15.6 9.2 %collective-permute-done.4.refs_13_ = bf16[64,1664]{1,0:T(8,128)(2,1)S(1)} collective-permute-done((bf16[64,1664]{1,0:T(8,128)(2,1)S(1)}, bf16[64,1664]{1,0:T(8,128)(2,1)S(1)}, u32[]{:S(2)}, u32[]{:S(2)}) %collective-permute-start.4) | collective-permute-done | bytes 213024 | tf_op jit(solution)/shard_map/ppermute | solution.py:733
  24.7 3.7 collective-permute-start.6
  32.4 3.0 collective-permute-done.6.refs_12_
  36.9 9.4 %collective-permute-done.7.refs_14_ = bf16[64,1664]{1,0:T(8,128)(2,1)S(1)} collective-permute-done((bf16[64,1664]{1,0:T(8,128)(2,1)S(1)}, bf16[64,1664]{1,0:T(8,128)(2,1)S(1)}, u32[]{:S(2)}, u32[]{:S(2)}) %collective-permute-start.7) | collective-permute-done | bytes 213024 | tf_op jit(solution)/shard_map/ppermute | solution.py:733
  54.0 3.1 collective-permute-done.10.refs_18_
  62.1 3.9 collective-permute-done.14.refs_22_
  71.7 11.4 %collective-permute-done.18.refs_2_.refs_10_ = bf16[128,896]{1,0:T(8,128)(2,1)S(1)} collective-permute-done((bf16[128,896]{1,0:T(8,128)(2,1)S(1)}, bf16[128,896]{1,0:T(8,128)(2,1)S(1)}, u32[]{:S(2)}, u32[]{:S(2)}) %collective-permute-start.18) | collective-permute-done | bytes 229408 | tf_op jit(solution)/shard_map/ppermute | solution.py:733
  83.1 3.0 collective-permute-start.20
  89.6 2.9 collective-permute-done.20.refs_17_
  102.3 22.8 %mixer_forward.1 = (bf16[512,512]{1,0:T(8,128)(2,1)}, f32[512,1536]{1,0:T(8,128)}, f32[512,128]{1,0:T(8,128)}, f32[512,512]{1,0:T(8,128)}, f32[4,2,128,256]{3,2,...) custom-call(s32[17]{0:T(128)} %pad_add_fusion.1.ids_ref.refs_0_, ...), custom_call_target="tpu_custom_call" | custom-call | tf_op jit(solution)/shard_map/mixer_forward/pallas_call | solution.py:634
  125.9 4.0 out_product.1
  136.7 2.4 collective-permute-start.29
  142.5 6.1 %collective-permute-done.29.refs_25_ = bf16[128,896]{1,0:T(8,128)(2,1)S(1)} collective-permute-done((bf16[128,896]{1,0:T(8,128)(2,1)S(1)}, bf16[128,896]{1,0:T(8,128)(2,1)S(1)}, u32[]{:S(2)}, u32[]{:S(2)}) %collective-permute-start.29) | collective-permute-done | bytes 229408 | tf_op jit(solution)/shard_map/ppermute | solution.py:733
  149.6 8.7 %collective-permute-done.30.refs_26_ = bf16[128,896]{1,0:T(8,128)(2,1)S(1)} collective-permute-done((bf16[128,896]{1,0:T(8,128)(2,1)S(1)}, bf16[128,896]{1,0:T(8,128)(2,1)S(1)}, u32[]{:S(2)}, u32[]{:S(2)}) %collective-permute-start.30) | collective-permute-done | bytes 229408 | tf_op jit(solution)/shard_map/ppermute | solution.py:733
  162.7 3.6 collective-permute-done.34.refs_22_
  166.2 3.3 collective-permute-done.35.refs_23_
  171.0 5.0 %collective-permute-done.37.refs_2_ = bf16[128,1024]{1,0:T(8,128)(2,1)S(1)} collective-permute-done((bf16[128,1024]{1,0:T(8,128)(2,1)}, bf16[128,1024]{1,0:T(8,128)(2,1)S(1)}, u32[]{:S(2)}, u32[]{:S(2)}) %collective-permute-start.37) | collective-permute-done | bytes 262176 | tf_op jit(solution)/shard_map/ppermute | solution.py:733
  179.2 5.3 %collective-permute-done.40.refs_29_ = bf16[128,896]{1,0:T(8,128)(2,1)S(1)} collective-permute-done((bf16[128,896]{1,0:T(8,128)(2,1)S(1)}, bf16[128,896]{1,0:T(8,128)(2,1)S(1)}, u32[]{:S(2)}, u32[]{:S(2)}) %collective-permute-start.40) | collective-permute-done | bytes 229408 | tf_op jit(solution)/shard_map/ppermute | solution.py:733
  184.5 4.9 %collective-permute-done.41.refs_30_ = bf16[128,896]{1,0:T(8,128)(2,1)S(1)} collective-permute-done((bf16[128,896]{1,0:T(8,128)(2,1)S(1)}, bf16[128,896]{1,0:T(8,128)(2,1)S(1)}, u32[]{:S(2)}, u32[]{:S(2)}) %collective-permute-start.41) | collective-permute-done | bytes 229408 | tf_op jit(solution)/shard_map/ppermute | solution.py:733
  189.4 4.5 %collective-permute-done.42.refs_31_ = bf16[128,896]{1,0:T(8,128)(2,1)S(1)} collective-permute-done((bf16[128,896]{1,0:T(8,128)(2,1)S(1)}, bf16[128,896]{1,0:T(8,128)(2,1)S(1)}, u32[]{:S(2)}, u32[]{:S(2)}) %collective-permute-start.42) | collective-permute-done | bytes 229408 | tf_op jit(solution)/shard_map/ppermute | solution.py:733
  195.4 10.9 %feed_forward.1 = (bf16[512,1024]{1,0:T(8,128)(2,1)}, bf16[512,1024]{1,0:T(8,128)(2,1)}, bf16[512,704]{1,0:T(8,128)(2,1)}, bf16[512,1408]{1,0:T(8,128)(2,1)}, bf...) custom-call(bf16[128,1024]{1,0:T(8,128)(2,1)} %get-tuple-element.106.refs_0_, ...), custom_call_target="tpu_custom_call" | custom-call | tf_op jit(solution)/shard_map/feed_forward/pallas_call | solution.py:634
  213.9 2.4 back_fold.1
  217.5 2.3 ffn_fold.1
  221.4 6.0 %collective-permute-done.73 = bf16[512,704]{0,1:T(8,128)(2,1)S(1)} collective-permute-done((bf16[512,704]{0,1:T(8,128)(2,1)S(1)}, bf16[512,704]{0,1:T(8,128)(2,1)S(1)}, u32[]{:S(2)}, u32[]{:S(2)}) %collective-permute-start.73) | collective-permute-done | bytes 720928 | tf_op jit(solution)/shard_map/ppermute | solution.py:733
  228.7 2.6 middle_back.1
  232.0 2.5 collective-permute-start.75
  236.4 4.4 %collective-permute-done.74 = bf16[128,704]{0,1:T(8,128)(2,1)S(1)} collective-permute-done((bf16[128,704]{0,1:T(8,128)(2,1)S(1)}, bf16[128,704]{0,1:T(8,128)(2,1)S(1)}, u32[]{:S(2)}, u32[]{:S(2)}) %collective-permute-start.74) | collective-permute-done | bytes 180256 | tf_op jit(solution)/shard_map/ppermute | solution.py:733
  243.5 2.7 collective-permute-done.75
  247.9 23.3 %mixer_backward.1 = (bf16[512,1664]{1,0:T(8,128)(2,1)}, f32[8,512]{1,0:T(8,128)}, f32[1,256]{1,0:T(1,128)}, f32[2,128]{1,0:T(2,128)}, bf16[512,896]{1,0:T(8,128)...) custom-call(s32[17]{0:T(128)} %pad_add_fusion.1.ids_ref.refs_0_, f32[1,128]{1,0:T(1,128)} %pad.21.refs_2_.refs_1_, ...), custom_call_target="tpu_custom_call" | custom-call | tf_op jit(solution)/shard_map/mixer_backward/pallas_call | solution.py:634
  271.2 2.3 convolution_convert_fusion.2
  275.5 8.5 %mixer_products.1 = (f32[512,896]{1,0:T(8,128)}, f32[512,768]{1,0:T(8,128)}, bf16[256,1024]{1,0:T(8,128)(2,1)}, f32[256,1024]{1,0:T(8,128)}) custom-call(s32[17]{0:T(128)} %pad_add_fusion.1.ids_ref.refs_0_, bf16[512,1024]{1,0:T(8,128)(2,1)} %get-tuple-element.120.refs_22_.refs_1_, bf16[512,1664]{1,0:T(8,128)(2,1)} %get-tuple-element.134.refs_2_, ...), custom_call_target="tpu_custom_call" | custom-call | tf_op jit(solution)/shard_map/mixer_products/pallas_call | solution.py:634
  284.6 3.0 fusion.29
  288.6 2.7 collective-permute-start.70
  297.5 2.7 fusion.28
  300.2 4.1 %collective-permute-done.51.got_ref = bf16[128,1024]{1,0:T(8,128)(2,1)S(1)} collective-permute-done((bf16[128,1024]{1,0:T(8,128)(2,1)}, bf16[128,1024]{1,0:T(8,128)(2,1)S(1)}, u32[]{:S(2)}, u32[]{:S(2)}) %collective-permute-start.51) | collective-permute-done | bytes 262176 | tf_op jit(solution)/shard_map/ppermute | solution.py:733
  305.0 2.6 last_grad.1
  312.2 7.1 %collective-permute-done.71 = bf16[128,1408]{1,0:T(8,128)(2,1)} collective-permute-done((bf16[128,1408]{1,0:T(8,128)(2,1)}, bf16[128,1408]{1,0:T(8,128)(2,1)}, u32[]{:S(2)}, u32[]{:S(2)}) %collective-permute-start.71) | collective-permute-done | bytes 360480 | tf_op jit(solution)/shard_map/ppermute | solution.py:733
  325.0 2.4 copy.45
  330.1 5.3 %collective-permute-done.67 = bf16[128,512]{1,0:T(8,128)(2,1)S(1)} collective-permute-done((bf16[128,512]{1,0:T(8,128)(2,1)}, bf16[128,512]{1,0:T(8,128)(2,1)S(1)}, u32[]{:S(2)}, u32[]{:S(2)}) %collective-permute-start.67) | collective-permute-done | bytes 131104 | tf_op jit(solution)/shard_map/ppermute | solution.py:733
  337.2 8.9 %collective-permute-done.54 = f32[8,384]{1,0:T(8,128)S(1)} collective-permute-done((f32[8,384]{1,0:T(8,128)S(1)}, f32[8,384]{1,0:T(8,128)S(1)}, u32[]{:S(2)}, u32[]{:S(2)}) %collective-permute-start.54) | collective-permute-done | bytes 12320 | tf_op jit(solution)/shard_map/ppermute | solution.py:733
  346.2 14.3 %collective-permute-start.55 = (f32[8,384]{1,0:T(8,128)S(1)}, f32[8,384]{1,0:T(8,128)S(1)}, u32[]{:S(2)}, u32[]{:S(2)}) collective-permute-start(f32[8,384]{1,0:T(8,128)S(1)} %add.114), channel_id=1, source_target_pairs={{0,8},{4,12},{8,0},{12,4},{16,24},{20,28},{24,16},{28,20},{1,9},{5... | collective-permute-start | bytes 36872 | tf_op jit(solution)/shard_map/ppermute | solution.py:733
  362.1 2.5 collective-permute-start.56
  365.5 2.5 collective-permute-start.63
  374.4 2.5 collective-permute-start.59
  379.6 2.8 collective-permute-done.63
  385.7 13.8 %collective-permute-done.59 = bf16[128,896]{1,0:T(8,128)(2,1)} collective-permute-done((bf16[128,896]{1,0:T(8,128)(2,1)}, bf16[128,896]{1,0:T(8,128)(2,1)}, u32[]{:S(2)}, u32[]{:S(2)}) %collective-permute-start.59) | collective-permute-done | bytes 229408 | tf_op jit(solution)/shard_map/ppermute | solution.py:733
  (320 shorter events, 130.1 us)
Async XLA Ops:
  6.5 18.2 %collective-permute-start.4 = (bf16[64,1664]{1,0:T(8,128)(2,1)S(1)}, bf16[64,1664]{1,0:T(8,128)(2,1)S(1)}, u32[]{:S(2)}, u32[]{:S(2)}) collective-permute-start(bf16[64,1664]{1,0:T(8,128)(2,1)S(1)} %get-tuple-element.201.refs_9_), channel_id=1, source_target_pairs={{0,16},{4,20},{8,24},{12,28},{16,0},{20,4},{24,8},{28,12},{1,17},{... | collective-permute-start | bytes 638984 | tf_op jit(solution)/shard_map/ppermute | solution.py:733
  9.1 15.6 %collective-permute-start.5 = (bf16[64,1664]{1,0:T(8,128)(2,1)S(1)}, bf16[64,1664]{1,0:T(8,128)(2,1)S(1)}, u32[]{:S(2)}, u32[]{:S(2)}) collective-permute-start(bf16[64,1664]{1,0:T(8,128)(2,1)S(1)} %get-tuple-element.201.refs_9_), channel_id=1, source_target_pairs={{0,24},{4,28},{8,16},{12,20},{16,8},{20,12},{24,0},{28,4},{1,25},{... | collective-permute-start | bytes 638984 | tf_op jit(solution)/shard_map/ppermute | solution.py:733
  11.9 46.7 %collective-permute-start.1 = (bf16[256,1024]{1,0:T(8,128)(2,1)}, bf16[256,1024]{1,0:T(8,128)(2,1)S(1)}, u32[]{:S(2)}, u32[]{:S(2)}) collective-permute-start(bf16[256,1024]{1,0:T(8,128)(2,1)} %get-tuple-element.84.refs_5_.refs_4_.both_ref), channel_id=1, source_target_pairs={{0,2},{1,3},{2,0},{3,1},{4,6},{5,7},{6,4},{7,5},{8,10},{9,11},{10,... | collective-permute-start | bytes 1572872 | tf_op jit(solution)/shard_map/ppermute | solution.py:733
  13.6 17.3 %collective-permute-start.9 = (bf16[64,1664]{1,0:T(8,128)(2,1)S(1)}, bf16[64,1664]{1,0:T(8,128)(2,1)S(1)}, u32[]{:S(2)}, u32[]{:S(2)}) collective-permute-start(bf16[64,1664]{1,0:T(8,128)(2,1)S(1)} %get-tuple-element.201.refs_9_), channel_id=1, source_target_pairs={{0,4},{4,0},{8,12},{12,8},{16,20},{20,16},{24,28},{28,24},{1,5},{5... | collective-permute-start | bytes 638984 | tf_op jit(solution)/shard_map/ppermute | solution.py:733
  28.4 17.9 %collective-permute-start.7 = (bf16[64,1664]{1,0:T(8,128)(2,1)S(1)}, bf16[64,1664]{1,0:T(8,128)(2,1)S(1)}, u32[]{:S(2)}, u32[]{:S(2)}) collective-permute-start(bf16[64,1664]{1,0:T(8,128)(2,1)S(1)} %get-tuple-element.85.refs_10_), channel_id=1, source_target_pairs={{0,16},{4,20},{8,24},{12,28},{16,0},{20,4},{24,8},{28,12},{1,17},{... | collective-permute-start | bytes 638984 | tf_op jit(solution)/shard_map/ppermute | solution.py:733
  29.4 18.4 %collective-permute-start.8 = (bf16[64,1664]{1,0:T(8,128)(2,1)S(1)}, bf16[64,1664]{1,0:T(8,128)(2,1)S(1)}, u32[]{:S(2)}, u32[]{:S(2)}) collective-permute-start(bf16[64,1664]{1,0:T(8,128)(2,1)S(1)} %get-tuple-element.85.refs_10_), channel_id=1, source_target_pairs={{0,24},{4,28},{8,16},{12,20},{16,8},{20,12},{24,0},{28,4},{1,25},{... | collective-permute-start | bytes 638984 | tf_op jit(solution)/shard_map/ppermute | solution.py:733
  30.9 17.8 %collective-permute-start.11 = (bf16[64,1664]{1,0:T(8,128)(2,1)S(1)}, bf16[64,1664]{1,0:T(8,128)(2,1)}, u32[]{:S(2)}, u32[]{:S(2)}) collective-permute-start(bf16[64,1664]{1,0:T(8,128)(2,1)S(1)} %collective-permute-done.3.refs_11_), channel_id=1, source_target_pairs={{0,4},{4,0},{8,12},{12,8},{16,20},{20,16},{24,28},{28,24},{1,5},{5... | collective-permute-start | bytes 638984 | tf_op jit(solution)/shard_map/ppermute | solution.py:733
  35.4 13.4 %collective-permute-start.13 = (bf16[64,1664]{1,0:T(8,128)(2,1)S(1)}, bf16[64,1664]{1,0:T(8,128)(2,1)}, u32[]{:S(2)}, u32[]{:S(2)}) collective-permute-start(bf16[64,1664]{1,0:T(8,128)(2,1)S(1)} %collective-permute-done.4.refs_13_), channel_id=1, source_target_pairs={{0,4},{4,0},{8,12},{12,8},{16,20},{20,16},{24,28},{28,24},{1,5},{5... | collective-permute-start | bytes 638984 | tf_op jit(solution)/shard_map/ppermute | solution.py:733
  48.8 37.8 %collective-permute-start = (bf16[256,1024]{1,0:T(8,128)(2,1)}, bf16[256,1024]{1,0:T(8,128)(2,1)S(1)}, u32[]{:S(2)}, u32[]{:S(2)}) collective-permute-start(bf16[256,1024]{1,0:T(8,128)(2,1)} %get-tuple-element.84.refs_5_.refs_4_.both_ref), channel_id=1, source_target_pairs={{0,1},{1,0},{2,3},{3,2},{4,5},{5,4},{6,7},{7,6},{8,9},{9,8},{10,11... | collective-permute-start | bytes 1572872 | tf_op jit(solution)/shard_map/ppermute | solution.py:733
  48.9 12.7 %collective-permute-start.12 = (bf16[64,1664]{1,0:T(8,128)(2,1)S(1)}, bf16[64,1664]{1,0:T(8,128)(2,1)S(1)}, u32[]{:S(2)}, u32[]{:S(2)}) collective-permute-start(bf16[64,1664]{1,0:T(8,128)(2,1)S(1)} %collective-permute-done.6.refs_12_), channel_id=1, source_target_pairs={{0,4},{4,0},{8,12},{12,8},{16,20},{20,16},{24,28},{28,24},{1,5},{5... | collective-permute-start | bytes 638984 | tf_op jit(solution)/shard_map/ppermute | solution.py:733
  52.5 13.4 %collective-permute-start.14 = (bf16[64,1664]{1,0:T(8,128)(2,1)S(1)}, bf16[64,1664]{1,0:T(8,128)(2,1)S(1)}, u32[]{:S(2)}, u32[]{:S(2)}) collective-permute-start(bf16[64,1664]{1,0:T(8,128)(2,1)S(1)} %collective-permute-done.7.refs_14_), channel_id=1, source_target_pairs={{0,4},{4,0},{8,12},{12,8},{16,20},{20,16},{24,28},{28,24},{1,5},{5... | collective-permute-start | bytes 638984 | tf_op jit(solution)/shard_map/ppermute | solution.py:733
  58.6 35.0 %collective-permute-start.2 = (bf16[256,1024]{1,0:T(8,128)(2,1)S(1)}, bf16[256,1024]{1,0:T(8,128)(2,1)S(1)}, u32[]{:S(2)}, u32[]{:S(2)}) collective-permute-start(bf16[256,1024]{1,0:T(8,128)(2,1)S(1)} %collective-permute-done.1.refs_7_.refs_6_), channel_id=1, source_target_pairs={{0,1},{1,0},{2,3},{3,2},{4,5},{5,4},{6,7},{7,6},{8,9},{9,8},{10,11... | collective-permute-start | bytes 1572872 | tf_op jit(solution)/shard_map/ppermute | solution.py:733
  65.9 17.1 %collective-permute-start.18 = (bf16[128,896]{1,0:T(8,128)(2,1)S(1)}, bf16[128,896]{1,0:T(8,128)(2,1)S(1)}, u32[]{:S(2)}, u32[]{:S(2)}) collective-permute-start(bf16[128,896]{1,0:T(8,128)(2,1)S(1)} %get-tuple-element.87.refs_0_.refs_8_), channel_id=1, source_target_pairs={{0,16},{4,20},{8,24},{12,28},{16,0},{20,4},{24,8},{28,12},{1,17},{... | collective-permute-start | bytes 688136 | tf_op jit(solution)/shard_map/ppermute | solution.py:733
  68.2 14.9 %collective-permute-start.19 = (bf16[128,896]{1,0:T(8,128)(2,1)S(1)}, bf16[128,896]{1,0:T(8,128)(2,1)S(1)}, u32[]{:S(2)}, u32[]{:S(2)}) collective-permute-start(bf16[128,896]{1,0:T(8,128)(2,1)S(1)} %get-tuple-element.87.refs_0_.refs_8_), channel_id=1, source_target_pairs={{0,24},{4,28},{8,16},{12,20},{16,8},{20,12},{24,0},{28,4},{1,25},{... | collective-permute-start | bytes 688136 | tf_op jit(solution)/shard_map/ppermute | solution.py:733
  70.1 18.3 %collective-permute-start.23 = (bf16[128,896]{1,0:T(8,128)(2,1)S(1)}, bf16[128,896]{1,0:T(8,128)(2,1)S(1)}, u32[]{:S(2)}, u32[]{:S(2)}) collective-permute-start(bf16[128,896]{1,0:T(8,128)(2,1)S(1)} %get-tuple-element.87.refs_0_.refs_8_), channel_id=1, source_target_pairs={{0,4},{4,0},{8,12},{12,8},{16,20},{20,16},{24,28},{28,24},{1,5},{5... | collective-permute-start | bytes 688136 | tf_op jit(solution)/shard_map/ppermute | solution.py:733
  86.1 39.0 %collective-permute-start.21 = (bf16[128,896]{1,0:T(8,128)(2,1)}, bf16[128,896]{1,0:T(8,128)(2,1)}, u32[]{:S(2)}, u32[]{:S(2)}) collective-permute-start(bf16[128,896]{1,0:T(8,128)(2,1)} %get-tuple-element.102.refs_16_), channel_id=1, source_target_pairs={{0,16},{4,20},{8,24},{12,28},{16,0},{20,4},{24,8},{28,12},{1,17},{... | collective-permute-start | bytes 688136 | tf_op jit(solution)/shard_map/ppermute | solution.py:733
  86.5 38.6 %collective-permute-start.22 = (bf16[128,896]{1,0:T(8,128)(2,1)}, bf16[128,896]{1,0:T(8,128)(2,1)}, u32[]{:S(2)}, u32[]{:S(2)}) collective-permute-start(bf16[128,896]{1,0:T(8,128)(2,1)} %get-tuple-element.102.refs_16_), channel_id=1, source_target_pairs={{0,24},{4,28},{8,16},{12,20},{16,8},{20,12},{24,0},{28,4},{1,25},{... | collective-permute-start | bytes 688136 | tf_op jit(solution)/shard_map/ppermute | solution.py:733
  88.5 36.7 %collective-permute-start.24 = (bf16[128,896]{1,0:T(8,128)(2,1)S(1)}, bf16[128,896]{1,0:T(8,128)(2,1)S(1)}, u32[]{:S(2)}, u32[]{:S(2)}) collective-permute-start(bf16[128,896]{1,0:T(8,128)(2,1)S(1)} %collective-permute-done.17.refs_1_.refs_9_), channel_id=1, source_target_pairs={{0,4},{4,0},{8,12},{12,8},{16,20},{20,16},{24,28},{28,24},{1,5},{5... | collective-permute-start | bytes 688136 | tf_op jit(solution)/shard_map/ppermute | solution.py:733
  92.5 32.7 %collective-permute-start.25 = (bf16[128,896]{1,0:T(8,128)(2,1)S(1)}, bf16[128,896]{1,0:T(8,128)(2,1)S(1)}, u32[]{:S(2)}, u32[]{:S(2)}) collective-permute-start(bf16[128,896]{1,0:T(8,128)(2,1)S(1)} %collective-permute-done.18.refs_2_.refs_10_), channel_id=1, source_target_pairs={{0,4},{4,0},{8,12},{12,8},{16,20},{20,16},{24,28},{28,24},{1,5},{5... | collective-permute-start | bytes 688136 | tf_op jit(solution)/shard_map/ppermute | solution.py:733
  93.6 31.6 %collective-permute-start.26 = (bf16[128,896]{1,0:T(8,128)(2,1)S(1)}, bf16[128,896]{1,0:T(8,128)(2,1)}, u32[]{:S(2)}, u32[]{:S(2)}) collective-permute-start(bf16[128,896]{1,0:T(8,128)(2,1)S(1)} %collective-permute-done.19.refs_3_.refs_11_), channel_id=1, source_target_pairs={{0,4},{4,0},{8,12},{12,8},{16,20},{20,16},{24,28},{28,24},{1,5},{5... | collective-permute-start | bytes 688136 | tf_op jit(solution)/shard_map/ppermute | solution.py:733
  135.1 24.2 %collective-permute-start.28 = (bf16[128,1024]{1,0:T(8,128)(2,1)}, bf16[128,1024]{1,0:T(8,128)(2,1)S(1)}, u32[]{:S(2)}, u32[]{:S(2)}) collective-permute-start(bf16[128,1024]{1,0:T(8,128)(2,1)} %get-tuple-element.97), channel_id=1, source_target_pairs={{0,2},{1,3},{2,0},{3,1},{4,6},{5,7},{6,4},{7,5},{8,10},{9,11},{10,... | collective-permute-start | bytes 786440 | tf_op jit(solution)/shard_map/ppermute | solution.py:733
  139.1 19.3 %collective-permute-start.30 = (bf16[128,896]{1,0:T(8,128)(2,1)S(1)}, bf16[128,896]{1,0:T(8,128)(2,1)S(1)}, u32[]{:S(2)}, u32[]{:S(2)}) collective-permute-start(bf16[128,896]{1,0:T(8,128)(2,1)S(1)} %slice.186.refs_24_), channel_id=1, source_target_pairs={{0,16},{4,20},{8,24},{12,28},{16,0},{20,4},{24,8},{28,12},{1,17},{... | collective-permute-start | bytes 688136 | tf_op jit(solution)/shard_map/ppermute | solution.py:733
  139.5 23.1 %collective-permute-start.31 = (bf16[128,896]{1,0:T(8,128)(2,1)S(1)}, bf16[128,896]{1,0:T(8,128)(2,1)S(1)}, u32[]{:S(2)}, u32[]{:S(2)}) collective-permute-start(bf16[128,896]{1,0:T(8,128)(2,1)S(1)} %slice.186.refs_24_), channel_id=1, source_target_pairs={{0,24},{4,28},{8,16},{12,20},{16,8},{20,12},{24,0},{28,4},{1,25},{... | collective-permute-start | bytes 688136 | tf_op jit(solution)/shard_map/ppermute | solution.py:733
  141.4 21.2 %collective-permute-start.32 = (bf16[128,896]{1,0:T(8,128)(2,1)}, bf16[128,896]{1,0:T(8,128)(2,1)S(1)}, u32[]{:S(2)}, u32[]{:S(2)}) collective-permute-start(bf16[128,896]{1,0:T(8,128)(2,1)} %get-tuple-element.102.refs_16_), channel_id=1, source_target_pairs={{0,4},{4,0},{8,12},{12,8},{16,20},{20,16},{24,28},{28,24},{1,5},{5... | collective-permute-start | bytes 688136 | tf_op jit(solution)/shard_map/ppermute | solution.py:733
  148.6 14.1 %collective-permute-start.33 = (bf16[128,896]{1,0:T(8,128)(2,1)S(1)}, bf16[128,896]{1,0:T(8,128)(2,1)S(1)}, u32[]{:S(2)}, u32[]{:S(2)}) collective-permute-start(bf16[128,896]{1,0:T(8,128)(2,1)S(1)} %copy-done.37), channel_id=1, source_target_pairs={{0,4},{4,0},{8,12},{12,8},{16,20},{20,16},{24,28},{28,24},{1,5},{5... | collective-permute-start | bytes 688136 | tf_op jit(solution)/shard_map/ppermute | solution.py:733
  171.0 22.9 %collective-permute-start.36 = (bf16[128,1024]{1,0:T(8,128)(2,1)}, bf16[128,1024]{1,0:T(8,128)(2,1)S(1)}, u32[]{:S(2)}, u32[]{:S(2)}) collective-permute-start(bf16[128,1024]{1,0:T(8,128)(2,1)} %get-tuple-element.106.refs_0_), channel_id=1, source_target_pairs={{0,1},{1,0},{2,3},{3,2},{4,5},{5,4},{6,7},{7,6},{8,9},{9,8},{10,11... | collective-permute-start | bytes 786440 | tf_op jit(solution)/shard_map/ppermute | solution.py:733
  176.1 17.9 %collective-permute-start.38 = (bf16[128,1024]{1,0:T(8,128)(2,1)S(1)}, bf16[128,1024]{1,0:T(8,128)(2,1)S(1)}, u32[]{:S(2)}, u32[]{:S(2)}) collective-permute-start(bf16[128,1024]{1,0:T(8,128)(2,1)S(1)} %collective-permute-done.37.refs_2_), channel_id=1, source_target_pairs={{0,1},{1,0},{2,3},{3,2},{4,5},{5,4},{6,7},{7,6},{8,9},{9,8},{10,11... | collective-permute-start | bytes 786440 | tf_op jit(solution)/shard_map/ppermute | solution.py:733
  178.1 15.8 %collective-permute-start.42 = (bf16[128,896]{1,0:T(8,128)(2,1)S(1)}, bf16[128,896]{1,0:T(8,128)(2,1)S(1)}, u32[]{:S(2)}, u32[]{:S(2)}) collective-permute-start(bf16[128,896]{1,0:T(8,128)(2,1)S(1)} %collective-permute-done.31.refs_27_), channel_id=1, source_target_pairs={{0,4},{4,0},{8,12},{12,8},{16,20},{20,16},{24,28},{28,24},{1,5},{5... | collective-permute-start | bytes 688136 | tf_op jit(solution)/shard_map/ppermute | solution.py:733
  208.3 19.1 %collective-permute-start.73 = (bf16[512,704]{0,1:T(8,128)(2,1)S(1)}, bf16[512,704]{0,1:T(8,128)(2,1)S(1)}, u32[]{:S(2)}, u32[]{:S(2)}) collective-permute-start(bf16[512,704]{0,1:T(8,128)(2,1)S(1)} %convolution_convert_fusion.1), channel_id=1, source_target_pairs={{0,4},{4,0},{8,12},{12,8},{16,20},{20,16},{24,28},{28,24},{1,5},{5... | collective-permute-start | bytes 2162696 | tf_op jit(solution)/shard_map/ppermute | solution.py:733
  212.0 72.6 %collective-permute-start.69 = (bf16[512,1408]{1,0:T(8,128)(2,1)S(1)}, bf16[512,1408]{1,0:T(8,128)(2,1)}, u32[]{:S(2)}, u32[]{:S(2)}) collective-permute-start(bf16[512,1408]{1,0:T(8,128)(2,1)S(1)} %convolution_convert_fusion), channel_id=1, source_target_pairs={{0,4},{4,0},{8,12},{12,8},{16,20},{20,16},{24,28},{28,24},{1,5},{5... | collective-permute-start | bytes 4325384 | tf_op jit(solution)/shard_map/ppermute | solution.py:733
  219.8 14.6 %collective-permute-start.44 = (bf16[128,1024]{1,0:T(8,128)(2,1)}, bf16[128,1024]{1,0:T(8,128)(2,1)S(1)}, u32[]{:S(2)}, u32[]{:S(2)}) collective-permute-start(bf16[128,1024]{1,0:T(8,128)(2,1)} %get-tuple-element.118), channel_id=1, source_target_pairs={{0,2},{1,3},{2,0},{3,1},{4,6},{5,7},{6,4},{7,5},{8,10},{9,11},{10,... | collective-permute-start | bytes 786440 | tf_op jit(solution)/shard_map/ppermute | solution.py:733
  232.0 14.2 %collective-permute-start.75 = (bf16[128,704]{0,1:T(8,128)(2,1)S(1)}, bf16[128,704]{0,1:T(8,128)(2,1)S(1)}, u32[]{:S(2)}, u32[]{:S(2)}) collective-permute-start(bf16[128,704]{0,1:T(8,128)(2,1)S(1)} %get-tuple-element.196), channel_id=1, source_target_pairs={{0,16},{4,20},{8,24},{12,28},{16,0},{20,4},{24,8},{28,12},{1,17},{... | collective-permute-start | bytes 540680 | tf_op jit(solution)/shard_map/ppermute | solution.py:733
  273.5 22.5 %collective-permute-start.65 = (bf16[512,512]{1,0:T(8,128)(2,1)}, bf16[512,512]{1,0:T(8,128)(2,1)}, u32[]{:S(2)}, u32[]{:S(2)}) collective-permute-start(bf16[512,512]{1,0:T(8,128)(2,1)} %convolution_convert_fusion.2), channel_id=1, source_target_pairs={{0,4},{4,0},{8,12},{12,8},{16,20},{20,16},{24,28},{28,24},{1,5},{5... | collective-permute-start | bytes 1572872 | tf_op jit(solution)/shard_map/ppermute | solution.py:733
  274.5 86.0 %collective-permute-start.61 = (bf16[512,768]{1,0:T(8,128)(2,1)}, bf16[512,768]{1,0:T(8,128)(2,1)}, u32[]{:S(2)}, u32[]{:S(2)}) collective-permute-start(bf16[512,768]{1,0:T(8,128)(2,1)} %get-tuple-element.149), channel_id=1, source_target_pairs={{0,4},{4,0},{8,12},{12,8},{16,20},{20,16},{24,28},{28,24},{1,5},{5... | collective-permute-start | bytes 2359304 | tf_op jit(solution)/shard_map/ppermute | solution.py:733
  288.6 22.0 %collective-permute-start.70 = (bf16[128,1408]{1,0:T(8,128)(2,1)}, bf16[128,1408]{1,0:T(8,128)(2,1)}, u32[]{:S(2)}, u32[]{:S(2)}) collective-permute-start(bf16[128,1408]{1,0:T(8,128)(2,1)} %get-tuple-element.185), channel_id=1, source_target_pairs={{0,8},{4,12},{8,0},{12,4},{16,24},{20,28},{24,16},{28,20},{1,9},{5... | collective-permute-start | bytes 1081352 | tf_op jit(solution)/shard_map/ppermute | solution.py:733
  291.3 28.0 %collective-permute-start.71 = (bf16[128,1408]{1,0:T(8,128)(2,1)}, bf16[128,1408]{1,0:T(8,128)(2,1)}, u32[]{:S(2)}, u32[]{:S(2)}) collective-permute-start(bf16[128,1408]{1,0:T(8,128)(2,1)} %get-tuple-element.187), channel_id=1, source_target_pairs={{0,16},{4,20},{8,24},{12,28},{16,0},{20,4},{24,8},{28,12},{1,17},{... | collective-permute-start | bytes 1081352 | tf_op jit(solution)/shard_map/ppermute | solution.py:733
  291.8 29.5 %collective-permute-start.72 = (bf16[128,1408]{1,0:T(8,128)(2,1)}, bf16[128,1408]{1,0:T(8,128)(2,1)}, u32[]{:S(2)}, u32[]{:S(2)}) collective-permute-start(bf16[128,1408]{1,0:T(8,128)(2,1)} %get-tuple-element.186), channel_id=1, source_target_pairs={{0,24},{4,28},{8,16},{12,20},{16,8},{20,12},{24,0},{28,4},{1,25},{... | collective-permute-start | bytes 1081352 | tf_op jit(solution)/shard_map/ppermute | solution.py:733
  309.7 19.4 %collective-permute-start.66 = (bf16[128,512]{1,0:T(8,128)(2,1)}, bf16[128,512]{1,0:T(8,128)(2,1)S(1)}, u32[]{:S(2)}, u32[]{:S(2)}) collective-permute-start(bf16[128,512]{1,0:T(8,128)(2,1)} %get-tuple-element.197), channel_id=1, source_target_pairs={{0,8},{4,12},{8,0},{12,4},{16,24},{20,28},{24,16},{28,20},{1,9},{5... | collective-permute-start | bytes 393224 | tf_op jit(solution)/shard_map/ppermute | solution.py:733
  310.5 24.8 %collective-permute-start.67 = (bf16[128,512]{1,0:T(8,128)(2,1)}, bf16[128,512]{1,0:T(8,128)(2,1)S(1)}, u32[]{:S(2)}, u32[]{:S(2)}) collective-permute-start(bf16[128,512]{1,0:T(8,128)(2,1)} %get-tuple-element.199), channel_id=1, source_target_pairs={{0,16},{4,20},{8,24},{12,28},{16,0},{20,4},{24,8},{28,12},{1,17},{... | collective-permute-start | bytes 393224 | tf_op jit(solution)/shard_map/ppermute | solution.py:733
  319.3 16.0 %collective-permute-start.68 = (bf16[128,512]{1,0:T(8,128)(2,1)}, bf16[128,512]{1,0:T(8,128)(2,1)S(1)}, u32[]{:S(2)}, u32[]{:S(2)}) collective-permute-start(bf16[128,512]{1,0:T(8,128)(2,1)} %get-tuple-element.198), channel_id=1, source_target_pairs={{0,24},{4,28},{8,16},{12,20},{16,8},{20,12},{24,0},{28,4},{1,25},{... | collective-permute-start | bytes 393224 | tf_op jit(solution)/shard_map/ppermute | solution.py:733
  327.4 44.3 %collective-permute-start.57 = (bf16[512,896]{1,0:T(8,128)(2,1)}, bf16[512,896]{1,0:T(8,128)(2,1)}, u32[]{:S(2)}, u32[]{:S(2)}) collective-permute-start(bf16[512,896]{1,0:T(8,128)(2,1)} %get-tuple-element.147), channel_id=1, source_target_pairs={{0,4},{4,0},{8,12},{12,8},{16,20},{20,16},{24,28},{28,24},{1,5},{5... | collective-permute-start | bytes 2752520 | tf_op jit(solution)/shard_map/ppermute | solution.py:733
  329.1 17.0 %collective-permute-start.54 = (f32[8,384]{1,0:T(8,128)S(1)}, f32[8,384]{1,0:T(8,128)S(1)}, u32[]{:S(2)}, u32[]{:S(2)}) collective-permute-start(f32[8,384]{1,0:T(8,128)S(1)} %add.113), channel_id=1, source_target_pairs={{0,4},{4,0},{8,12},{12,8},{16,20},{20,16},{24,28},{28,24},{1,5},{5... | collective-permute-start | bytes 36872 | tf_op jit(solution)/shard_map/ppermute | solution.py:733
  346.2 16.0 %collective-permute-start.55 = (f32[8,384]{1,0:T(8,128)S(1)}, f32[8,384]{1,0:T(8,128)S(1)}, u32[]{:S(2)}, u32[]{:S(2)}) collective-permute-start(f32[8,384]{1,0:T(8,128)S(1)} %add.114), channel_id=1, source_target_pairs={{0,8},{4,12},{8,0},{12,4},{16,24},{20,28},{24,16},{28,20},{1,9},{5... | collective-permute-start | bytes 36872 | tf_op jit(solution)/shard_map/ppermute | solution.py:733
  365.5 12.6 %collective-permute-start.62 = (bf16[128,768]{1,0:T(8,128)(2,1)}, bf16[128,768]{1,0:T(8,128)(2,1)}, u32[]{:S(2)}, u32[]{:S(2)}) collective-permute-start(bf16[128,768]{1,0:T(8,128)(2,1)} %get-tuple-element.191), channel_id=1, source_target_pairs={{0,8},{4,12},{8,0},{12,4},{16,24},{20,28},{24,16},{28,20},{1,9},{5... | collective-permute-start | bytes 589832 | tf_op jit(solution)/shard_map/ppermute | solution.py:733
  365.5 16.9 %collective-permute-start.63 = (bf16[128,768]{1,0:T(8,128)(2,1)}, bf16[128,768]{1,0:T(8,128)(2,1)}, u32[]{:S(2)}, u32[]{:S(2)}) collective-permute-start(bf16[128,768]{1,0:T(8,128)(2,1)} %get-tuple-element.193), channel_id=1, source_target_pairs={{0,16},{4,20},{8,24},{12,28},{16,0},{20,4},{24,8},{28,12},{1,17},{... | collective-permute-start | bytes 589832 | tf_op jit(solution)/shard_map/ppermute | solution.py:733
  367.9 14.5 %collective-permute-start.64 = (bf16[128,768]{1,0:T(8,128)(2,1)}, bf16[128,768]{1,0:T(8,128)(2,1)}, u32[]{:S(2)}, u32[]{:S(2)}) collective-permute-start(bf16[128,768]{1,0:T(8,128)(2,1)} %get-tuple-element.192), channel_id=1, source_target_pairs={{0,24},{4,28},{8,16},{12,20},{16,8},{20,12},{24,0},{28,4},{1,25},{... | collective-permute-start | bytes 589832 | tf_op jit(solution)/shard_map/ppermute | solution.py:733
  374.4 25.1 %collective-permute-start.59 = (bf16[128,896]{1,0:T(8,128)(2,1)}, bf16[128,896]{1,0:T(8,128)(2,1)}, u32[]{:S(2)}, u32[]{:S(2)}) collective-permute-start(bf16[128,896]{1,0:T(8,128)(2,1)} %get-tuple-element.190), channel_id=1, source_target_pairs={{0,16},{4,20},{8,24},{12,28},{16,0},{20,4},{24,8},{28,12},{1,17},{... | collective-permute-start | bytes 688136 | tf_op jit(solution)/shard_map/ppermute | solution.py:733
  378.1 21.4 %collective-permute-start.60 = (bf16[128,896]{1,0:T(8,128)(2,1)}, bf16[128,896]{1,0:T(8,128)(2,1)}, u32[]{:S(2)}, u32[]{:S(2)}) collective-permute-start(bf16[128,896]{1,0:T(8,128)(2,1)} %get-tuple-element.189), channel_id=1, source_target_pairs={{0,24},{4,28},{8,16},{12,20},{16,8},{20,12},{24,0},{28,4},{1,25},{... | collective-permute-start | bytes 688136 | tf_op jit(solution)/shard_map/ppermute | solution.py:733
  (95 other events, 1775.8 us)
